TPU v7x, 32 devices: a whole 2x2x4 slice. The times are simulated.
32 devices in a mesh: gx: 4 (over x, core), gy: 8 (over z, y).
Axes of the slice: x: 2, y: 2, z: 4, core: 2. Of those that a mesh axis runs over, the one named last changes fastest.
Arguments:
- adj_electric: float32 [3, 128, 64, 128], P(None, 'gx', 'gy'), may hold values from -6 to 6
- adj_magnetic: float32 [3, 128, 64, 128], P(None, 'gx', 'gy'), may hold values from -6 to 6
- polarization: float32 [3, 128, 64, 128], P(None, 'gx', 'gy'), may hold values from -6 to 6
- pol_rate: float32 [3, 128, 64, 128], P(None, 'gx', 'gy'), may hold values from -6 to 6
- density: float32 [128, 64, 128], P('gx', 'gy'), may hold values from 0 to 1
- forward_rate: float32 [2, 3, 128, 64, 128], P(None, None, 'gx', 'gy'), may hold values from -6 to 6
- design_mask: int32 [128, 64, 128], P('gx', 'gy'), may hold values 0 or 1
- partner_rows: int32 [64], P('gy'), may hold values from 0 to 7, as said below
- filter_radius: int32 [128, 64], P('gx', 'gy'), may hold values from 1 to 4
Outputs:
- electric_out: float32 [3, 128, 64, 128], P(None, 'gx', 'gy')
- magnetic_out: float32 [3, 128, 64, 128], P(None, 'gx', 'gy')
- density_out: float32 [128, 64, 128], P('gx', 'gy')
Inputs may be any that keep to these rules, and one draw needn't show every extreme that they name: `partner_rows`: within each block of 8 rows the values are a permutation of 0 to 7.
All inputs are finite; a program needn't handle non-finite values. No bound on the sum of `design_mask` on one device may be relied on, other than what follows from the above.
Results may differ from a plain program's by a relative error of at most 0.0001.
Values sent between devices are 32-bit elements; how exact they have to be, the bound alone decides.
No kernel may reach another device: no remote copies, remote signals or barrier semaphores. Data moves between devices by JAX's collectives and lax.ppermute only.
A program may use at most 64 MiB of HBM per device.

v0:
```python
import math

import jax
import jax.numpy as jnp
from jax import lax
from jax.sharding import PartitionSpec as P

STEPS = 2
RMAX = 4


COURANT = 0.5
DAMPING = 0.9
OMEGA_SQUARED = 0.3
LORENTZ_STRENGTH = 2.0
EPS_MATERIAL = 4.0
UPDATE_STEP = 0.25
SHARPNESS = 4.0
THRESHOLD = 0.5


def padded(array, sides, width):
    for axis, dim in sides:
        peers, length = (lax.axis_size(axis), array.shape[dim])
        up = [(i, (i + 1) % peers) for i in range(peers - 1)]
        down = [(j, i) for i, j in up]
        last = lax.slice_in_dim(array, length - width, length, axis=dim)
        initial = lax.slice_in_dim(array, 0, width, axis=dim)
        before = lax.ppermute(last, axis, up)
        after = lax.ppermute(initial, axis, down)
        array = jnp.concatenate([before, array, after], axis=dim)
    return array


def swapped(block, axis, stride):
    count = lax.axis_size(axis)
    route = []
    for low in range(count):
        high = low | 1 << stride
        if high != low and high < count:
            route += [(low, high), (high, low)]
    return lax.ppermute(block, axis, route)


def ahead(values, dimension):
    count = values.shape[dimension]
    rest = lax.slice_in_dim(values, 1, count, axis=dimension)
    edge = jnp.zeros_like(lax.slice_in_dim(values, 0, 1, axis=dimension))
    return jnp.concatenate([rest, edge], dimension)


def behind(values, dimension):
    count = values.shape[dimension]
    rest = lax.slice_in_dim(values, 0, count - 1, axis=dimension)
    edge = jnp.zeros_like(lax.slice_in_dim(values, 0, 1, axis=dimension))
    return jnp.concatenate([edge, rest], dimension)


def advance(electric, magnetic, polar_now, velocity, material, inside):
    eps_local = 1.0 + (EPS_MATERIAL - 1.0) * material
    e_x, e_y, e_z = (electric[0], electric[1], electric[2])
    curl_e = jnp.stack(
        [
            ahead(e_z, 1) - e_z - (ahead(e_y, 2) - e_y),
            ahead(e_x, 2) - e_x - (ahead(e_z, 0) - e_z),
            ahead(e_y, 0) - e_y - (ahead(e_x, 1) - e_x),
        ]
    )
    magnetic = (magnetic - COURANT * curl_e) * inside
    h_x, h_y, h_z = (magnetic[0], magnetic[1], magnetic[2])
    curl_h = jnp.stack(
        [
            h_z - behind(h_z, 1) - (h_y - behind(h_y, 2)),
            h_x - behind(h_x, 2) - (h_z - behind(h_z, 0)),
            h_y - behind(h_y, 0) - (h_x - behind(h_x, 1)),
        ]
    )
    velocity = (
        DAMPING * velocity
        - OMEGA_SQUARED * polar_now
        + OMEGA_SQUARED * LORENTZ_STRENGTH * material * electric
    )
    polar_now = polar_now + velocity
    electric = (electric + (COURANT * curl_h - velocity) / eps_local) * inside
    return (electric, magnetic, polar_now, velocity)


def project(filtered):
    top = math.tanh(SHARPNESS * THRESHOLD)
    bottom = top + math.tanh(SHARPNESS * (1.0 - THRESHOLD))
    return (top + jnp.tanh(SHARPNESS * (filtered - THRESHOLD))) / bottom


def local(
    adj_electric,
    adj_magnetic,
    polarization,
    pol_rate,
    density,
    forward_rate,
    design_mask,
    partner_rows,
    filter_radius,
):
    rows_x, rows_y, depth = density.shape
    total_x = rows_x * lax.axis_size("gx")
    total_y = rows_y * lax.axis_size("gy")
    x_first = lax.axis_index("gx") * rows_x
    y_first = lax.axis_index("gy") * rows_y

    def inside_frame(width):
        x_cells = x_first + jnp.arange(-width, rows_x + width, dtype=jnp.int32)
        y_cells = y_first + jnp.arange(-width, rows_y + width, dtype=jnp.int32)
        in_x = ((x_cells >= 0) & (x_cells < total_x)).astype(jnp.float32)
        in_y = ((y_cells >= 0) & (y_cells < total_y)).astype(jnp.float32)
        return in_x[:, None, None] * in_y[None, :, None]

    fields = jnp.concatenate([adj_electric, adj_magnetic], 0)
    states = jnp.concatenate([polarization, pol_rate, density[None]], 0)
    framed_fields = padded(fields, (("gx", 1), ("gy", 2)), STEPS)
    narrow = padded(states, (("gx", 1), ("gy", 2)), STEPS - 1)
    framed_states = jnp.pad(narrow, ((0, 0), (1, 1), (1, 1), (0, 0)))
    electric = framed_fields[:3]
    magnetic = framed_fields[3:]
    polar_now = framed_states[:3]
    velocity = framed_states[3:6]
    material = framed_states[6]
    inside = inside_frame(STEPS)
    gradient = jnp.zeros((rows_x, rows_y, depth), jnp.float32)
    for step_index in range(STEPS):
        electric, magnetic, polar_now, velocity = advance(
            electric, magnetic, polar_now, velocity, material, inside
        )
        owned = electric[:, STEPS : STEPS + rows_x, STEPS : STEPS + rows_y, :]
        gradient = gradient + jnp.sum(owned * forward_rate[step_index], axis=0)
    electric_out = electric[:, STEPS : STEPS + rows_x, STEPS : STEPS + rows_y, :]
    magnetic_out = magnetic[:, STEPS : STEPS + rows_x, STEPS : STEPS + rows_y, :]
    partner = gradient
    for bit_index in range(lax.axis_size("gx").bit_length() - 1):
        partner = swapped(partner, "gx", bit_index)
    mirrored = jnp.take(partner[::-1], partner_rows, axis=1)
    symmetric = 0.5 * (gradient + mirrored)
    updated = density - UPDATE_STEP * design_mask.astype(jnp.float32) * symmetric
    width = RMAX - 1
    framed_design = padded(updated, (("gx", 0), ("gy", 1)), width)
    covered = inside_frame(width)
    radius = filter_radius.astype(jnp.float32)[:, :, None]
    numer = jnp.zeros((rows_x, rows_y, depth), jnp.float32)
    denom = jnp.zeros((rows_x, rows_y, 1), jnp.float32)
    for shift_x in range(-width, width + 1):
        for shift_y in range(-width, width + 1):
            distance = math.sqrt(shift_x * shift_x + shift_y * shift_y)
            weight = jnp.maximum(radius - distance, 0.0)
            window = framed_design[
                width + shift_x : width + shift_x + rows_x,
                width + shift_y : width + shift_y + rows_y,
                :,
            ]
            within = covered[
                width + shift_x : width + shift_x + rows_x,
                width + shift_y : width + shift_y + rows_y,
                :,
            ]
            numer = numer + weight * (within * window)
            denom = denom + weight * within
    density_out = project(numer / denom)
    return (electric_out, magnetic_out, density_out)


def solution(mesh):
    in_specs = (
        P(None, "gx", "gy", None),
        P(None, "gx", "gy", None),
        P(None, "gx", "gy", None),
        P(None, "gx", "gy", None),
        P("gx", "gy", None),
        P(None, None, "gx", "gy", None),
        P("gx", "gy", None),
        P("gy"),
        P("gx", "gy"),
    )
    out_specs = (P(None, "gx", "gy", None), P(None, "gx", "gy", None), P("gx", "gy", None))
    return jax.shard_map(local, mesh=mesh, in_specs=in_specs, out_specs=out_specs, check_vma=False)
```

profile of v0, /device:TPU:6, one launch (start us, length us, event | category | flops | bytes accessed | tf_op | source)
XLA Modules:
  0.0 70.0 jit_solution(14695502055758143592)
XLA Ops:
  0.7 1.1 %constant_dynamic-update-slice_fusion.1 = f32[6,32,8,128]{3,2,1,0:T(8,128)S(1)} fusion(f32[3,32,8,128]{3,2,1,0:T(8,128)} %param.9), kind=kLoop, calls=%fused_computation.266 | loop fusion | bytes 786432
  1.8 1.0 %constant_dynamic-update-slice_fusion = f32[6,32,8,128]{3,2,1,0:T(8,128)S(1)} fusion(f32[6,32,8,128]{3,2,1,0:T(8,128)S(1)} %constant_dynamic-update-slice_fusion.1, f32[3,32,8,128]{3,2,1,0:T(8,128)} %param.10), kind=kLoop, calls=%fused_computation.265 | loop fusion | bytes 786432 | tf_op jit(solution)/shard_map/concatenate | solution.py:118
  2.8 1.9 %collective-permute-start.1 = (f32[6,2,8,128]{3,2,1,0:T(8,128)S(1)}, f32[6,2,8,128]{3,2,1,0:T(8,128)S(1)}, u32[]{:S(2)}, u32[]{:S(2)}) collective-permute-start(f32[6,2,8,128]{3,2,1,0:T(8,128)S(1)} %get-tuple-element.57), channel_id=1, source_target_pairs={{8,0},{16,8},{24,16},{9,1},{17,9},{25,17},{10,2},{18,10},{26,18},{... | collective-permute-start | bytes 147464 | tf_op jit(solution)/shard_map/ppermute | solution.py:30
  4.7 2.4 %collective-permute-start = (f32[6,2,8,128]{3,2,1,0:T(8,128)S(1)}, f32[6,2,8,128]{3,2,1,0:T(8,128)S(1)}, u32[]{:S(2)}, u32[]{:S(2)}) collective-permute-start(f32[6,2,8,128]{3,2,1,0:T(8,128)S(1)} %get-tuple-element.56), channel_id=1, source_target_pairs={{0,8},{8,16},{16,24},{1,9},{9,17},{17,25},{2,10},{10,18},{18,26},{... | collective-permute-start | bytes 147464 | tf_op jit(solution)/shard_map/ppermute | solution.py:29
  8.0 3.1 %collective-permute-start.5 = (f32[7,1,8,128]{3,2,1,0:T(8,128)S(1)}, f32[7,1,8,128]{3,2,1,0:T(8,128)S(1)}, u32[]{:S(2)}, u32[]{:S(2)}) collective-permute-start(f32[7,1,8,128]{3,2,1,0:T(8,128)S(1)} %get-tuple-element.27), channel_id=1, source_target_pairs={{8,0},{16,8},{24,16},{9,1},{17,9},{25,17},{10,2},{18,10},{26,18},{... | collective-permute-start | bytes 86024 | tf_op jit(solution)/shard_map/ppermute | solution.py:30
  11.1 1.9 %collective-permute-start.4 = (f32[7,1,8,128]{3,2,1,0:T(8,128)S(1)}, f32[7,1,8,128]{3,2,1,0:T(8,128)S(1)}, u32[]{:S(2)}, u32[]{:S(2)}) collective-permute-start(f32[7,1,8,128]{3,2,1,0:T(8,128)S(1)} %get-tuple-element.26), channel_id=1, source_target_pairs={{0,8},{8,16},{16,24},{1,9},{9,17},{17,25},{2,10},{10,18},{18,26},{... | collective-permute-start | bytes 86024 | tf_op jit(solution)/shard_map/ppermute | solution.py:29
  13.6 2.7 %collective-permute-done.4 = f32[7,1,8,128]{3,2,1,0:T(8,128)S(1)} collective-permute-done((f32[7,1,8,128]{3,2,1,0:T(8,128)S(1)}, f32[7,1,8,128]{3,2,1,0:T(8,128)S(1)}, u32[]{:S(2)}, u32[]{:S(2)}) %collective-permute-start.4) | collective-permute-done | bytes 28704 | tf_op jit(solution)/shard_map/ppermute | solution.py:29
  16.5 2.4 %collective-permute-start.7 = (f32[7,34,1,128]{3,2,1,0:T(1,128)S(1)}, f32[7,34,1,128]{3,2,1,0:T(1,128)S(1)}, u32[]{:S(2)}, u32[]{:S(2)}) collective-permute-start(f32[7,34,1,128]{3,2,1,0:T(1,128)S(1)} %get-tuple-element.25), channel_id=1, source_target_pairs={{1,0},{2,1},{3,2},{4,3},{5,4},{6,5},{7,6},{9,8},{10,9},{11,10},{12... | collective-permute-start | bytes 365576 | tf_op jit(solution)/shard_map/ppermute | solution.py:30
  18.9 4.3 %collective-permute-start.6 = (f32[7,34,1,128]{3,2,1,0:T(1,128)S(1)}, f32[7,34,1,128]{3,2,1,0:T(1,128)S(1)}, u32[]{:S(2)}, u32[]{:S(2)}) collective-permute-start(f32[7,34,1,128]{3,2,1,0:T(1,128)S(1)} %get-tuple-element.24), channel_id=1, source_target_pairs={{0,1},{1,2},{2,3},{3,4},{4,5},{5,6},{6,7},{8,9},{9,10},{10,11},{11... | collective-permute-start | bytes 365576 | tf_op jit(solution)/shard_map/ppermute | solution.py:29
  23.4 1.9 %collective-permute-start.3 = (f32[6,36,2,128]{3,2,1,0:T(2,128)S(1)}, f32[6,36,2,128]{3,2,1,0:T(2,128)S(1)}, u32[]{:S(2)}, u32[]{:S(2)}) collective-permute-start(f32[6,36,2,128]{3,2,1,0:T(2,128)S(1)} %get-tuple-element.55), channel_id=1, source_target_pairs={{1,0},{2,1},{3,2},{4,3},{5,4},{6,5},{7,6},{9,8},{10,9},{11,10},{12... | collective-permute-start | bytes 663560 | tf_op jit(solution)/shard_map/ppermute | solution.py:30
  25.3 4.8 %collective-permute-start.2 = (f32[6,36,2,128]{3,2,1,0:T(2,128)S(1)}, f32[6,36,2,128]{3,2,1,0:T(2,128)S(1)}, u32[]{:S(2)}, u32[]{:S(2)}) collective-permute-start(f32[6,36,2,128]{3,2,1,0:T(2,128)S(1)} %get-tuple-element.54), channel_id=1, source_target_pairs={{0,1},{1,2},{2,3},{3,4},{4,5},{5,6},{6,7},{8,9},{9,10},{10,11},{11... | collective-permute-start | bytes 663560 | tf_op jit(solution)/shard_map/ppermute | solution.py:29
  30.2 2.1 %select_maximum_fusion = f32[7,36,12,128]{3,2,1,0:T(8,128)S(1)} fusion(f32[7,34,1,128]{3,2,1,0:T(1,128)S(1)} %collective-permute-done.7, f32[7,34,1,128]{3,2,1,0:T(1,128)S(1)} %collective-permute-done.6, f32[7,1,8,128]{3,2,1,0:T(8,128)S(1)} %collective-permute-done.5, f32[7,1,8,128]{3,2,1,0:T(8,128)S(1)} %collective-permute-done.4, ...), kind=kLoop, calls=%fused_computation.5 | loop fusion | flops 10450944 | bytes 2766848 | tf_op jit(solution)/shard_map/concatenate | solution.py:31
  32.4 3.2 %collective-permute-done.2 = f32[6,36,2,128]{3,2,1,0:T(2,128)S(1)} collective-permute-done((f32[6,36,2,128]{3,2,1,0:T(2,128)S(1)}, f32[6,36,2,128]{3,2,1,0:T(2,128)S(1)}, u32[]{:S(2)}, u32[]{:S(2)}) %collective-permute-start.2) | collective-permute-done | bytes 221216 | tf_op jit(solution)/shard_map/ppermute | solution.py:29
  40.1 1.1 %fusion.20 = (f32[32,8,128]{2,1,0:T(8,128)S(1)}, f32[32,8,128]{2,1,0:T(8,128)S(1)}, f32[3,32,8,128]{3,2,1,0:T(8,128)}) fusion(f32[2,3,32,8,128]{4,3,2,1,0:T(8,128)S(1)} %copy-done.3, f32[3,36,12,128]{3,2,1,0:T(8,128)S(1)} %get-tuple-element.12, f32[32,8]{1,0:T(8,128)S(1)} %slice.764, f32[32,8,128]{2,1,0:T(8,128)S(1)} %slice.763, ...), kind=kLoop, calls=%fused_computation.44 | loop fusion | flops 1310720 | bytes 3548160 | tf_op jit(solution)/shard_map/reduce_sum | solution.py:135
  41.3 1.3 %collective-permute-done.8 = f32[32,8,128]{2,0,1:T(8,128)S(1)} collective-permute-done((f32[32,8,128]{2,0,1:T(8,128)S(1)}, f32[32,8,128]{2,0,1:T(8,128)S(1)}, u32[]{:S(2)}, u32[]{:S(2)}) %collective-permute-start.8) | collective-permute-done | bytes 131104 | tf_op jit(solution)/shard_map/ppermute | solution.py:42
  42.6 1.5 %collective-permute-start.9 = (f32[32,8,128]{2,0,1:T(8,128)S(1)}, f32[32,8,128]{2,0,1:T(8,128)S(1)}, u32[]{:S(2)}, u32[]{:S(2)}) collective-permute-start(f32[32,8,128]{2,0,1:T(8,128)S(1)} %collective-permute-done.8), channel_id=1, source_target_pairs={{0,16},{16,0},{8,24},{24,8},{1,17},{17,1},{9,25},{25,9},{2,18},{18... | collective-permute-start | bytes 393224 | tf_op jit(solution)/shard_map/ppermute | solution.py:42
  44.2 4.0 %collective-permute-done.9 = f32[32,8,128]{2,0,1:T(8,128)S(1)} collective-permute-done((f32[32,8,128]{2,0,1:T(8,128)S(1)}, f32[32,8,128]{2,0,1:T(8,128)S(1)}, u32[]{:S(2)}, u32[]{:S(2)}) %collective-permute-start.9) | collective-permute-done | bytes 131104 | tf_op jit(solution)/shard_map/ppermute | solution.py:42
  48.9 2.4 %collective-permute-start.11 = (f32[3,8,128]{2,0,1:T(4,128)S(1)}, f32[3,8,128]{2,0,1:T(4,128)S(1)}, u32[]{:S(2)}, u32[]{:S(2)}) collective-permute-start(f32[3,8,128]{2,0,1:T(4,128)S(1)} %get-tuple-element.63), channel_id=1, source_target_pairs={{8,0},{16,8},{24,16},{9,1},{17,9},{25,17},{10,2},{18,10},{26,18},{... | collective-permute-start | bytes 36872 | tf_op jit(solution)/shard_map/ppermute | solution.py:30
  51.3 2.0 %collective-permute-start.10 = (f32[3,8,128]{2,0,1:T(4,128)S(1)}, f32[3,8,128]{2,0,1:T(4,128)S(1)}, u32[]{:S(2)}, u32[]{:S(2)}) collective-permute-start(f32[3,8,128]{2,0,1:T(4,128)S(1)} %get-tuple-element.62), channel_id=1, source_target_pairs={{0,8},{8,16},{16,24},{1,9},{9,17},{17,25},{2,10},{10,18},{18,26},{... | collective-permute-start | bytes 36872 | tf_op jit(solution)/shard_map/ppermute | solution.py:29
  53.3 3.1 %collective-permute-done.10 = f32[3,8,128]{2,0,1:T(4,128)S(1)} collective-permute-done((f32[3,8,128]{2,0,1:T(4,128)S(1)}, f32[3,8,128]{2,0,1:T(4,128)S(1)}, u32[]{:S(2)}, u32[]{:S(2)}) %collective-permute-start.10) | collective-permute-done | bytes 12320 | tf_op jit(solution)/shard_map/ppermute | solution.py:29
  56.4 3.2 %collective-permute-start.12 = (f32[38,3,128]{2,0,1:T(8,128)S(1)}, f32[38,3,128]{2,0,1:T(8,128)S(1)}, u32[]{:S(2)}, u32[]{:S(2)}) collective-permute-start(f32[38,3,128]{2,0,1:T(8,128)S(1)} %get-tuple-element.60), channel_id=1, source_target_pairs={{0,1},{1,2},{2,3},{3,4},{4,5},{5,6},{6,7},{8,9},{9,10},{10,11},{11... | collective-permute-start | bytes 175112 | tf_op jit(solution)/shard_map/ppermute | solution.py:29
  59.6 2.7 %collective-permute-start.13 = (f32[38,3,128]{2,0,1:T(8,128)S(1)}, f32[38,3,128]{2,0,1:T(8,128)S(1)}, u32[]{:S(2)}, u32[]{:S(2)}) collective-permute-start(f32[38,3,128]{2,0,1:T(8,128)S(1)} %get-tuple-element.61), channel_id=1, source_target_pairs={{1,0},{2,1},{3,2},{4,3},{5,4},{6,5},{7,6},{9,8},{10,9},{11,10},{12... | collective-permute-start | bytes 175112 | tf_op jit(solution)/shard_map/ppermute | solution.py:30
  63.1 3.4 %collective-permute-done.13 = f32[38,3,128]{2,0,1:T(8,128)S(1)} collective-permute-done((f32[38,3,128]{2,0,1:T(8,128)S(1)}, f32[38,3,128]{2,0,1:T(8,128)S(1)}, u32[]{:S(2)}, u32[]{:S(2)}) %collective-permute-start.13) | collective-permute-done | bytes 58400 | tf_op jit(solution)/shard_map/ppermute | solution.py:30
  66.6 2.6 %add_multiply_fusion.1 = f32[32,8,128]{2,0,1:T(8,128)S(1)} fusion(f32[38,11,128]{2,0,1:T(8,128)S(1)} %get-tuple-element.59, f32[3,8,128]{2,0,1:T(4,128)S(1)} %collective-permute-done.11, f32[32,8,128]{2,0,1:T(8,128)S(1)} %fusion.131, f32[38,11,128]{2,0,1:T(8,128)S(1)} %get-tuple-element.58, f32[3,8,128]{2,0,1:T(4,128)S(1)} %collective-permute-done.10, ...), kind=kLoop, calls=%fused_computation.251 | loop fusion | flops 5144576 | bytes 5853184 | tf_op jit(solution)/shard_map/div | solution.py:91
  (79 shorter events, 8.5 us)
Async XLA Ops:
  0.6 15.7 %copy-start.2 = (f32[32,8,128]{2,1,0:T(8,128)S(1)}, f32[32,8,128]{2,1,0:T(8,128)}, u32[]{:S(2)}) copy-start(f32[32,8,128]{2,1,0:T(8,128)} %param.13) | copy-start | bytes 393220
  0.6 15.7 %copy-start = (f32[3,32,8,128]{3,2,1,0:T(8,128)S(1)}, f32[3,32,8,128]{3,2,1,0:T(8,128)}, u32[]{:S(2)}) copy-start(f32[3,32,8,128]{3,2,1,0:T(8,128)} %param.12) | copy-start | bytes 1179652
  0.7 15.7 %copy-start.1 = (f32[3,32,8,128]{3,2,1,0:T(8,128)S(1)}, f32[3,32,8,128]{3,2,1,0:T(8,128)}, u32[]{:S(2)}) copy-start(f32[3,32,8,128]{3,2,1,0:T(8,128)} %param.11) | copy-start | bytes 1179652
  2.8 20.4 %collective-permute-start.1 = (f32[6,2,8,128]{3,2,1,0:T(8,128)S(1)}, f32[6,2,8,128]{3,2,1,0:T(8,128)S(1)}, u32[]{:S(2)}, u32[]{:S(2)}) collective-permute-start(f32[6,2,8,128]{3,2,1,0:T(8,128)S(1)} %get-tuple-element.57), channel_id=1, source_target_pairs={{8,0},{16,8},{24,16},{9,1},{17,9},{25,17},{10,2},{18,10},{26,18},{... | collective-permute-start | bytes 147464 | tf_op jit(solution)/shard_map/ppermute | solution.py:30
  4.7 18.5 %collective-permute-start = (f32[6,2,8,128]{3,2,1,0:T(8,128)S(1)}, f32[6,2,8,128]{3,2,1,0:T(8,128)S(1)}, u32[]{:S(2)}, u32[]{:S(2)}) collective-permute-start(f32[6,2,8,128]{3,2,1,0:T(8,128)S(1)} %get-tuple-element.56), channel_id=1, source_target_pairs={{0,8},{8,16},{16,24},{1,9},{9,17},{17,25},{2,10},{10,18},{18,26},{... | collective-permute-start | bytes 147464 | tf_op jit(solution)/shard_map/ppermute | solution.py:29
  8.0 5.6 %collective-permute-start.5 = (f32[7,1,8,128]{3,2,1,0:T(8,128)S(1)}, f32[7,1,8,128]{3,2,1,0:T(8,128)S(1)}, u32[]{:S(2)}, u32[]{:S(2)}) collective-permute-start(f32[7,1,8,128]{3,2,1,0:T(8,128)S(1)} %get-tuple-element.27), channel_id=1, source_target_pairs={{8,0},{16,8},{24,16},{9,1},{17,9},{25,17},{10,2},{18,10},{26,18},{... | collective-permute-start | bytes 86024 | tf_op jit(solution)/shard_map/ppermute | solution.py:30
  11.1 5.2 %collective-permute-start.4 = (f32[7,1,8,128]{3,2,1,0:T(8,128)S(1)}, f32[7,1,8,128]{3,2,1,0:T(8,128)S(1)}, u32[]{:S(2)}, u32[]{:S(2)}) collective-permute-start(f32[7,1,8,128]{3,2,1,0:T(8,128)S(1)} %get-tuple-element.26), channel_id=1, source_target_pairs={{0,8},{8,16},{16,24},{1,9},{9,17},{17,25},{2,10},{10,18},{18,26},{... | collective-permute-start | bytes 86024 | tf_op jit(solution)/shard_map/ppermute | solution.py:29
  16.5 13.7 %collective-permute-start.7 = (f32[7,34,1,128]{3,2,1,0:T(1,128)S(1)}, f32[7,34,1,128]{3,2,1,0:T(1,128)S(1)}, u32[]{:S(2)}, u32[]{:S(2)}) collective-permute-start(f32[7,34,1,128]{3,2,1,0:T(1,128)S(1)} %get-tuple-element.25), channel_id=1, source_target_pairs={{1,0},{2,1},{3,2},{4,3},{5,4},{6,5},{7,6},{9,8},{10,9},{11,10},{12... | collective-permute-start | bytes 365576 | tf_op jit(solution)/shard_map/ppermute | solution.py:30
  18.9 11.3 %collective-permute-start.6 = (f32[7,34,1,128]{3,2,1,0:T(1,128)S(1)}, f32[7,34,1,128]{3,2,1,0:T(1,128)S(1)}, u32[]{:S(2)}, u32[]{:S(2)}) collective-permute-start(f32[7,34,1,128]{3,2,1,0:T(1,128)S(1)} %get-tuple-element.24), channel_id=1, source_target_pairs={{0,1},{1,2},{2,3},{3,4},{4,5},{5,6},{6,7},{8,9},{9,10},{10,11},{11... | collective-permute-start | bytes 365576 | tf_op jit(solution)/shard_map/ppermute | solution.py:29
  23.4 9.0 %collective-permute-start.3 = (f32[6,36,2,128]{3,2,1,0:T(2,128)S(1)}, f32[6,36,2,128]{3,2,1,0:T(2,128)S(1)}, u32[]{:S(2)}, u32[]{:S(2)}) collective-permute-start(f32[6,36,2,128]{3,2,1,0:T(2,128)S(1)} %get-tuple-element.55), channel_id=1, source_target_pairs={{1,0},{2,1},{3,2},{4,3},{5,4},{6,5},{7,6},{9,8},{10,9},{11,10},{12... | collective-permute-start | bytes 663560 | tf_op jit(solution)/shard_map/ppermute | solution.py:30
  25.3 10.3 %collective-permute-start.2 = (f32[6,36,2,128]{3,2,1,0:T(2,128)S(1)}, f32[6,36,2,128]{3,2,1,0:T(2,128)S(1)}, u32[]{:S(2)}, u32[]{:S(2)}) collective-permute-start(f32[6,36,2,128]{3,2,1,0:T(2,128)S(1)} %get-tuple-element.54), channel_id=1, source_target_pairs={{0,1},{1,2},{2,3},{3,4},{4,5},{5,6},{6,7},{8,9},{9,10},{10,11},{11... | collective-permute-start | bytes 663560 | tf_op jit(solution)/shard_map/ppermute | solution.py:29
  38.9 1.1 %copy-start.3 = (f32[2,3,32,8,128]{4,3,2,1,0:T(8,128)S(1)}, f32[2,3,32,8,128]{4,3,2,1,0:T(8,128)}, u32[]{:S(2)}) copy-start(f32[2,3,32,8,128]{4,3,2,1,0:T(8,128)} %param.14) | copy-start | bytes 2359300
  40.1 1.2 %copy-start.6 = (s32[8]{0:T(128)S(1)}, s32[8]{0:T(128)}, u32[]{:S(2)}) copy-start(s32[8]{0:T(128)} %param.16) | copy-start | bytes 100
  40.1 8.7 %copy-start.4 = (s32[32,8,128]{2,1,0:T(8,128)S(1)}, s32[32,8,128]{2,1,0:T(8,128)}, u32[]{:S(2)}) copy-start(s32[32,8,128]{2,1,0:T(8,128)} %param.15) | copy-start | bytes 393220
  40.1 13.2 %copy-start.5 = (s32[32,8]{0,1:T(8,128)S(1)}, s32[32,8]{0,1:T(8,128)}, u32[]{:S(2)}) copy-start(s32[32,8]{0,1:T(8,128)} %param.17) | copy-start | bytes 3076
  41.2 1.4 %collective-permute-start.8 = (f32[32,8,128]{2,0,1:T(8,128)S(1)}, f32[32,8,128]{2,0,1:T(8,128)S(1)}, u32[]{:S(2)}, u32[]{:S(2)}) collective-permute-start(f32[32,8,128]{2,0,1:T(8,128)S(1)} %copy_add_fusion), channel_id=1, source_target_pairs={{0,8},{8,0},{16,24},{24,16},{1,9},{9,1},{17,25},{25,17},{2,10},{10... | collective-permute-start | bytes 393224 | tf_op jit(solution)/shard_map/ppermute | solution.py:42
  42.6 5.6 %collective-permute-start.9 = (f32[32,8,128]{2,0,1:T(8,128)S(1)}, f32[32,8,128]{2,0,1:T(8,128)S(1)}, u32[]{:S(2)}, u32[]{:S(2)}) collective-permute-start(f32[32,8,128]{2,0,1:T(8,128)S(1)} %collective-permute-done.8), channel_id=1, source_target_pairs={{0,16},{16,0},{8,24},{24,8},{1,17},{17,1},{9,25},{25,9},{2,18},{18... | collective-permute-start | bytes 393224 | tf_op jit(solution)/shard_map/ppermute | solution.py:42
  48.9 4.4 %collective-permute-start.11 = (f32[3,8,128]{2,0,1:T(4,128)S(1)}, f32[3,8,128]{2,0,1:T(4,128)S(1)}, u32[]{:S(2)}, u32[]{:S(2)}) collective-permute-start(f32[3,8,128]{2,0,1:T(4,128)S(1)} %get-tuple-element.63), channel_id=1, source_target_pairs={{8,0},{16,8},{24,16},{9,1},{17,9},{25,17},{10,2},{18,10},{26,18},{... | collective-permute-start | bytes 36872 | tf_op jit(solution)/shard_map/ppermute | solution.py:30
  51.3 5.1 %collective-permute-start.10 = (f32[3,8,128]{2,0,1:T(4,128)S(1)}, f32[3,8,128]{2,0,1:T(4,128)S(1)}, u32[]{:S(2)}, u32[]{:S(2)}) collective-permute-start(f32[3,8,128]{2,0,1:T(4,128)S(1)} %get-tuple-element.62), channel_id=1, source_target_pairs={{0,8},{8,16},{16,24},{1,9},{9,17},{17,25},{2,10},{10,18},{18,26},{... | collective-permute-start | bytes 36872 | tf_op jit(solution)/shard_map/ppermute | solution.py:29
  56.4 6.8 %collective-permute-start.12 = (f32[38,3,128]{2,0,1:T(8,128)S(1)}, f32[38,3,128]{2,0,1:T(8,128)S(1)}, u32[]{:S(2)}, u32[]{:S(2)}) collective-permute-start(f32[38,3,128]{2,0,1:T(8,128)S(1)} %get-tuple-element.60), channel_id=1, source_target_pairs={{0,1},{1,2},{2,3},{3,4},{4,5},{5,6},{6,7},{8,9},{9,10},{10,11},{11... | collective-permute-start | bytes 175112 | tf_op jit(solution)/shard_map/ppermute | solution.py:29
  59.6 7.0 %collective-permute-start.13 = (f32[38,3,128]{2,0,1:T(8,128)S(1)}, f32[38,3,128]{2,0,1:T(8,128)S(1)}, u32[]{:S(2)}, u32[]{:S(2)}) collective-permute-start(f32[38,3,128]{2,0,1:T(8,128)S(1)} %get-tuple-element.61), channel_id=1, source_target_pairs={{1,0},{2,1},{3,2},{4,3},{5,4},{6,5},{7,6},{9,8},{10,9},{11,10},{12... | collective-permute-start | bytes 175112 | tf_op jit(solution)/shard_map/ppermute | solution.py:30
where the time goes:
time: 70.5 us; the launch traced here: 70 us
  starting transfers between devices  34.6 us (49%)
  waiting for transfers between devices  17.8 us (25%)
  other arithmetic  9.97 us (14%)
  local copies, waits for them, and re-layouts  6.44 us (9%)
  between operations  1.18 us (2%)
    ppermute x6, starting transfers between devices, padded(): before = lax.ppermute(last, axis, up)  18.6 us
    ppermute x6, starting transfers between devices, padded(): after = lax.ppermute(initial, axis, down)  14.4 us
    ppermute x6, waiting for transfers between devices, padded(): before = lax.ppermute(last, axis, up)  9 us
    ppermute x2, waiting for transfers between devices, swapped(): return lax.ppermute(block, axis, route)  5.31 us
    ppermute x6, waiting for transfers between devices, padded(): after = lax.ppermute(initial, axis, down)  3.44 us
    div x1, other arithmetic, project(): return (top + jnp.tanh(SHARPNESS * (filtered - THRESHOLD))) / bottom  2.64 us
    unnamed x16, local copies, waits for them, and re-layouts  2.64 us
    concatenate x3, other arithmetic, padded(): array = jnp.concatenate([before, array, after], axis=dim)  2.48 us
  transfers between devices with their start and end apart: 14, of which 6 were waited for; matrix products, arithmetic and copies ran while one was open for 7% of the time, Pallas kernels for 0%

commit v1 on v0

v1 whole, which is shorter than its diff:
```python
import functools
import math

import jax
import jax.numpy as jnp
from jax import lax
from jax.experimental import pallas as pl
from jax.experimental.pallas import tpu as pltpu
from jax.sharding import PartitionSpec as P

STEPS = 2
RMAX = 4

COURANT = 0.5
DAMPING = 0.9
OMEGA_SQUARED = 0.3
LORENTZ_STRENGTH = 2.0
EPS_MATERIAL = 4.0
UPDATE_STEP = 0.25
SHARPNESS = 4.0
THRESHOLD = 0.5

AXES = ("gx", "gy")
WIDTH = RMAX - 1
SLOTS = 20
BASE = 8
EXTRA = 8
VMEM = pltpu.VMEM


def x_even(x, y, nx, ny):
    return x ^ 1, y


def x_odd(x, y, nx, ny):
    other = x + 1 if x % 2 else x - 1
    return (other, y) if 0 <= other < nx else (x, y ^ 1)


def y_even(x, y, nx, ny):
    return x, y ^ 1


def y_odd(x, y, nx, ny):
    other = y + 1 if y % 2 else y - 1
    return (x, other) if 0 <= other < ny else (x ^ 1, y)


def mirror(x, y, nx, ny):
    return nx - 1 - x, y


def mirror_even(x, y, nx, ny):
    return nx - 1 - (x ^ 1), y


def mirror_odd(x, y, nx, ny):
    other = x + 1 if x % 2 else x - 1
    return (nx - 1 - other, y) if 0 <= other < nx else (nx - 1 - x, y)


def send(block, rule):
    nx, ny = lax.axis_size("gx"), lax.axis_size("gy")
    route = []
    for x in range(nx):
        for y in range(ny):
            to_x, to_y = rule(x, y, nx, ny)
            route.append((x * ny + y, to_x * ny + to_y))
    return lax.ppermute(block, AXES, route)


def odd_x():
    return lax.rem(lax.axis_index("gx"), 2) == 1


def odd_y():
    return lax.rem(lax.axis_index("gy"), 2) == 1


def edges():
    x, y = lax.axis_index("gx"), lax.axis_index("gy")
    return (x > 0, x < lax.axis_size("gx") - 1, y > 0, y < lax.axis_size("gy") - 1)


def rows_of(shape):
    return lax.broadcasted_iota(jnp.int32, shape, len(shape) - 2)


def lanes_of(shape):
    return lax.broadcasted_iota(jnp.int32, shape, len(shape) - 1)


def ahead_z(v):
    depth = v.shape[-1]
    return jnp.where(lanes_of(v.shape) == depth - 1, 0.0, pltpu.roll(v, depth - 1, v.ndim - 1))


def behind_z(v):
    return jnp.where(lanes_of(v.shape) == 0, 0.0, pltpu.roll(v, 1, v.ndim - 1))


def ahead_y(v, edge=0.0):
    rows = v.shape[-2]
    return jnp.where(rows_of(v.shape) == rows - 1, edge, pltpu.roll(v, rows - 1, v.ndim - 2))


def behind_y(v, edge=0.0):
    return jnp.where(rows_of(v.shape) == 0, edge, pltpu.roll(v, 1, v.ndim - 2))


def keep(flag, v):
    return jnp.where(flag, v, 0.0)


def call(kernel, outs, args, aliases=None, flops=0):
    args = [a if m is pltpu.SMEM else pltpu.with_memory_space_constraint(a, VMEM) for a, m in [(a, VMEM) for a in args]]
    shapes = tuple(VMEM(s, jnp.float32) for s in outs)
    spec = pl.BlockSpec(memory_space=VMEM)
    traffic = 4 * (sum(math.prod(s) for s in outs) + sum(math.prod(a.shape) for a in args))
    return pl.pallas_call(
        kernel,
        out_shape=shapes,
        in_specs=[spec] * len(args),
        out_specs=tuple([spec] * len(outs)),
        input_output_aliases=aliases or {},
        cost_estimate=pl.CostEstimate(flops=flops, bytes_accessed=traffic, transcendentals=0),
        compiler_params=pltpu.CompilerParams(vmem_limit_bytes=16 * 2**20),
    )(*args)


def pack_x(n, r, e, h, p, q, d, m, even_out, odd_out):
    odd = odd_x()
    for out, low in ((even_out, odd), (odd_out, jnp.logical_not(odd))):
        near = jnp.where(low, 0, n - 1)
        step = jnp.where(low, 1, -1)
        at = [pl.ds(pl.multiple_of((near + k * step) * r, r), r) for k in range(WIDTH)]

        def put(slot, v):
            out[slot * r : (slot + 1) * r, :] = v

        for c in range(3):
            put(c, e[c, at[0], :])
            put(3 + c, h[c, at[0], :])
            put(6 + c, DAMPING * q[c, at[0], :] - OMEGA_SQUARED * p[c, at[0], :])
            put(10 + c, e[c, at[1], :])
        put(9, d[at[0], :])
        put(13, h[1, at[1], :])
        put(14, h[2, at[1], :])
        put(15, d[at[1], :])
        put(16, d[at[2], :])
        for k in range(WIDTH):
            put(17 + k, m[at[k], :].astype(jnp.float32))


def new_h(h, e, e_next, edge_x=0.0, edge_z=0.0):
    ex, ey, ez = e
    return (
        h[0] - COURANT * ((ahead_y(ez, edge_z) - ez) - (ahead_z(ey) - ey)),
        h[1] - COURANT * ((ahead_z(ex) - ex) - (e_next[2] - ez)),
        h[2] - COURANT * ((e_next[1] - ey) - (ahead_y(ex, edge_x) - ex)),
    )


def curl_h(h, h_last, edge_x=0.0, edge_z=0.0):
    hx, hy, hz = h
    return (
        (hz - behind_y(hz, edge_z)) - (hy - behind_z(hy)),
        (hx - behind_z(hx)) - (hz - h_last[2]),
        (hy - h_last[1]) - (hx - behind_y(hx, edge_x)),
    )


def half_over_eps(d):
    return COURANT / (1.0 + (EPS_MATERIAL - 1.0) * d)


def step_inner(n, r, block, e, h, p, q, d, h_out, e_out, c_out, t_out):
    def plane(ref, x, c=None):
        at = pl.ds(pl.multiple_of(x * r, r), r)
        return ref[at, :] if c is None else ref[c, at, :]

    def put(ref, x, v, c=None):
        at = pl.ds(pl.multiple_of(x * r, r), r)
        if c is None:
            ref[at, :] = v
        else:
            ref[c, at, :] = v

    def one(x, last):
        now = [plane(e, x, c) for c in range(3)]
        nxt = [plane(e, jnp.minimum(x + 1, n - 1), c) for c in range(3)]
        mine = new_h([plane(h, x, c) for c in range(3)], now, nxt)
        dd = plane(d, x)
        half = half_over_eps(dd)
        put(c_out, x + 1, half)
        curl = curl_h(mine, last)
        for c in range(3):
            old = plane(p, x, c)
            rate = DAMPING * plane(q, x, c) - OMEGA_SQUARED * old + (OMEGA_SQUARED * LORENTZ_STRENGTH) * dd * now[c]
            put(t_out, x, (DAMPING - OMEGA_SQUARED) * rate - OMEGA_SQUARED * old, c)
            put(h_out, x + 1, mine[c], c)
            put(e_out, x + 1, now[c] + half * (curl[c] - 2.0 * rate), c)
        return mine

    def body(i, last):
        for k in range(block):
            last = one(i * block + k, last)
        return last

    zero = jnp.zeros((r, e.shape[-1]), jnp.float32)
    lax.fori_loop(0, n // block, body, (zero, zero, zero))


def step_edges(n, r, e, h, p, q, d, even, odd, h_in, e_in, c_in, h_out, e_out, c_out, rows_out, even_y, odd_y_out):
    del h_in, e_in, c_in
    flip = odd_x()
    below, above, _, _ = edges()

    def lo(slot):
        at = slice(slot * r, (slot + 1) * r)
        return keep(below, jnp.where(flip, even[at, :], odd[at, :]))

    def hi(slot):
        at = slice(slot * r, (slot + 1) * r)
        return keep(above, jnp.where(flip, odd[at, :], even[at, :]))

    def own(ref, x):
        return [ref[c, x * r : (x + 1) * r, :] for c in range(3)]

    def at(x):
        return slice((x + 1) * r, (x + 2) * r)

    e_m2, e_m1 = [lo(10), lo(11), lo(12)], [lo(0), lo(1), lo(2)]
    e_n, e_n1 = [hi(0), hi(1), hi(2)], [hi(10), hi(11), hi(12)]
    e_0, e_l = own(e, 0), own(e, n - 1)
    h_m2 = new_h([lo(13), lo(13), lo(14)], e_m2, e_m1)
    h_m1 = [keep(below, v) for v in new_h([lo(3), lo(4), lo(5)], e_m1, e_0)]
    h_l = new_h(own(h, n - 1), e_l, e_n)
    h_n = new_h([hi(3), hi(4), hi(5)], e_n, e_n1)
    h_0 = [h_out[c, at(0), :] for c in range(3)]
    h_l1 = [h_out[c, at(n - 2), :] for c in range(3)]

    def new_e(x, electric, magnetic, last, drift, density, flag=None):
        half = half_over_eps(density)
        if flag is not None:
            half = keep(flag, half)
            c_out[at(x), :] = half
        curl = curl_h(magnetic, last)
        for c in range(3):
            rate = drift[c] + (OMEGA_SQUARED * LORENTZ_STRENGTH) * density * electric[c]
            e_out[c, at(x), :] = electric[c] + half * (curl[c] - 2.0 * rate)

    def drift(x):
        return [DAMPING * b - OMEGA_SQUARED * a for a, b in zip(own(p, x), own(q, x))]

    for c in range(3):
        h_out[c, at(-1), :] = h_m1[c]
        h_out[c, at(n - 1), :] = h_l[c]
        h_out[c, at(n), :] = h_n[c]
    new_e(-1, e_m1, h_m1, h_m2, [lo(6), lo(7), lo(8)], lo(9), below)
    new_e(0, e_0, h_0, h_m1, drift(0), d[:r, :])
    new_e(n - 1, e_l, h_l, h_l1, drift(n - 1), d[(n - 1) * r :, :])
    new_e(n, e_n, h_n, h_l, [hi(6), hi(7), hi(8)], hi(9), above)

    for k, c in enumerate((0, 2)):
        rows_out[k, BASE - 1 : BASE, :] = e_m1[c][:1]
        rows_out[k, BASE : BASE + n, :] = e[c, pl.ds(0, n, stride=r), :]
        rows_out[k, BASE + n : BASE + n + 1, :] = e_n[c][:1]

    def row(ref, y, first, c=None):
        start = (first + 1) * r + y
        if c is None:
            return ref[pl.ds(start, n, stride=r), :]
        return ref[c, pl.ds(start, n, stride=r), :]

    last = r - 1
    g_x, g_z = row(h_out, last, 0, 0), row(h_out, last, 0, 2)
    a_x, a_y, a_y1, a_z = (row(e_out, last, 0, 0), row(e_out, last, 0, 1), row(e_out, last, 1, 1), row(e_out, last, 0, 2))
    up = [
        g_x,
        g_z,
        g_x + COURANT * a_z + COURANT * (ahead_z(a_y) - a_y),
        g_z - COURANT * (a_y1 - a_y) - COURANT * a_x,
        row(c_out, last, 0),
    ]
    down = [row(e_out, 0, 0, 0), row(e_out, 0, 0, 2), row(c_out, 0, 0), rows_out[0, BASE : BASE + n, :], rows_out[1, BASE : BASE + n, :]]
    flip_y = odd_y()
    for k in range(5):
        even_y[k * n : (k + 1) * n, :] = jnp.where(flip_y, down[k], up[k])
        odd_y_out[k * n : (k + 1) * n, :] = jnp.where(flip_y, up[k], down[k])
    up_more = [
        h_m1[0][last:],
        h_n[0][last:],
        h_m1[2][last:],
        c_out[(n + 1) * r + last : (n + 1) * r + last + 1, :],
    ]
    down_more = [
        e_out[0, 0:1, :],
        c_out[0:1, :],
        e_m2[0][:1],
        e_m1[0][:1],
        e_m1[2][:1],
        e_n[0][:1],
        e_n[2][:1],
    ]
    zero = jnp.zeros_like(up_more[0])
    for k in range(EXTRA):
        u = up_more[k] if k < len(up_more) else zero
        v = down_more[k] if k < len(down_more) else zero
        even_y[5 * n + k : 5 * n + k + 1, :] = jnp.where(flip_y, v, u)
        odd_y_out[5 * n + k : 5 * n + k + 1, :] = jnp.where(flip_y, u, v)


def step_last(n, r, block, h, e, c_ref, t, d, rows, even, odd, f, e_out, h_out, g_out, edge_out, hs, es, fix, h_edge):
    flip = odd_y()
    below, above, low, high = edges()
    hxm, hzm, dx, dz, ry, exp_, ezp, hxm2, hzm2, wm = range(10)
    last = r - 1

    def up(k, size=None):
        start, size = (k * n, n) if size is None else (5 * n + k, 1)
        return keep(low, jnp.where(flip, even[start : start + size, :], odd[start : start + size, :]))

    def down(k, size=None):
        start, size = (k * n, n) if size is None else (5 * n + k, 1)
        return keep(high, jnp.where(flip, odd[start : start + size, :], even[start : start + size, :]))

    def put(which, v, x=0):
        fix[which, BASE + x : BASE + x + v.shape[0], :] = v

    def get(which, x=0, size=n):
        return fix[which, BASE + x : BASE + x + size, :]

    def row_e(k, x=0, size=n):
        return rows[k, BASE + x : BASE + x + size, :]

    def strided(ref, y, c, x=0):
        return ref[c, pl.ds((x + 1) * r + y, n, stride=r), :]

    put(hxm, up(0) - COURANT * keep(low, row_e(1)))
    put(hxm, up(0, 1) - COURANT * keep(low, row_e(1, -1, 1)), -1)
    put(hxm, up(1, 1) - COURANT * keep(low, row_e(1, n, 1)), n)
    put(hzm, up(1) + COURANT * keep(low, row_e(0)))
    put(hzm, up(2, 1) + COURANT * keep(low, row_e(0, -1, 1)), -1)
    put(hzm, jnp.zeros((1, hs.shape[-1]), jnp.float32), n)
    put(dz, COURANT * down(3))
    put(dz, COURANT * down(2, 1), -2)
    put(dz, COURANT * down(3, 1), -1)
    put(dz, COURANT * down(5, 1), n)
    put(dx, -COURANT * down(4))
    put(dx, -COURANT * down(4, 1), -1)
    put(dx, -COURANT * down(6, 1), n)
    for x, size in ((0, n), (-1, 1), (n, 1)):
        delta = get(dx, x, size)
        put(ry, delta - behind_z(delta) - get(dz, x, size) + get(dz, x - 1, size), x)

    shape = (r, hs.shape[-1])
    first_row, last_row = rows_of(shape) == 0, rows_of(shape) == last

    def spread(which, x):
        return fix[which, pl.ds(BASE + x, 1), :]

    def amend(x):
        at = pl.ds(pl.multiple_of((x + 1) * r, r), r)
        half = c_ref[at, :]
        d_x, d_z = jnp.where(last_row, spread(dx, x), 0.0), jnp.where(last_row, spread(dz, x), 0.0)
        hs[0, at, :] = h[0, at, :] + d_x
        hs[1, at, :] = h[1, at, :]
        hs[2, at, :] = h[2, at, :] + d_z
        es[0, at, :] = e[0, at, :] + half * jnp.where(first_row, -spread(hzm, x), d_z)
        es[1, at, :] = e[1, at, :] + half * jnp.where(last_row, spread(ry, x), 0.0)
        es[2, at, :] = e[2, at, :] + half * jnp.where(first_row, spread(hxm, x), -d_x)

    def amend_block(i, carry):
        for k in range(block):
            amend(i * block + k)
        return carry

    amend(-1)
    amend(n)
    lax.fori_loop(0, n // block, amend_block, 0)

    half = down(2)
    put(exp_, down(0) - half * strided(hs, last, 2))
    put(exp_, down(0, 1) - down(1, 1) * hs[2, last : last + 1, :], -1)
    put(ezp, down(1) + half * strided(hs, last, 0))
    half = up(4)

    def gain(x, size, factor):
        delta = -COURANT * row_e(1, x, size)
        step = COURANT * (row_e(0, x, size) - row_e(0, x - 1, size))
        return factor * (delta - behind_z(delta) - step)

    put(wm, gain(0, n, half))
    put(wm, gain(n, 1, up(3, 1)), n)
    delta_x, delta_z = -COURANT * row_e(1), COURANT * row_e(0)
    change = get(wm)
    put(
        hxm2,
        keep(
            low,
            up(2) + delta_x - COURANT * half * delta_x + COURANT * (ahead_z(change) - change) - COURANT * strided(es, 0, 2),
        ),
    )
    put(
        hzm2,
        keep(
            low,
            up(3) + delta_z - COURANT * (get(wm, 1) - change) - COURANT * half * delta_z + COURANT * strided(es, 0, 0),
        ),
    )

    def fields(ref, x):
        at = pl.ds(pl.multiple_of((x + 1) * r, r), r)
        return [ref[c, at, :] for c in range(3)]

    def second_h(x):
        return new_h(fields(hs, x), fields(es, x), fields(es, x + 1), spread(exp_, x), spread(ezp, x))

    def one(x, last_h):
        now = fields(es, x)
        mine = second_h(x)
        at = pl.ds(pl.multiple_of(x * r, r), r)
        half = c_ref[pl.ds(pl.multiple_of((x + 1) * r, r), r), :]
        dd = d[at, :]
        curl = curl_h(mine, last_h, spread(hxm2, x), spread(hzm2, x))
        total = None
        for c in range(3):
            rate = t[c, at, :] + (OMEGA_SQUARED * LORENTZ_STRENGTH) * dd * now[c]
            after = now[c] + half * (curl[c] - 2.0 * rate)
            e_out[c, at, :] = after
            h_out[c, at, :] = mine[c]
            part = now[c] * f[c, at, :] + after * f[3 + c, at, :]
            total = part if total is None else total + part
        g_out[at, :] = total
        return mine

    def body(i, last_h):
        for k in range(block):
            last_h = one(i * block + k, last_h)
        return last_h

    start = tuple(keep(below, v) for v in second_h(-1))
    lax.fori_loop(0, n // block, body, start)
    first = jnp.where(odd_x(), 0, n - WIDTH)
    edge_out[...] = g_out[pl.ds(pl.multiple_of(first * r, r), WIDTH * r), :]


def update(n, r, generic, *refs):
    if generic:
        g, other, edge, edge_m, far, far_m, d, m, even, odd, order, u_out, even_y, odd_y_out, u_pad = refs
    else:
        g, other, edge, edge_m, d, m, even, odd, order, u_out, even_y, odd_y_out, u_pad = refs
    flip = odd_x()
    below, above, _, _ = edges()
    perm = order[...]

    def paired(v):
        return jnp.take_along_axis(v, perm, axis=0, mode="promise_in_bounds")

    def plane(ref, x):
        return ref[pl.ds(pl.multiple_of(x * r, r), r), :]

    def put(k, v):
        at = pl.ds(pl.multiple_of(k * r, r), r)
        u_out[at, :] = v
        u_pad[at, :] = v

    scale = 0.5 * UPDATE_STEP
    for x in range(n):
        put(x + WIDTH, plane(d, x) - scale * plane(m, x).astype(jnp.float32) * (plane(g, x) + paired(plane(other, n - 1 - x))))
    slots = (9, 15, 16)
    for j in range(WIDTH):
        high, low = n + WIDTH + j, WIDTH - 1 - j
        back, forth = jnp.where(flip, j, WIDTH - 1 - j), jnp.where(flip, WIDTH - 1 - j, j)
        u = plane(even, slots[j]) - scale * plane(even, 17 + j) * (plane(edge, forth) + paired(plane(edge_m, back)))
        put(jnp.where(flip, low, high), u)
        if generic:
            near, mirrored = plane(far, back), plane(far_m, forth)
        else:
            near = plane(other, jnp.where(flip, j, n - 1 - j))
            mirrored = plane(g, jnp.where(flip, n - 1 - j, j))
        u = plane(odd, slots[j]) - scale * plane(odd, 17 + j) * (near + paired(mirrored))
        put(jnp.where(flip, high, low), keep(jnp.where(flip, above, below), u))
    flip_y = odd_y()
    wide = u_pad.shape[0] // r
    for j in range(WIDTH):
        upper = u_pad[pl.ds(r - WIDTH + j, wide, stride=r), :]
        lower = u_pad[pl.ds(j, wide, stride=r), :]
        at = slice(j * wide, (j + 1) * wide)
        even_y[at, :] = jnp.where(flip_y, lower, upper)
        odd_y_out[at, :] = jnp.where(flip_y, upper, lower)


CLASSES = (
    (0.0, ((0, 0),)),
    (1.0, ((0, 1), (1, 0))),
    (2.0, ((1, 1),)),
    (4.0, ((2, 0), (0, 2))),
    (5.0, ((2, 1), (1, 2))),
    (8.0, ((2, 2),)),
    (9.0, ((3, 0), (0, 3))),
    (10.0, ((3, 1), (1, 3))),
    (13.0, ((3, 2), (2, 3))),
    (18.0, ((3, 3),)),
)


def weight(radius, square):
    return jnp.maximum(radius - math.sqrt(square), 0.0)


def cover(n, r, radius, out):
    x0, y0 = lax.axis_index("gx") * n, lax.axis_index("gy") * r
    total_x, total_y = n * lax.axis_size("gx"), r * lax.axis_size("gy")
    shape = (r, out.shape[-1])
    y = y0 + rows_of(shape)
    one = jnp.ones(shape, jnp.float32)

    def there(where, total):
        return ((where >= 0) & (where < total)).astype(jnp.float32)

    across = [one] + [there(y - b, total_y) + there(y + b, total_y) for b in range(1, RMAX)]

    def body(x, carry):
        at = pl.ds(pl.multiple_of(x * r, r), r)
        rad = radius[at, :]
        where = jnp.full(shape, x0 + x, jnp.int32)
        along = [one] + [there(where - a, total_x) + there(where + a, total_x) for a in range(1, RMAX)]
        total = None
        for square, members in CLASSES:
            part = sum(across[b] * along[a] for b, a in members)
            part = weight(rad, square) * part
            total = part if total is None else total + part
        out[at, :] = 1.0 / total
        return carry

    lax.fori_loop(0, n, body, 0)


def smooth(n, r, block, u, even, odd, radius, inverse, out, halo, sums):
    flip = odd_y()
    _, _, low, high = edges()
    wide = even.shape[0] // WIDTH
    full = n + 2 * WIDTH
    for j in range(WIDTH):
        at = slice(j * wide, (j + 1) * wide)
        lower = keep(low, jnp.where(flip, even[at, :], odd[at, :]))
        upper = keep(high, jnp.where(flip, odd[at, :], even[at, :]))
        halo[pl.ds(r - WIDTH + j, wide, stride=r), :] = lower
        halo[pl.ds(j, wide, stride=r), :] = upper
    shape = (r, u.shape[-1])
    row = rows_of(shape)

    def fold(k):
        at = pl.ds(pl.multiple_of(k * r, r), r)
        mine, beside = u[at, :], halo[at, :]
        for b in range(1, RMAX):
            upper = pltpu.roll(jnp.where(row < b, beside, mine), r - b, 0)
            lower = pltpu.roll(jnp.where(row >= r - b, beside, mine), b, 0)
            sums[b - 1, at, :] = upper + lower

    def fold_block(i, carry):
        for k in range(block):
            fold(i * block + k)
        return carry

    whole = full // block
    lax.fori_loop(0, whole, fold_block, 0)
    for k in range(whole * block, full):
        fold(k)

    top = math.tanh(SHARPNESS * THRESHOLD)
    bottom = top + math.tanh(SHARPNESS * (1.0 - THRESHOLD))

    def one(x):
        at = pl.ds(pl.multiple_of(x * r, r), r)
        rad = radius[at, :]

        def line(b, a):
            where = pl.ds(pl.multiple_of((x + WIDTH + a) * r, r), r)
            return u[where, :] if b == 0 else sums[b - 1, where, :]

        total = None
        for square, members in CLASSES:
            part = None
            for b, a in members:
                v = line(b, 0) if a == 0 else line(b, a) + line(b, -a)
                part = v if part is None else part + v
            part = weight(rad, square) * part
            total = part if total is None else total + part
        filtered = total * inverse[at, :]
        out[at, :] = (top + jnp.tanh(SHARPNESS * (filtered - THRESHOLD))) / bottom

    def body(i, carry):
        for k in range(block):
            one(i * block + k)
        return carry

    lax.fori_loop(0, n // block, body, 0)


def local(
    adj_electric,
    adj_magnetic,
    polarization,
    pol_rate,
    density,
    forward_rate,
    design_mask,
    partner_rows,
    filter_radius,
):
    n, r, depth = density.shape
    size = n * r
    e, h = adj_electric.reshape(3, size, depth), adj_magnetic.reshape(3, size, depth)
    p, q = polarization.reshape(3, size, depth), pol_rate.reshape(3, size, depth)
    d, m = density.reshape(size, depth), design_mask.reshape(size, depth)
    f = forward_rate.reshape(3 * STEPS, size, depth)
    more = size + 2 * r
    face_x = (SLOTS * r, depth)
    face_y = (5 * n + EXTRA, depth)
    lines = n + 2 * BASE

    pack = functools.partial(pack_x, n, r)
    even, odd = call(pack, [face_x] * 2, [e, h, p, q, d, m])
    odd = send(odd, x_odd)
    even = send(even, x_even)

    inner = functools.partial(step_inner, n, r, 4)
    h1, e1, c1, t1 = call(inner, [(3, more, depth)] * 2 + [(more, depth), (3, size, depth)], [e, h, p, q, d], flops=100 * size * depth)
    ends = functools.partial(step_edges, n, r)
    h1, e1, c1, rows, even_y, odd_y_ = call(
        ends,
        [(3, more, depth)] * 2 + [(more, depth), (2, lines, depth)] + [face_y] * 2,
        [e, h, p, q, d, even, odd, h1, e1, c1],
        aliases={7: 0, 8: 1, 9: 2},
    )
    odd_y_ = send(odd_y_, y_odd)
    even_y = send(even_y, y_even)

    radius = jnp.broadcast_to(filter_radius.astype(jnp.float32)[:, :, None], (n, r, depth)).reshape(size, depth)
    order = jnp.broadcast_to(partner_rows[:, None], (r, depth))
    (inverse,) = call(functools.partial(cover, n, r), [(size, depth)], [radius], flops=100 * size * depth)

    final = functools.partial(step_last, n, r, 4)
    args = [h1, e1, c1, t1, d, rows, even_y, odd_y_, f]
    e2, h2, g, edge = step_call(final, n, r, depth, args)
    other = send(g, mirror)
    edge_m = send(edge, mirror_even)
    edge_e = send(edge, x_even)
    generic = lax.axis_size("gx") != 4
    extra = []
    if generic:
        start = jnp.where(lax.axis_index("gx") % 2 == 1, (n - WIDTH) * r, 0)
        far = lax.dynamic_slice_in_dim(g, start, WIDTH * r, 0)
        extra = [send(far, x_odd), send(far, mirror_odd)]
    full = n + 2 * WIDTH
    wide = -(-full // 8) * 8
    u, even_u, odd_u = scratch_call(
        functools.partial(update, n, r, generic),
        [(full * r, depth), (WIDTH * wide, depth), (WIDTH * wide, depth)],
        [g, other, edge_e, edge_m] + extra + [d, m, even, odd, order],
        [VMEM((wide * r, depth), jnp.float32)],
    )
    odd_u = send(odd_u, y_odd)
    even_u = send(even_u, y_even)
    (out,) = scratch_call(
        functools.partial(smooth, n, r, 4),
        [(size, depth)],
        [u, even_u, odd_u, radius, inverse],
        [VMEM((wide * r, depth), jnp.float32), VMEM((WIDTH, full * r, depth), jnp.float32)],
    )
    return (
        e2.reshape(3, n, r, depth),
        h2.reshape(3, n, r, depth),
        out.reshape(n, r, depth),
    )


def scratch_call(kernel, outs, args, scratch):
    args = [pltpu.with_memory_space_constraint(a, VMEM) for a in args]
    spec = pl.BlockSpec(memory_space=VMEM)
    return pl.pallas_call(
        kernel,
        out_shape=tuple(VMEM(s, jnp.float32) for s in outs),
        in_specs=[spec] * len(args),
        out_specs=tuple([spec] * len(outs)),
        scratch_shapes=scratch,
        compiler_params=pltpu.CompilerParams(vmem_limit_bytes=16 * 2**20),
    )(*args)


def step_call(kernel, n, r, depth, args):
    more = (3, (n + 2) * r, depth)
    scratch = [VMEM(more, jnp.float32)] * 2 + [VMEM((10, n + 2 * BASE, depth), jnp.float32), VMEM((2, r, depth), jnp.float32)]
    size = (3, n * r, depth)
    return scratch_call(kernel, [size, size, (n * r, depth), (WIDTH * r, depth)], args, scratch)


def solution(mesh):
    in_specs = (
        P(None, "gx", "gy", None),
        P(None, "gx", "gy", None),
        P(None, "gx", "gy", None),
        P(None, "gx", "gy", None),
        P("gx", "gy", None),
        P(None, None, "gx", "gy", None),
        P("gx", "gy", None),
        P("gy"),
        P("gx", "gy"),
    )
    out_specs = (P(None, "gx", "gy", None), P(None, "gx", "gy", None), P("gx", "gy", None))
    return jax.shard_map(local, mesh=mesh, in_specs=in_specs, out_specs=out_specs, check_vma=False)
```

time: 70.5 us -> 33.3 us (0.47)
  the two profiles are of different devices: /device:TPU:6 before, /device:TPU:8 now
where the time goes in v1:
time: 33.3 us; the launch traced here: 33 us
  waiting for transfers between devices  12.9 us (39%)
  local copies, waits for them, and re-layouts  8.28 us (25%)
  starting transfers between devices  6.51 us (20%)
  Pallas kernels  4.58 us (14%)
  between operations  0.73 us (2%)
    ppermute x9, waiting for transfers between devices, send(): return lax.ppermute(block, AXES, route)  12.9 us
    unnamed x25, local copies, waits for them, and re-layouts  7.95 us
    ppermute x9, starting transfers between devices, send(): return lax.ppermute(block, AXES, route)  6.51 us
    pallas_call x3, Pallas kernels, scratch_call(): pl.pallas_call(kernel, out_shape=tuple((VMEM(s, jnp.float32) for s in out...  2.31 us
    pallas_call x4, Pallas kernels, call(): pl.pallas_call(kernel, out_shape=shapes, in_specs=[spec] * len(args), out...  2.27 us
  transfers between devices with their start and end apart: 9, of which 7 were waited for; matrix products, arithmetic and copies ran while one was open for 5% of the time, Pallas kernels for 6%

profile of v1, /device:TPU:8, one launch (start us, length us, event | category | flops | bytes accessed | tf_op | source)
XLA Modules:
  0.0 33.0 jit_solution(17302119398495473362)
XLA Ops:
  0.6 1.0 %copy-done = f32[3,32,8,128]{3,2,1,0:T(8,128)S(1)} copy-done((f32[3,32,8,128]{3,2,1,0:T(8,128)S(1)}, f32[3,32,8,128]{3,2,1,0:T(8,128)}, u32[]{:S(2)}) %copy-start) | copy-done | bytes 393240
  1.6 1.0 %copy-done.1 = f32[3,32,8,128]{3,2,1,0:T(8,128)S(1)} copy-done((f32[3,32,8,128]{3,2,1,0:T(8,128)S(1)}, f32[3,32,8,128]{3,2,1,0:T(8,128)}, u32[]{:S(2)}) %copy-start.1) | copy-done | bytes 393240
  2.6 1.0 %copy-done.2 = f32[3,32,8,128]{3,2,1,0:T(8,128)S(1)} copy-done((f32[3,32,8,128]{3,2,1,0:T(8,128)S(1)}, f32[3,32,8,128]{3,2,1,0:T(8,128)}, u32[]{:S(2)}) %copy-start.2) | copy-done | bytes 393240
  3.6 1.0 %copy-done.3 = f32[3,32,8,128]{3,2,1,0:T(8,128)S(1)} copy-done((f32[3,32,8,128]{3,2,1,0:T(8,128)S(1)}, f32[3,32,8,128]{3,2,1,0:T(8,128)}, u32[]{:S(2)}) %copy-start.3) | copy-done | bytes 393240
  4.6 0.9 %copy-done.4 = f32[32,8,128]{2,1,0:T(8,128)S(1)} copy-done((f32[32,8,128]{2,1,0:T(8,128)S(1)}, f32[32,8,128]{2,1,0:T(8,128)}, u32[]{:S(2)}) %copy-start.4) | copy-done | bytes 131096
  5.5 0.9 %copy-done.7 = s32[32,8,128]{2,1,0:T(8,128)S(1)} copy-done((s32[32,8,128]{2,1,0:T(8,128)S(1)}, s32[32,8,128]{2,1,0:T(8,128)}, u32[]{:S(2)}) %copy-start.7) | copy-done | bytes 131096
  6.5 1.6 %collective-permute-start.1 = (f32[160,128]{1,0:T(8,128)S(1)}, f32[160,128]{1,0:T(8,128)S(1)}, u32[]{:S(2)}, u32[]{:S(2)}) collective-permute-start(f32[160,128]{1,0:T(8,128)S(1)} %get-tuple-element.23), channel_id=1, source_target_pairs={{0,1},{1,0},{2,3},{3,2},{4,5},{5,4},{6,7},{7,6},{8,16},{9,17},{10,... | collective-permute-start | bytes 245768 | tf_op jit(solution)/shard_map/ppermute | solution.py:69
  8.1 1.3 %shard_map.113 = (f32[3,272,128]{2,1,0:T(8,128)S(1)}, f32[3,272,128]{2,1,0:T(8,128)S(1)}, f32[272,128]{1,0:T(8,128)S(1)}, f32[3,256,128]{2,1,0:T(8,128)S(1)}) custom-call(f32[3,256,128]{2,1,0:T(8,128)S(1)} %bitcast.14, f32[3,256,128]{2,1,0:T(8,128)S(1)} %bitcast.17, f32[3,256,128]{2,1,0:T(8,128)S(1)} %bitcast.20, f32[3,256,128]{2,1,0:T(8,128)S(1)} %bitcast.23, ...), custom_call_target="tpu_custom_call" | custom-call | flops 3276800 | bytes 3072000 | tf_op jit(solution)/shard_map/pallas_call | solution.py:120
  9.4 1.7 %collective-permute-done.1.odd.refs_7_ = f32[160,128]{1,0:T(8,128)S(1)} collective-permute-done((f32[160,128]{1,0:T(8,128)S(1)}, f32[160,128]{1,0:T(8,128)S(1)}, u32[]{:S(2)}, u32[]{:S(2)}) %collective-permute-start.1) | collective-permute-done | bytes 81952 | tf_op jit(solution)/shard_map/ppermute | solution.py:69
  11.3 1.6 %collective-permute-start.2 = (f32[168,128]{1,0:T(8,128)S(1)}, f32[168,128]{1,0:T(8,128)S(1)}, u32[]{:S(2)}, u32[]{:S(2)}) collective-permute-start(f32[168,128]{1,0:T(8,128)S(1)} %get-tuple-element.32), channel_id=1, source_target_pairs={{0,1},{1,0},{2,3},{3,2},{4,5},{5,4},{6,7},{7,6},{8,9},{9,8},{10,11... | collective-permute-start | bytes 258056 | tf_op jit(solution)/shard_map/ppermute | solution.py:69
  12.8 3.9 %collective-permute-done.2.even = f32[168,128]{1,0:T(8,128)S(1)} collective-permute-done((f32[168,128]{1,0:T(8,128)S(1)}, f32[168,128]{1,0:T(8,128)S(1)}, u32[]{:S(2)}, u32[]{:S(2)}) %collective-permute-start.2) | collective-permute-done | bytes 86048 | tf_op jit(solution)/shard_map/ppermute | solution.py:69
  16.8 1.4 %collective-permute-done.3.odd = f32[168,128]{1,0:T(8,128)S(1)} collective-permute-done((f32[168,128]{1,0:T(8,128)S(1)}, f32[168,128]{1,0:T(8,128)S(1)}, u32[]{:S(2)}, u32[]{:S(2)}) %collective-permute-start.3) | collective-permute-done | bytes 86048 | tf_op jit(solution)/shard_map/ppermute | solution.py:69
  18.2 1.7 %shard_map.115 = (f32[3,256,128]{2,1,0:T(8,128)S(1)}, f32[3,256,128]{2,1,0:T(8,128)S(1)}, f32[256,128]{1,0:T(8,128)S(1)}, f32[24,128]{1,0:T(8,128)S(1)}) custom-call(f32[3,272,128]{2,1,0:T(8,128)S(1)} %get-tuple-element.27.h, f32[3,272,128]{2,1,0:T(8,128)S(1)} %get-tuple-element.28.e, f32[272,128]{1,0:T(8,128)S(1)} %get-tuple-element.29.c_ref, ...), custom_call_target="tpu_custom_call" | custom-call | tf_op jit(solution)/shard_map/pallas_call | solution.py:684
  20.0 1.0 %collective-permute-start.5 = (f32[24,128]{1,0:T(8,128)S(1)}, f32[24,128]{1,0:T(8,128)S(1)}, u32[]{:S(2)}, u32[]{:S(2)}) collective-permute-start(f32[24,128]{1,0:T(8,128)S(1)} %get-tuple-element.37), channel_id=1, source_target_pairs={{0,8},{1,9},{2,10},{3,11},{4,12},{5,13},{6,14},{7,15},{8,0},{9,1},... | collective-permute-start | bytes 36872 | tf_op jit(solution)/shard_map/ppermute | solution.py:69
  21.0 1.1 %collective-permute-start.6 = (f32[24,128]{1,0:T(8,128)S(1)}, f32[24,128]{1,0:T(8,128)S(1)}, u32[]{:S(2)}, u32[]{:S(2)}) collective-permute-start(f32[24,128]{1,0:T(8,128)S(1)} %get-tuple-element.37), channel_id=1, source_target_pairs={{0,16},{1,17},{2,18},{3,19},{4,20},{5,21},{6,22},{7,23},{8,24},{9,... | collective-permute-start | bytes 36872 | tf_op jit(solution)/shard_map/ppermute | solution.py:69
  22.2 2.9 %collective-permute-done.6.refs_3_ = f32[24,128]{1,0:T(8,128)S(1)} collective-permute-done((f32[24,128]{1,0:T(8,128)S(1)}, f32[24,128]{1,0:T(8,128)S(1)}, u32[]{:S(2)}, u32[]{:S(2)}) %collective-permute-start.6) | collective-permute-done | bytes 12320 | tf_op jit(solution)/shard_map/ppermute | solution.py:69
  25.6 1.1 %collective-permute-start.7 = (f32[120,128]{1,0:T(8,128)S(1)}, f32[120,128]{1,0:T(8,128)S(1)}, u32[]{:S(2)}, u32[]{:S(2)}) collective-permute-start(f32[120,128]{1,0:T(8,128)S(1)} %get-tuple-element.39), channel_id=1, source_target_pairs={{0,1},{1,0},{2,3},{3,2},{4,5},{5,4},{6,7},{7,6},{8,9},{9,8},{10,11... | collective-permute-start | bytes 184328 | tf_op jit(solution)/shard_map/ppermute | solution.py:69
  26.9 0.8 %shard_map.117.inverse = f32[256,128]{1,0:T(8,128)S(1)} custom-call(f32[256,128]{1,0:T(8,128)S(1)} %broadcast_in_dim.16.radius), custom_call_target="tpu_custom_call" | custom-call | flops 3276800 | bytes 262144 | tf_op jit(solution)/shard_map/pallas_call | solution.py:120
  27.7 0.7 %copy.19 = f32[3,32,8,128]{3,2,1,0:T(8,128)} copy(f32[3,32,8,128]{3,2,1,0:T(8,128)S(1)} %bitcast.12) | data formatting | bytes 786432
  28.5 0.7 %copy.20 = f32[3,32,8,128]{3,2,1,0:T(8,128)} copy(f32[3,32,8,128]{3,2,1,0:T(8,128)S(1)} %bitcast.11) | data formatting | bytes 786432
  29.2 0.6 %collective-permute-done.7.even = f32[120,128]{1,0:T(8,128)S(1)} collective-permute-done((f32[120,128]{1,0:T(8,128)S(1)}, f32[120,128]{1,0:T(8,128)S(1)}, u32[]{:S(2)}, u32[]{:S(2)}) %collective-permute-start.7) | collective-permute-done | bytes 61472 | tf_op jit(solution)/shard_map/ppermute | solution.py:69
  29.9 1.9 %collective-permute-done.8.odd = f32[120,128]{1,0:T(8,128)S(1)} collective-permute-done((f32[120,128]{1,0:T(8,128)S(1)}, f32[120,128]{1,0:T(8,128)S(1)}, u32[]{:S(2)}, u32[]{:S(2)}) %collective-permute-start.8) | collective-permute-done | bytes 61472 | tf_op jit(solution)/shard_map/ppermute | solution.py:69
  31.8 0.5 %shard_map.118 = f32[256,128]{1,0:T(8,128)S(1)} custom-call(f32[304,128]{1,0:T(8,128)S(1)} %get-tuple-element.38.u, f32[120,128]{1,0:T(8,128)S(1)} %collective-permute-done.7.even, f32[120,128]{1,0:T(8,128)S(1)} %collective-permute-done.8.odd, f32[256,128]{1,0:T(8,128)S(1)} %broadcast_in_dim.16.radius, f32[256,128]{1,0:T(8,128)S(1)} %shard_map.117.inverse), custom_call_target="tpu_custom_call" | custom-call | tf_op jit(solution)/shard_map/pallas_call | solution.py:684
  32.3 0.7 %copy.21 = f32[32,8,128]{2,1,0:T(8,128)} copy(f32[32,8,128]{2,1,0:T(8,128)S(1)} %bitcast.10) | data formatting | bytes 262144
  (31 shorter events, 1.2 us)
Async XLA Ops:
  0.6 1.0 %copy-start = (f32[3,32,8,128]{3,2,1,0:T(8,128)S(1)}, f32[3,32,8,128]{3,2,1,0:T(8,128)}, u32[]{:S(2)}) copy-start(f32[3,32,8,128]{3,2,1,0:T(8,128)} %param.9) | copy-start | bytes 1179652
  1.6 1.0 %copy-start.1 = (f32[3,32,8,128]{3,2,1,0:T(8,128)S(1)}, f32[3,32,8,128]{3,2,1,0:T(8,128)}, u32[]{:S(2)}) copy-start(f32[3,32,8,128]{3,2,1,0:T(8,128)} %param.10) | copy-start | bytes 1179652
  2.6 1.0 %copy-start.2 = (f32[3,32,8,128]{3,2,1,0:T(8,128)S(1)}, f32[3,32,8,128]{3,2,1,0:T(8,128)}, u32[]{:S(2)}) copy-start(f32[3,32,8,128]{3,2,1,0:T(8,128)} %param.11) | copy-start | bytes 1179652
  3.6 1.0 %copy-start.3 = (f32[3,32,8,128]{3,2,1,0:T(8,128)S(1)}, f32[3,32,8,128]{3,2,1,0:T(8,128)}, u32[]{:S(2)}) copy-start(f32[3,32,8,128]{3,2,1,0:T(8,128)} %param.12) | copy-start | bytes 1179652
  4.6 0.9 %copy-start.4 = (f32[32,8,128]{2,1,0:T(8,128)S(1)}, f32[32,8,128]{2,1,0:T(8,128)}, u32[]{:S(2)}) copy-start(f32[32,8,128]{2,1,0:T(8,128)} %param.13) | copy-start | bytes 393220
  5.5 0.9 %copy-start.7 = (s32[32,8,128]{2,1,0:T(8,128)S(1)}, s32[32,8,128]{2,1,0:T(8,128)}, u32[]{:S(2)}) copy-start(s32[32,8,128]{2,1,0:T(8,128)} %param.15) | copy-start | bytes 393220
  6.5 2.9 %collective-permute-start = (f32[160,128]{1,0:T(8,128)S(1)}, f32[160,128]{1,0:T(8,128)S(1)}, u32[]{:S(2)}, u32[]{:S(2)}) collective-permute-start(f32[160,128]{1,0:T(8,128)S(1)} %get-tuple-element.22), channel_id=1, source_target_pairs={{0,8},{1,9},{2,10},{3,11},{4,12},{5,13},{6,14},{7,15},{8,0},{9,1},... | collective-permute-start | bytes 245768 | tf_op jit(solution)/shard_map/ppermute | solution.py:69
  6.5 4.5 %collective-permute-start.1 = (f32[160,128]{1,0:T(8,128)S(1)}, f32[160,128]{1,0:T(8,128)S(1)}, u32[]{:S(2)}, u32[]{:S(2)}) collective-permute-start(f32[160,128]{1,0:T(8,128)S(1)} %get-tuple-element.23), channel_id=1, source_target_pairs={{0,1},{1,0},{2,3},{3,2},{4,5},{5,4},{6,7},{7,6},{8,16},{9,17},{10,... | collective-permute-start | bytes 245768 | tf_op jit(solution)/shard_map/ppermute | solution.py:69
  11.0 7.2 %copy-start.5 = (f32[32,8,128]{2,1,0:T(8,128)S(1)}, f32[32,8,128]{2,1,0:T(8,128)}, u32[]{:S(2)}) copy-start(f32[32,8,128]{2,1,0:T(8,128)} %param.13) | copy-start | bytes 393220
  11.0 7.2 %copy-start.6 = (f32[2,3,32,8,128]{4,3,2,1,0:T(8,128)S(1)}, f32[2,3,32,8,128]{4,3,2,1,0:T(8,128)}, u32[]{:S(2)}) copy-start(f32[2,3,32,8,128]{4,3,2,1,0:T(8,128)} %param.14) | copy-start | bytes 2359300
  11.3 5.5 %collective-permute-start.2 = (f32[168,128]{1,0:T(8,128)S(1)}, f32[168,128]{1,0:T(8,128)S(1)}, u32[]{:S(2)}, u32[]{:S(2)}) collective-permute-start(f32[168,128]{1,0:T(8,128)S(1)} %get-tuple-element.32), channel_id=1, source_target_pairs={{0,1},{1,0},{2,3},{3,2},{4,5},{5,4},{6,7},{7,6},{8,9},{9,8},{10,11... | collective-permute-start | bytes 258056 | tf_op jit(solution)/shard_map/ppermute | solution.py:69
  12.8 5.4 %collective-permute-start.3 = (f32[168,128]{1,0:T(8,128)S(1)}, f32[168,128]{1,0:T(8,128)S(1)}, u32[]{:S(2)}, u32[]{:S(2)}) collective-permute-start(f32[168,128]{1,0:T(8,128)S(1)} %get-tuple-element.33), channel_id=1, source_target_pairs={{0,8},{1,2},{2,1},{3,4},{4,3},{5,6},{6,5},{7,15},{8,0},{9,10},{10,... | collective-permute-start | bytes 258056 | tf_op jit(solution)/shard_map/ppermute | solution.py:69
  18.2 7.3 %copy-start.8 = (s32[32,8,128]{2,1,0:T(8,128)S(1)}, s32[32,8,128]{2,1,0:T(8,128)}, u32[]{:S(2)}) copy-start(s32[32,8,128]{2,1,0:T(8,128)} %param.15) | copy-start | bytes 393220
  19.9 5.5 %copy-start.10 = (s32[8]{0:T(128)S(1)}, s32[8]{0:T(128)}, u32[]{:S(2)}) copy-start(s32[8]{0:T(128)} %param.16) | copy-start | bytes 100
  19.9 5.5 %collective-permute-start.4 = (f32[256,128]{1,0:T(8,128)S(1)}, f32[256,128]{1,0:T(8,128)S(1)}, u32[]{:S(2)}, u32[]{:S(2)}) collective-permute-start(f32[256,128]{1,0:T(8,128)S(1)} %get-tuple-element.36.refs_0_), channel_id=1, source_target_pairs={{0,24},{1,25},{2,26},{3,27},{4,28},{5,29},{6,30},{7,31},{8,16},{9,... | collective-permute-start | bytes 393224 | tf_op jit(solution)/shard_map/ppermute | solution.py:69
  20.0 2.1 %collective-permute-start.5 = (f32[24,128]{1,0:T(8,128)S(1)}, f32[24,128]{1,0:T(8,128)S(1)}, u32[]{:S(2)}, u32[]{:S(2)}) collective-permute-start(f32[24,128]{1,0:T(8,128)S(1)} %get-tuple-element.37), channel_id=1, source_target_pairs={{0,8},{1,9},{2,10},{3,11},{4,12},{5,13},{6,14},{7,15},{8,0},{9,1},... | collective-permute-start | bytes 36872 | tf_op jit(solution)/shard_map/ppermute | solution.py:69
  21.0 4.0 %collective-permute-start.6 = (f32[24,128]{1,0:T(8,128)S(1)}, f32[24,128]{1,0:T(8,128)S(1)}, u32[]{:S(2)}, u32[]{:S(2)}) collective-permute-start(f32[24,128]{1,0:T(8,128)S(1)} %get-tuple-element.37), channel_id=1, source_target_pairs={{0,16},{1,17},{2,18},{3,19},{4,20},{5,21},{6,22},{7,23},{8,24},{9,... | collective-permute-start | bytes 36872 | tf_op jit(solution)/shard_map/ppermute | solution.py:69
  25.5 1.2 %copy-start.9 = (s32[32,8]{0,1:T(8,128)S(1)}, s32[32,8]{0,1:T(8,128)}, u32[]{:S(2)}) copy-start(s32[32,8]{0,1:T(8,128)} %param.17) | copy-start | bytes 3076
  25.6 4.3 %collective-permute-start.7 = (f32[120,128]{1,0:T(8,128)S(1)}, f32[120,128]{1,0:T(8,128)S(1)}, u32[]{:S(2)}, u32[]{:S(2)}) collective-permute-start(f32[120,128]{1,0:T(8,128)S(1)} %get-tuple-element.39), channel_id=1, source_target_pairs={{0,1},{1,0},{2,3},{3,2},{4,5},{5,4},{6,7},{7,6},{8,9},{9,8},{10,11... | collective-permute-start | bytes 184328 | tf_op jit(solution)/shard_map/ppermute | solution.py:69
  26.7 5.1 %collective-permute-start.8 = (f32[120,128]{1,0:T(8,128)S(1)}, f32[120,128]{1,0:T(8,128)S(1)}, u32[]{:S(2)}, u32[]{:S(2)}) collective-permute-start(f32[120,128]{1,0:T(8,128)S(1)} %get-tuple-element.40), channel_id=1, source_target_pairs={{0,8},{1,2},{2,1},{3,4},{4,3},{5,6},{6,5},{7,15},{8,0},{9,10},{10,... | collective-permute-start | bytes 184328 | tf_op jit(solution)/shard_map/ppermute | solution.py:69

commit v2 on v1

--- a/solution.py
+++ b/solution.py
@@ -128,28 +128,44 @@
     )(*args)
 
 
-def pack_x(n, r, e, h, p, q, d, m, even_out, odd_out):
+def pack_x(n, r, e, h, p, q, d, m, even_out, odd_out, e_at, h_at, p_at, q_at, d_at, m_at, sems):
+    copies = []
+    for end in range(2):
+        for k, (ref, held, planes) in enumerate(
+            ((e, e_at, 2), (h, h_at, 2), (p, p_at, 1), (q, q_at, 1), (d, d_at, WIDTH), (m, m_at, WIDTH))
+        ):
+            rows = pl.ds((n - planes) * r if end else 0, planes * r)
+            src = ref.at[:, rows, :] if len(ref.shape) == 3 else ref.at[rows, :]
+            copies.append(pltpu.make_async_copy(src, held.at[end], sems.at[end, k]))
+    for copy in copies:
+        copy.start()
+    for copy in copies:
+        copy.wait()
     odd = odd_x()
-    for out, low in ((even_out, odd), (odd_out, jnp.logical_not(odd))):
-        near = jnp.where(low, 0, n - 1)
-        step = jnp.where(low, 1, -1)
-        at = [pl.ds(pl.multiple_of((near + k * step) * r, r), r) for k in range(WIDTH)]
-
-        def put(slot, v):
-            out[slot * r : (slot + 1) * r, :] = v
-
-        for c in range(3):
-            put(c, e[c, at[0], :])
-            put(3 + c, h[c, at[0], :])
-            put(6 + c, DAMPING * q[c, at[0], :] - OMEGA_SQUARED * p[c, at[0], :])
-            put(10 + c, e[c, at[1], :])
-        put(9, d[at[0], :])
-        put(13, h[1, at[1], :])
-        put(14, h[2, at[1], :])
-        put(15, d[at[1], :])
-        put(16, d[at[2], :])
-        for k in range(WIDTH):
-            put(17 + k, m[at[k], :].astype(jnp.float32))
+
+    def take(ref, planes, k, c=None):
+        low, high = slice(k * r, (k + 1) * r), slice((planes - 1 - k) * r, (planes - k) * r)
+        if c is None:
+            return ref[0, low, :], ref[1, high, :]
+        return ref[0, c, low, :], ref[1, c, high, :]
+
+    def put(slot, pair):
+        at = slice(slot * r, (slot + 1) * r)
+        even_out[at, :] = jnp.where(odd, pair[0], pair[1])
+        odd_out[at, :] = jnp.where(odd, pair[1], pair[0])
+
+    for c in range(3):
+        put(c, take(e_at, 2, 0, c))
+        put(3 + c, take(h_at, 2, 0, c))
+        put(6 + c, [DAMPING * b - OMEGA_SQUARED * a for a, b in zip(take(p_at, 1, 0, c), take(q_at, 1, 0, c))])
+        put(10 + c, take(e_at, 2, 1, c))
+    put(9, take(d_at, WIDTH, 0))
+    put(13, take(h_at, 2, 1, 1))
+    put(14, take(h_at, 2, 1, 2))
+    put(15, take(d_at, WIDTH, 1))
+    put(16, take(d_at, WIDTH, 2))
+    for k in range(WIDTH):
+        put(17 + k, [v.astype(jnp.float32) for v in take(m_at, WIDTH, k)])
 
 
 def new_h(h, e, e_next, edge_x=0.0, edge_z=0.0):
@@ -622,12 +638,26 @@
     face_y = (5 * n + EXTRA, depth)
     lines = n + 2 * BASE
 
-    pack = functools.partial(pack_x, n, r)
-    even, odd = call(pack, [face_x] * 2, [e, h, p, q, d, m])
+    f32 = jnp.float32
+    even, odd = pl.pallas_call(
+        functools.partial(pack_x, n, r),
+        out_shape=(VMEM(face_x, f32), VMEM(face_x, f32)),
+        in_specs=[pl.BlockSpec(memory_space=pl.ANY)] * 6,
+        out_specs=(pl.BlockSpec(memory_space=VMEM), pl.BlockSpec(memory_space=VMEM)),
+        scratch_shapes=[
+            VMEM((2, 3, 2 * r, depth), f32),
+            VMEM((2, 3, 2 * r, depth), f32),
+            VMEM((2, 3, r, depth), f32),
+            VMEM((2, 3, r, depth), f32),
+            VMEM((2, WIDTH * r, depth), f32),
+            VMEM((2, WIDTH * r, depth), jnp.int32),
+            pltpu.SemaphoreType.DMA((2, 6)),
+        ],
+    )(e, h, p, q, d, m)
+    even = send(even, x_even)
     odd = send(odd, x_odd)
-    even = send(even, x_even)
-
-    inner = functools.partial(step_inner, n, r, 4)
+
+    inner = functools.partial(step_inner, n, r, 16)
     h1, e1, c1, t1 = call(inner, [(3, more, depth)] * 2 + [(more, depth), (3, size, depth)], [e, h, p, q, d], flops=100 * size * depth)
     ends = functools.partial(step_edges, n, r)
     h1, e1, c1, rows, even_y, odd_y_ = call(
@@ -643,12 +673,12 @@
     order = jnp.broadcast_to(partner_rows[:, None], (r, depth))
     (inverse,) = call(functools.partial(cover, n, r), [(size, depth)], [radius], flops=100 * size * depth)
 
-    final = functools.partial(step_last, n, r, 4)
+    final = functools.partial(step_last, n, r, 16)
     args = [h1, e1, c1, t1, d, rows, even_y, odd_y_, f]
     e2, h2, g, edge = step_call(final, n, r, depth, args)
+    edge_e = send(edge, x_even)
+    edge_m = send(edge, mirror_even)
     other = send(g, mirror)
-    edge_m = send(edge, mirror_even)
-    edge_e = send(edge, x_even)
     generic = lax.axis_size("gx") != 4
     extra = []
     if generic:
@@ -666,7 +696,7 @@
     odd_u = send(odd_u, y_odd)
     even_u = send(even_u, y_even)
     (out,) = scratch_call(
-        functools.partial(smooth, n, r, 4),
+        functools.partial(smooth, n, r, 16),
         [(size, depth)],
         [u, even_u, odd_u, radius, inverse],
         [VMEM((wide * r, depth), jnp.float32), VMEM((WIDTH, full * r, depth), jnp.float32)],

time: 33.3 us -> 27.5 us (0.83)
  local copies, waits for them, and re-layouts: 8.28 us -> 2.52 us
  waiting for transfers between devices: 12.9 us -> 13.7 us
  Pallas kernels: 4.58 us -> 3.8 us
    unnamed x25 -> x21, local copies, waits for them, and re-layouts: 7.95 us -> 2.19 us
    pallas_call x0 -> x1, Pallas kernels: none -> 1.06 us  [local(): pl.pallas_call(functools.partial(pack_x, n, r), out_shape=(VMEM(face_x, f...]
    pallas_call x3, Pallas kernels: 2.31 us -> 1.31 us  [scratch_call(): pl.pallas_call(kernel, out_shape=tuple((VMEM(s, jnp.float32) for s in out...]
    pallas_call x4 -> x3, Pallas kernels: 2.27 us -> 1.43 us  [call(): pl.pallas_call(kernel, out_shape=shapes, in_specs=[spec] * len(args), out...]
    ppermute x9, waiting for transfers between devices: 12.9 us -> 13.7 us  [send(): return lax.ppermute(block, AXES, route)]
  transfers between devices with their start and end apart: 9 -> 9, of which waited for: 7 -> 7; matrix products, arithmetic and copies ran while one was open for 5% -> 6% of each run, Pallas kernels for 6% -> 4%
where the time goes in v2:
time: 27.5 us; the launch traced here: 27.3 us
  waiting for transfers between devices  13.7 us (50%)
  starting transfers between devices  6.5 us (24%)
  Pallas kernels  3.8 us (14%)
  local copies, waits for them, and re-layouts  2.52 us (9%)
  between operations  0.78 us (3%)
    ppermute x9, waiting for transfers between devices, send(): return lax.ppermute(block, AXES, route)  13.7 us
    ppermute x9, starting transfers between devices, send(): return lax.ppermute(block, AXES, route)  6.5 us
    unnamed x21, local copies, waits for them, and re-layouts  2.19 us
    pallas_call x3, Pallas kernels, call(): pl.pallas_call(kernel, out_shape=shapes, in_specs=[spec] * len(args), out...  1.43 us
    pallas_call x3, Pallas kernels, scratch_call(): pl.pallas_call(kernel, out_shape=tuple((VMEM(s, jnp.float32) for s in out...  1.31 us
    pallas_call x1, Pallas kernels, local(): pl.pallas_call(functools.partial(pack_x, n, r), out_shape=(VMEM(face_x, f...  1.06 us
  transfers between devices with their start and end apart: 9, of which 7 were waited for; matrix products, arithmetic and copies ran while one was open for 6% of the time, Pallas kernels for 4%

profile of v2, /device:TPU:8, one launch (start us, length us, event | category | flops | bytes accessed | tf_op | source)
XLA Modules:
  0.0 27.3 jit_solution(2023851357826261426)
XLA Ops:
  0.7 1.1 %shard_map.112 = (f32[160,128]{1,0:T(8,128)S(1)}, f32[160,128]{1,0:T(8,128)S(1)}) custom-call(f32[3,256,128]{2,1,0:T(8,128)} %bitcast.13, f32[3,256,128]{2,1,0:T(8,128)} %bitcast.16, f32[3,256,128]{2,1,0:T(8,128)} %bitcast.19, f32[3,256,128]{2,1,0:T(8,128)} %bitcast.22, f32[256,128]{1,0:T(8,128)} %bitcast.25, s32[256,128]{1,0:T(8,128)} %bitcast.31), custom_call_target="tpu_custom_call" | custom-call | tf_op jit(solution)/shard_map/pallas_call | solution.py:642
  1.8 1.6 %collective-permute-start.1 = (f32[160,128]{1,0:T(8,128)S(1)}, f32[160,128]{1,0:T(8,128)S(1)}, u32[]{:S(2)}, u32[]{:S(2)}) collective-permute-start(f32[160,128]{1,0:T(8,128)S(1)} %get-tuple-element.23), channel_id=1, source_target_pairs={{0,1},{1,0},{2,3},{3,2},{4,5},{5,4},{6,7},{7,6},{8,16},{9,17},{10,... | collective-permute-start | bytes 245768 | tf_op jit(solution)/shard_map/ppermute | solution.py:69
  3.4 0.4 %shard_map.113 = (f32[3,272,128]{2,1,0:T(8,128)S(1)}, f32[3,272,128]{2,1,0:T(8,128)S(1)}, f32[272,128]{1,0:T(8,128)S(1)}, f32[3,256,128]{2,1,0:T(8,128)S(1)}) custom-call(f32[3,256,128]{2,1,0:T(8,128)S(1)} %bitcast.14, f32[3,256,128]{2,1,0:T(8,128)S(1)} %bitcast.17, f32[3,256,128]{2,1,0:T(8,128)S(1)} %bitcast.20, f32[3,256,128]{2,1,0:T(8,128)S(1)} %bitcast.23, ...), custom_call_target="tpu_custom_call" | custom-call | flops 3276800 | bytes 3072000 | tf_op jit(solution)/shard_map/pallas_call | solution.py:120
  3.9 2.4 %collective-permute-done.1.odd.refs_7_ = f32[160,128]{1,0:T(8,128)S(1)} collective-permute-done((f32[160,128]{1,0:T(8,128)S(1)}, f32[160,128]{1,0:T(8,128)S(1)}, u32[]{:S(2)}, u32[]{:S(2)}) %collective-permute-start.1) | collective-permute-done | bytes 81952 | tf_op jit(solution)/shard_map/ppermute | solution.py:69
  6.3 0.2 shard_map.114
  6.6 1.6 %collective-permute-start.2 = (f32[168,128]{1,0:T(8,128)S(1)}, f32[168,128]{1,0:T(8,128)S(1)}, u32[]{:S(2)}, u32[]{:S(2)}) collective-permute-start(f32[168,128]{1,0:T(8,128)S(1)} %get-tuple-element.32), channel_id=1, source_target_pairs={{0,1},{1,0},{2,3},{3,2},{4,5},{5,4},{6,7},{7,6},{8,9},{9,8},{10,11... | collective-permute-start | bytes 258056 | tf_op jit(solution)/shard_map/ppermute | solution.py:69
  8.1 3.9 %collective-permute-done.2.even = f32[168,128]{1,0:T(8,128)S(1)} collective-permute-done((f32[168,128]{1,0:T(8,128)S(1)}, f32[168,128]{1,0:T(8,128)S(1)}, u32[]{:S(2)}, u32[]{:S(2)}) %collective-permute-start.2) | collective-permute-done | bytes 86048 | tf_op jit(solution)/shard_map/ppermute | solution.py:69
  12.1 1.4 %collective-permute-done.3.odd = f32[168,128]{1,0:T(8,128)S(1)} collective-permute-done((f32[168,128]{1,0:T(8,128)S(1)}, f32[168,128]{1,0:T(8,128)S(1)}, u32[]{:S(2)}, u32[]{:S(2)}) %collective-permute-start.3) | collective-permute-done | bytes 86048 | tf_op jit(solution)/shard_map/ppermute | solution.py:69
  13.5 0.8 %shard_map.115 = (f32[3,256,128]{2,1,0:T(8,128)S(1)}, f32[3,256,128]{2,1,0:T(8,128)S(1)}, f32[256,128]{1,0:T(8,128)S(1)}, f32[24,128]{1,0:T(8,128)S(1)}) custom-call(f32[3,272,128]{2,1,0:T(8,128)S(1)} %get-tuple-element.27.h, f32[3,272,128]{2,1,0:T(8,128)S(1)} %get-tuple-element.28.e, f32[272,128]{1,0:T(8,128)S(1)} %get-tuple-element.29.c_ref, ...), custom_call_target="tpu_custom_call" | custom-call | tf_op jit(solution)/shard_map/pallas_call | solution.py:714
  14.4 1.0 %collective-permute-start.5 = (f32[24,128]{1,0:T(8,128)S(1)}, f32[24,128]{1,0:T(8,128)S(1)}, u32[]{:S(2)}, u32[]{:S(2)}) collective-permute-start(f32[24,128]{1,0:T(8,128)S(1)} %get-tuple-element.37), channel_id=1, source_target_pairs={{0,8},{1,9},{2,10},{3,11},{4,12},{5,13},{6,14},{7,15},{8,0},{9,1},... | collective-permute-start | bytes 36872 | tf_op jit(solution)/shard_map/ppermute | solution.py:69
  15.5 1.1 %collective-permute-start.6 = (f32[24,128]{1,0:T(8,128)S(1)}, f32[24,128]{1,0:T(8,128)S(1)}, u32[]{:S(2)}, u32[]{:S(2)}) collective-permute-start(f32[24,128]{1,0:T(8,128)S(1)} %get-tuple-element.37), channel_id=1, source_target_pairs={{0,16},{1,17},{2,18},{3,19},{4,20},{5,21},{6,22},{7,23},{8,24},{9,... | collective-permute-start | bytes 36872 | tf_op jit(solution)/shard_map/ppermute | solution.py:69
  16.6 2.9 %collective-permute-done.6.refs_3_ = f32[24,128]{1,0:T(8,128)S(1)} collective-permute-done((f32[24,128]{1,0:T(8,128)S(1)}, f32[24,128]{1,0:T(8,128)S(1)}, u32[]{:S(2)}, u32[]{:S(2)}) %collective-permute-start.6) | collective-permute-done | bytes 12320 | tf_op jit(solution)/shard_map/ppermute | solution.py:69
  19.5 0.3 %collective-permute-done.4.refs_1_ = f32[256,128]{1,0:T(8,128)S(1)} collective-permute-done((f32[256,128]{1,0:T(8,128)S(1)}, f32[256,128]{1,0:T(8,128)S(1)}, u32[]{:S(2)}, u32[]{:S(2)}) %collective-permute-start.4) | collective-permute-done | bytes 131104 | tf_op jit(solution)/shard_map/ppermute | solution.py:69
  19.9 0.1 shard_map.116
  20.0 1.1 %collective-permute-start.7 = (f32[120,128]{1,0:T(8,128)S(1)}, f32[120,128]{1,0:T(8,128)S(1)}, u32[]{:S(2)}, u32[]{:S(2)}) collective-permute-start(f32[120,128]{1,0:T(8,128)S(1)} %get-tuple-element.39), channel_id=1, source_target_pairs={{0,1},{1,0},{2,3},{3,2},{4,5},{5,4},{6,7},{7,6},{8,9},{9,8},{10,11... | collective-permute-start | bytes 184328 | tf_op jit(solution)/shard_map/ppermute | solution.py:69
  21.2 0.1 broadcast_in_dim.7
  21.3 0.1 broadcast_in_dim.16.radius
  21.4 0.8 %shard_map.117.inverse = f32[256,128]{1,0:T(8,128)S(1)} custom-call(f32[256,128]{1,0:T(8,128)S(1)} %broadcast_in_dim.16.radius), custom_call_target="tpu_custom_call" | custom-call | flops 3276800 | bytes 262144 | tf_op jit(solution)/shard_map/pallas_call | solution.py:120
  22.1 0.7 %copy.19 = f32[3,32,8,128]{3,2,1,0:T(8,128)} copy(f32[3,32,8,128]{3,2,1,0:T(8,128)S(1)} %bitcast.12) | data formatting | bytes 786432
  22.9 0.7 %copy.20 = f32[3,32,8,128]{3,2,1,0:T(8,128)} copy(f32[3,32,8,128]{3,2,1,0:T(8,128)S(1)} %bitcast.11) | data formatting | bytes 786432
  23.6 0.6 %collective-permute-done.7.even = f32[120,128]{1,0:T(8,128)S(1)} collective-permute-done((f32[120,128]{1,0:T(8,128)S(1)}, f32[120,128]{1,0:T(8,128)S(1)}, u32[]{:S(2)}, u32[]{:S(2)}) %collective-permute-start.7) | collective-permute-done | bytes 61472 | tf_op jit(solution)/shard_map/ppermute | solution.py:69
  24.3 1.9 %collective-permute-done.8.odd = f32[120,128]{1,0:T(8,128)S(1)} collective-permute-done((f32[120,128]{1,0:T(8,128)S(1)}, f32[120,128]{1,0:T(8,128)S(1)}, u32[]{:S(2)}, u32[]{:S(2)}) %collective-permute-start.8) | collective-permute-done | bytes 61472 | tf_op jit(solution)/shard_map/ppermute | solution.py:69
  26.2 0.4 %shard_map.118 = f32[256,128]{1,0:T(8,128)S(1)} custom-call(f32[304,128]{1,0:T(8,128)S(1)} %get-tuple-element.38.u, f32[120,128]{1,0:T(8,128)S(1)} %collective-permute-done.7.even, f32[120,128]{1,0:T(8,128)S(1)} %collective-permute-done.8.odd, f32[256,128]{1,0:T(8,128)S(1)} %broadcast_in_dim.16.radius, f32[256,128]{1,0:T(8,128)S(1)} %shard_map.117.inverse), custom_call_target="tpu_custom_call" | custom-call | tf_op jit(solution)/shard_map/pallas_call | solution.py:714
  26.6 0.7 %copy.21 = f32[32,8,128]{2,1,0:T(8,128)} copy(f32[32,8,128]{2,1,0:T(8,128)S(1)} %bitcast.10) | data formatting | bytes 262144
  (27 shorter events, 0.3 us)
Async XLA Ops:
  0.6 2.8 %copy-start = (f32[3,32,8,128]{3,2,1,0:T(8,128)S(1)}, f32[3,32,8,128]{3,2,1,0:T(8,128)}, u32[]{:S(2)}) copy-start(f32[3,32,8,128]{3,2,1,0:T(8,128)} %param.9) | copy-start | bytes 1179652
  0.6 2.8 %copy-start.1 = (f32[3,32,8,128]{3,2,1,0:T(8,128)S(1)}, f32[3,32,8,128]{3,2,1,0:T(8,128)}, u32[]{:S(2)}) copy-start(f32[3,32,8,128]{3,2,1,0:T(8,128)} %param.10) | copy-start | bytes 1179652
  0.7 2.8 %copy-start.2 = (f32[3,32,8,128]{3,2,1,0:T(8,128)S(1)}, f32[3,32,8,128]{3,2,1,0:T(8,128)}, u32[]{:S(2)}) copy-start(f32[3,32,8,128]{3,2,1,0:T(8,128)} %param.11) | copy-start | bytes 1179652
  0.7 2.8 %copy-start.3 = (f32[3,32,8,128]{3,2,1,0:T(8,128)S(1)}, f32[3,32,8,128]{3,2,1,0:T(8,128)}, u32[]{:S(2)}) copy-start(f32[3,32,8,128]{3,2,1,0:T(8,128)} %param.12) | copy-start | bytes 1179652
  0.7 2.8 %copy-start.4 = (f32[32,8,128]{2,1,0:T(8,128)S(1)}, f32[32,8,128]{2,1,0:T(8,128)}, u32[]{:S(2)}) copy-start(f32[32,8,128]{2,1,0:T(8,128)} %param.13) | copy-start | bytes 393220
  1.7 2.1 %collective-permute-start = (f32[160,128]{1,0:T(8,128)S(1)}, f32[160,128]{1,0:T(8,128)S(1)}, u32[]{:S(2)}, u32[]{:S(2)}) collective-permute-start(f32[160,128]{1,0:T(8,128)S(1)} %get-tuple-element.22), channel_id=1, source_target_pairs={{0,8},{1,9},{2,10},{3,11},{4,12},{5,13},{6,14},{7,15},{8,0},{9,1},... | collective-permute-start | bytes 245768 | tf_op jit(solution)/shard_map/ppermute | solution.py:69
  1.8 4.5 %collective-permute-start.1 = (f32[160,128]{1,0:T(8,128)S(1)}, f32[160,128]{1,0:T(8,128)S(1)}, u32[]{:S(2)}, u32[]{:S(2)}) collective-permute-start(f32[160,128]{1,0:T(8,128)S(1)} %get-tuple-element.23), channel_id=1, source_target_pairs={{0,1},{1,0},{2,3},{3,2},{4,5},{5,4},{6,7},{7,6},{8,16},{9,17},{10,... | collective-permute-start | bytes 245768 | tf_op jit(solution)/shard_map/ppermute | solution.py:69
  6.3 7.2 %copy-start.5 = (f32[2,3,32,8,128]{4,3,2,1,0:T(8,128)S(1)}, f32[2,3,32,8,128]{4,3,2,1,0:T(8,128)}, u32[]{:S(2)}) copy-start(f32[2,3,32,8,128]{4,3,2,1,0:T(8,128)} %param.14) | copy-start | bytes 2359300
  6.6 5.5 %collective-permute-start.2 = (f32[168,128]{1,0:T(8,128)S(1)}, f32[168,128]{1,0:T(8,128)S(1)}, u32[]{:S(2)}, u32[]{:S(2)}) collective-permute-start(f32[168,128]{1,0:T(8,128)S(1)} %get-tuple-element.32), channel_id=1, source_target_pairs={{0,1},{1,0},{2,3},{3,2},{4,5},{5,4},{6,7},{7,6},{8,9},{9,8},{10,11... | collective-permute-start | bytes 258056 | tf_op jit(solution)/shard_map/ppermute | solution.py:69
  8.1 5.4 %collective-permute-start.3 = (f32[168,128]{1,0:T(8,128)S(1)}, f32[168,128]{1,0:T(8,128)S(1)}, u32[]{:S(2)}, u32[]{:S(2)}) collective-permute-start(f32[168,128]{1,0:T(8,128)S(1)} %get-tuple-element.33), channel_id=1, source_target_pairs={{0,8},{1,2},{2,1},{3,4},{4,3},{5,6},{6,5},{7,15},{8,0},{9,10},{10,... | collective-permute-start | bytes 258056 | tf_op jit(solution)/shard_map/ppermute | solution.py:69
  13.5 6.4 %copy-start.6 = (s32[32,8,128]{2,1,0:T(8,128)S(1)}, s32[32,8,128]{2,1,0:T(8,128)}, u32[]{:S(2)}) copy-start(s32[32,8,128]{2,1,0:T(8,128)} %param.15) | copy-start | bytes 393220
  14.3 5.5 %copy-start.8 = (s32[8]{0:T(128)S(1)}, s32[8]{0:T(128)}, u32[]{:S(2)}) copy-start(s32[8]{0:T(128)} %param.16) | copy-start | bytes 100
  14.4 5.5 %collective-permute-start.4 = (f32[256,128]{1,0:T(8,128)S(1)}, f32[256,128]{1,0:T(8,128)S(1)}, u32[]{:S(2)}, u32[]{:S(2)}) collective-permute-start(f32[256,128]{1,0:T(8,128)S(1)} %get-tuple-element.36.refs_0_), channel_id=1, source_target_pairs={{0,24},{1,25},{2,26},{3,27},{4,28},{5,29},{6,30},{7,31},{8,16},{9,... | collective-permute-start | bytes 393224 | tf_op jit(solution)/shard_map/ppermute | solution.py:69
  14.4 2.1 %collective-permute-start.5 = (f32[24,128]{1,0:T(8,128)S(1)}, f32[24,128]{1,0:T(8,128)S(1)}, u32[]{:S(2)}, u32[]{:S(2)}) collective-permute-start(f32[24,128]{1,0:T(8,128)S(1)} %get-tuple-element.37), channel_id=1, source_target_pairs={{0,8},{1,9},{2,10},{3,11},{4,12},{5,13},{6,14},{7,15},{8,0},{9,1},... | collective-permute-start | bytes 36872 | tf_op jit(solution)/shard_map/ppermute | solution.py:69
  15.5 4.0 %collective-permute-start.6 = (f32[24,128]{1,0:T(8,128)S(1)}, f32[24,128]{1,0:T(8,128)S(1)}, u32[]{:S(2)}, u32[]{:S(2)}) collective-permute-start(f32[24,128]{1,0:T(8,128)S(1)} %get-tuple-element.37), channel_id=1, source_target_pairs={{0,16},{1,17},{2,18},{3,19},{4,20},{5,21},{6,22},{7,23},{8,24},{9,... | collective-permute-start | bytes 36872 | tf_op jit(solution)/shard_map/ppermute | solution.py:69
  19.9 1.2 %copy-start.7 = (s32[32,8]{0,1:T(8,128)S(1)}, s32[32,8]{0,1:T(8,128)}, u32[]{:S(2)}) copy-start(s32[32,8]{0,1:T(8,128)} %param.17) | copy-start | bytes 3076
  20.0 4.3 %collective-permute-start.7 = (f32[120,128]{1,0:T(8,128)S(1)}, f32[120,128]{1,0:T(8,128)S(1)}, u32[]{:S(2)}, u32[]{:S(2)}) collective-permute-start(f32[120,128]{1,0:T(8,128)S(1)} %get-tuple-element.39), channel_id=1, source_target_pairs={{0,1},{1,0},{2,3},{3,2},{4,5},{5,4},{6,7},{7,6},{8,9},{9,8},{10,11... | collective-permute-start | bytes 184328 | tf_op jit(solution)/shard_map/ppermute | solution.py:69
  21.1 5.1 %collective-permute-start.8 = (f32[120,128]{1,0:T(8,128)S(1)}, f32[120,128]{1,0:T(8,128)S(1)}, u32[]{:S(2)}, u32[]{:S(2)}) collective-permute-start(f32[120,128]{1,0:T(8,128)S(1)} %get-tuple-element.40), channel_id=1, source_target_pairs={{0,8},{1,2},{2,1},{3,4},{4,3},{5,6},{6,5},{7,15},{8,0},{9,10},{10,... | collective-permute-start | bytes 184328 | tf_op jit(solution)/shard_map/ppermute | solution.py:69

commit v3 on v2

--- a/solution.py
+++ b/solution.py
@@ -24,8 +24,17 @@
 WIDTH = RMAX - 1
 SLOTS = 20
 BASE = 8
-EXTRA = 8
+REACH = STEPS
 VMEM = pltpu.VMEM
+
+
+def late_rows(n):
+    up = ((0, -1), (0, n), (1, -1), (1, n - 1), (2, 0), (2, n - 1), (3, 0), (3, n - 2), (3, n - 1), (4, n))
+    down = ((0, -1), (0, n - 1), (1, 0), (1, n - 1), (2, -1), (3, -2), (3, -1), (3, n), (4, -1), (4, n))
+    return up, down
+
+
+LATE = 16
 
 
 def x_even(x, y, nx, ny):
@@ -112,20 +121,19 @@
     return jnp.where(flag, v, 0.0)
 
 
-def call(kernel, outs, args, aliases=None, flops=0):
-    args = [a if m is pltpu.SMEM else pltpu.with_memory_space_constraint(a, VMEM) for a, m in [(a, VMEM) for a in args]]
-    shapes = tuple(VMEM(s, jnp.float32) for s in outs)
+def call(kernel, outs, args, aliases=None, flops=0, scratch=()):
     spec = pl.BlockSpec(memory_space=VMEM)
     traffic = 4 * (sum(math.prod(s) for s in outs) + sum(math.prod(a.shape) for a in args))
     return pl.pallas_call(
         kernel,
-        out_shape=shapes,
+        out_shape=tuple(VMEM(s, jnp.float32) for s in outs),
         in_specs=[spec] * len(args),
         out_specs=tuple([spec] * len(outs)),
+        scratch_shapes=scratch,
         input_output_aliases=aliases or {},
         cost_estimate=pl.CostEstimate(flops=flops, bytes_accessed=traffic, transcendentals=0),
         compiler_params=pltpu.CompilerParams(vmem_limit_bytes=16 * 2**20),
-    )(*args)
+    )(*[pltpu.with_memory_space_constraint(a, VMEM) for a in args])
 
 
 def pack_x(n, r, e, h, p, q, d, m, even_out, odd_out, e_at, h_at, p_at, q_at, d_at, m_at, sems):
@@ -190,7 +198,7 @@
     return COURANT / (1.0 + (EPS_MATERIAL - 1.0) * d)
 
 
-def step_inner(n, r, block, e, h, p, q, d, h_out, e_out, c_out, t_out):
+def step_inner(n, r, block, e, h, p, q, d, h_out, e_out, c_out, t_out, even_y, odd_y_out):
     def plane(ref, x, c=None):
         at = pl.ds(pl.multiple_of(x * r, r), r)
         return ref[at, :] if c is None else ref[c, at, :]
@@ -224,7 +232,40 @@
         return last
 
     zero = jnp.zeros((r, e.shape[-1]), jnp.float32)
+    for c in range(3):
+        put(h_out, n + 1, zero, c)
+        put(e_out, n + 1, zero, c)
     lax.fori_loop(0, n // block, body, (zero, zero, zero))
+    flip_y = odd_y()
+    for k, (u, v) in enumerate(zip(*faces(n, r, n, 0, e, h_out, e_out, c_out))):
+        even_y[k * n : (k + 1) * n, :] = jnp.where(flip_y, v, u)
+        odd_y_out[k * n : (k + 1) * n, :] = jnp.where(flip_y, u, v)
+
+
+def faces(n, r, size, x, e, h_out, e_out, c_out):
+    def row(ref, y, first, c=None):
+        at = pl.ds((first + 1) * r + y, size, stride=r)
+        return ref[at, :] if c is None else ref[c, at, :]
+
+    last = r - 1
+    g_x, g_z = row(h_out, last, x, 0), row(h_out, last, x, 2)
+    a_x, a_y, a_z = row(e_out, last, x, 0), row(e_out, last, x, 1), row(e_out, last, x, 2)
+    a_y1 = row(e_out, last, x + 1, 1)
+    up = (
+        g_x,
+        g_z,
+        g_x + COURANT * a_z + COURANT * (ahead_z(a_y) - a_y),
+        g_z - COURANT * (a_y1 - a_y) - COURANT * a_x,
+        row(c_out, last, x),
+    )
+    down = (
+        row(e_out, 0, x, 0),
+        row(e_out, 0, x, 2),
+        row(c_out, 0, x),
+        e[0, pl.ds(x * r, size, stride=r), :],
+        e[2, pl.ds(x * r, size, stride=r), :],
+    )
+    return up, down
 
 
 def step_edges(n, r, e, h, p, q, d, even, odd, h_in, e_in, c_in, h_out, e_out, c_out, rows_out, even_y, odd_y_out):
@@ -283,63 +324,97 @@
         rows_out[k, BASE : BASE + n, :] = e[c, pl.ds(0, n, stride=r), :]
         rows_out[k, BASE + n : BASE + n + 1, :] = e_n[c][:1]
 
-    def row(ref, y, first, c=None):
-        start = (first + 1) * r + y
-        if c is None:
-            return ref[pl.ds(start, n, stride=r), :]
-        return ref[c, pl.ds(start, n, stride=r), :]
-
-    last = r - 1
-    g_x, g_z = row(h_out, last, 0, 0), row(h_out, last, 0, 2)
-    a_x, a_y, a_y1, a_z = (row(e_out, last, 0, 0), row(e_out, last, 0, 1), row(e_out, last, 1, 1), row(e_out, last, 0, 2))
-    up = [
-        g_x,
-        g_z,
-        g_x + COURANT * a_z + COURANT * (ahead_z(a_y) - a_y),
-        g_z - COURANT * (a_y1 - a_y) - COURANT * a_x,
-        row(c_out, last, 0),
-    ]
-    down = [row(e_out, 0, 0, 0), row(e_out, 0, 0, 2), row(c_out, 0, 0), rows_out[0, BASE : BASE + n, :], rows_out[1, BASE : BASE + n, :]]
+    def up(field, x):
+        def at_last(ref, c, x):
+            start = (x + 1) * r + r - 1
+            return ref[c, start : start + 1, :]
+
+        g_x, g_z = at_last(h_out, 0, x), at_last(h_out, 2, x)
+        if field == 0:
+            return g_x
+        if field == 1:
+            return g_z
+        if field == 4:
+            return c_out[(x + 2) * r - 1 : (x + 2) * r, :]
+        a_y = at_last(e_out, 1, x)
+        if field == 2:
+            return g_x + COURANT * at_last(e_out, 2, x) + COURANT * (ahead_z(a_y) - a_y)
+        return g_z - COURANT * (at_last(e_out, 1, x + 1) - a_y) - COURANT * at_last(e_out, 0, x)
+
+    def down(field, x):
+        start = (x + 1) * r
+        if field < 2:
+            return e_out[2 * field, start : start + 1, :]
+        if field == 2:
+            return c_out[start : start + 1, :]
+        return {-2: e_m2, -1: e_m1, n: e_n}[x][2 * (field - 3)][:1]
+
     flip_y = odd_y()
-    for k in range(5):
-        even_y[k * n : (k + 1) * n, :] = jnp.where(flip_y, down[k], up[k])
-        odd_y_out[k * n : (k + 1) * n, :] = jnp.where(flip_y, up[k], down[k])
-    up_more = [
-        h_m1[0][last:],
-        h_n[0][last:],
-        h_m1[2][last:],
-        c_out[(n + 1) * r + last : (n + 1) * r + last + 1, :],
-    ]
-    down_more = [
-        e_out[0, 0:1, :],
-        c_out[0:1, :],
-        e_m2[0][:1],
-        e_m1[0][:1],
-        e_m1[2][:1],
-        e_n[0][:1],
-        e_n[2][:1],
-    ]
-    zero = jnp.zeros_like(up_more[0])
-    for k in range(EXTRA):
-        u = up_more[k] if k < len(up_more) else zero
-        v = down_more[k] if k < len(down_more) else zero
-        even_y[5 * n + k : 5 * n + k + 1, :] = jnp.where(flip_y, v, u)
-        odd_y_out[5 * n + k : 5 * n + k + 1, :] = jnp.where(flip_y, u, v)
-
-
-def step_last(n, r, block, h, e, c_ref, t, d, rows, even, odd, f, e_out, h_out, g_out, edge_out, hs, es, fix, h_edge):
+    zero = jnp.zeros((1, e.shape[-1]), jnp.float32)
+    upward, downward = late_rows(n)
+    for k in range(LATE):
+        u = up(*upward[k]) if k < len(upward) else zero
+        v = down(*downward[k]) if k < len(downward) else zero
+        even_y[k : k + 1, :] = jnp.where(flip_y, v, u)
+        odd_y_out[k : k + 1, :] = jnp.where(flip_y, u, v)
+
+
+def step_mid(n, r, block, h, e, c_ref, t, d, f, out, g):
+    below, _, _, _ = edges()
+
+    def fields(ref, x):
+        at = pl.ds(pl.multiple_of((x + 1) * r, r), r)
+        return [ref[c, at, :] for c in range(3)]
+
+    def one(x, last_h):
+        now = fields(e, x)
+        mine = new_h(fields(h, x), now, fields(e, x + 1))
+        at = pl.ds(pl.multiple_of(x * r, r), r)
+        half = c_ref[pl.ds(pl.multiple_of((x + 1) * r, r), r), :]
+        dd = d[at, :]
+        curl = curl_h(mine, last_h)
+        total = None
+        for c in range(3):
+            rate = t[c, at, :] + (OMEGA_SQUARED * LORENTZ_STRENGTH) * dd * now[c]
+            after = now[c] + half * (curl[c] - 2.0 * rate)
+            part = now[c] * f[c, at, :] + after * f[3 + c, at, :]
+            total = part if total is None else total + part
+        g[at, :] = total
+        return mine
+
+    def body(i, last_h):
+        for k in range(block):
+            last_h = one(i * block + k, last_h)
+        return last_h
+
+    start = tuple(keep(below, v) for v in new_h(fields(h, -1), fields(e, -1), fields(e, 0)))
+    lax.fori_loop(0, n // block, body, start)
+    for j in range(REACH, r - REACH):
+        out[(j - REACH) * n : (j - REACH + 1) * n, :] = g[pl.ds(j, n, stride=r), :]
+
+
+def step_last(
+    n, r, block, h, e, c_ref, t, d, rows, even, odd, even_late, odd_late, f, e_out, h_out, g_out, rim_out, edge_out, face, fix
+):
     flip = odd_y()
     below, above, low, high = edges()
     hxm, hzm, dx, dz, ry, exp_, ezp, hxm2, hzm2, wm = range(10)
     last = r - 1
-
-    def up(k, size=None):
-        start, size = (k * n, n) if size is None else (5 * n + k, 1)
-        return keep(low, jnp.where(flip, even[start : start + size, :], odd[start : start + size, :]))
-
-    def down(k, size=None):
-        start, size = (k * n, n) if size is None else (5 * n + k, 1)
-        return keep(high, jnp.where(flip, odd[start : start + size, :], even[start : start + size, :]))
+    upward, downward = late_rows(n)
+    for k in range(5):
+        at = slice(k * n, (k + 1) * n)
+        face[0, k, BASE : BASE + n, :] = jnp.where(flip, even[at, :], odd[at, :])
+        face[1, k, BASE : BASE + n, :] = jnp.where(flip, odd[at, :], even[at, :])
+    for k, ((field_u, x_u), (field_v, x_v)) in enumerate(zip(upward, downward)):
+        at = slice(k, k + 1)
+        face[0, field_u, BASE + x_u : BASE + x_u + 1, :] = jnp.where(flip, even_late[at, :], odd_late[at, :])
+        face[1, field_v, BASE + x_v : BASE + x_v + 1, :] = jnp.where(flip, odd_late[at, :], even_late[at, :])
+
+    def up(k, x=0, size=n):
+        return keep(low, face[0, k, BASE + x : BASE + x + size, :])
+
+    def down(k, x=0, size=n):
+        return keep(high, face[1, k, BASE + x : BASE + x + size, :])
 
     def put(which, v, x=0):
         fix[which, BASE + x : BASE + x + v.shape[0], :] = v
@@ -353,53 +428,22 @@
     def strided(ref, y, c, x=0):
         return ref[c, pl.ds((x + 1) * r + y, n, stride=r), :]
 
-    put(hxm, up(0) - COURANT * keep(low, row_e(1)))
-    put(hxm, up(0, 1) - COURANT * keep(low, row_e(1, -1, 1)), -1)
-    put(hxm, up(1, 1) - COURANT * keep(low, row_e(1, n, 1)), n)
-    put(hzm, up(1) + COURANT * keep(low, row_e(0)))
-    put(hzm, up(2, 1) + COURANT * keep(low, row_e(0, -1, 1)), -1)
-    put(hzm, jnp.zeros((1, hs.shape[-1]), jnp.float32), n)
-    put(dz, COURANT * down(3))
-    put(dz, COURANT * down(2, 1), -2)
-    put(dz, COURANT * down(3, 1), -1)
-    put(dz, COURANT * down(5, 1), n)
-    put(dx, -COURANT * down(4))
-    put(dx, -COURANT * down(4, 1), -1)
-    put(dx, -COURANT * down(6, 1), n)
+    for x, size in ((0, n), (-1, 1), (n, 1)):
+        put(hxm, keep(low, up(0, x, size) - COURANT * row_e(1, x, size)), x)
+        put(dx, -COURANT * down(4, x, size), x)
+        put(dz, COURANT * down(3, x, size), x)
+    put(dz, COURANT * down(3, -2, 1), -2)
+    for x, size in ((0, n), (-1, 1)):
+        put(hzm, keep(low, up(1, x, size) + COURANT * row_e(0, x, size)), x)
+    put(hzm, jnp.zeros((1, h.shape[-1]), jnp.float32), n)
     for x, size in ((0, n), (-1, 1), (n, 1)):
         delta = get(dx, x, size)
         put(ry, delta - behind_z(delta) - get(dz, x, size) + get(dz, x - 1, size), x)
 
-    shape = (r, hs.shape[-1])
-    first_row, last_row = rows_of(shape) == 0, rows_of(shape) == last
-
-    def spread(which, x):
-        return fix[which, pl.ds(BASE + x, 1), :]
-
-    def amend(x):
-        at = pl.ds(pl.multiple_of((x + 1) * r, r), r)
-        half = c_ref[at, :]
-        d_x, d_z = jnp.where(last_row, spread(dx, x), 0.0), jnp.where(last_row, spread(dz, x), 0.0)
-        hs[0, at, :] = h[0, at, :] + d_x
-        hs[1, at, :] = h[1, at, :]
-        hs[2, at, :] = h[2, at, :] + d_z
-        es[0, at, :] = e[0, at, :] + half * jnp.where(first_row, -spread(hzm, x), d_z)
-        es[1, at, :] = e[1, at, :] + half * jnp.where(last_row, spread(ry, x), 0.0)
-        es[2, at, :] = e[2, at, :] + half * jnp.where(first_row, spread(hxm, x), -d_x)
-
-    def amend_block(i, carry):
-        for k in range(block):
-            amend(i * block + k)
-        return carry
-
-    amend(-1)
-    amend(n)
-    lax.fori_loop(0, n // block, amend_block, 0)
-
     half = down(2)
-    put(exp_, down(0) - half * strided(hs, last, 2))
-    put(exp_, down(0, 1) - down(1, 1) * hs[2, last : last + 1, :], -1)
-    put(ezp, down(1) + half * strided(hs, last, 0))
+    put(exp_, down(0) - half * (strided(h, last, 2) + get(dz)))
+    put(exp_, down(0, -1, 1) - down(2, -1, 1) * (h[2, last : last + 1, :] + get(dz, -1, 1)), -1)
+    put(ezp, down(1) + half * (strided(h, last, 0) + get(dx)))
     half = up(4)
 
     def gain(x, size, factor):
@@ -408,34 +452,42 @@
         return factor * (delta - behind_z(delta) - step)
 
     put(wm, gain(0, n, half))
-    put(wm, gain(n, 1, up(3, 1)), n)
+    put(wm, gain(n, 1, up(4, n, 1)), n)
     delta_x, delta_z = -COURANT * row_e(1), COURANT * row_e(0)
     change = get(wm)
-    put(
-        hxm2,
-        keep(
-            low,
-            up(2) + delta_x - COURANT * half * delta_x + COURANT * (ahead_z(change) - change) - COURANT * strided(es, 0, 2),
-        ),
-    )
-    put(
-        hzm2,
-        keep(
-            low,
-            up(3) + delta_z - COURANT * (get(wm, 1) - change) - COURANT * half * delta_z + COURANT * strided(es, 0, 0),
-        ),
-    )
-
-    def fields(ref, x):
+    here = c_ref[pl.ds(r, n, stride=r), :]
+    first_z = strided(e, 0, 2) + here * get(hxm)
+    first_x = strided(e, 0, 0) - here * get(hzm)
+    add = up(2) + delta_x - COURANT * half * delta_x + COURANT * (ahead_z(change) - change) - COURANT * first_z
+    put(hxm2, keep(low, add))
+    add = up(3) + delta_z - COURANT * half * delta_z - COURANT * (get(wm, 1) - change) + COURANT * first_x
+    put(hzm2, keep(low, add))
+
+    shape = (r, h.shape[-1])
+    first_row, last_row = rows_of(shape) == 0, rows_of(shape) == last
+
+    def spread(which, x):
+        return fix[which, pl.ds(BASE + x, 1), :]
+
+    def after_one(x):
         at = pl.ds(pl.multiple_of((x + 1) * r, r), r)
-        return [ref[c, at, :] for c in range(3)]
-
-    def second_h(x):
-        return new_h(fields(hs, x), fields(es, x), fields(es, x + 1), spread(exp_, x), spread(ezp, x))
-
-    def one(x, last_h):
-        now = fields(es, x)
-        mine = second_h(x)
+        half = c_ref[at, :]
+        d_x, d_z = jnp.where(last_row, spread(dx, x), 0.0), jnp.where(last_row, spread(dz, x), 0.0)
+        magnetic = (h[0, at, :] + d_x, h[1, at, :], h[2, at, :] + d_z)
+        electric = (
+            e[0, at, :] + half * jnp.where(first_row, -spread(hzm, x), d_z),
+            e[1, at, :] + half * jnp.where(last_row, spread(ry, x), 0.0),
+            e[2, at, :] + half * jnp.where(first_row, spread(hxm, x), -d_x),
+        )
+        return magnetic, electric
+
+    def second_h(x, magnetic, now, ahead):
+        return new_h(magnetic, now, ahead, spread(exp_, x), spread(ezp, x))
+
+    def one(x, carry):
+        last_h, magnetic, now = carry
+        next_magnetic, ahead = after_one(x + 1)
+        mine = second_h(x, magnetic, now, ahead)
         at = pl.ds(pl.multiple_of(x * r, r), r)
         half = c_ref[pl.ds(pl.multiple_of((x + 1) * r, r), r), :]
         dd = d[at, :]
@@ -449,24 +501,36 @@
             part = now[c] * f[c, at, :] + after * f[3 + c, at, :]
             total = part if total is None else total + part
         g_out[at, :] = total
-        return mine
-
-    def body(i, last_h):
+        return mine, next_magnetic, ahead
+
+    def body(i, carry):
         for k in range(block):
-            last_h = one(i * block + k, last_h)
-        return last_h
-
-    start = tuple(keep(below, v) for v in second_h(-1))
-    lax.fori_loop(0, n // block, body, start)
+            carry = one(i * block + k, carry)
+        return carry
+
+    magnetic, now = after_one(-1)
+    next_magnetic, ahead = after_one(0)
+    start = tuple(keep(below, v) for v in second_h(-1, magnetic, now, ahead))
+    lax.fori_loop(0, n // block, body, (start, next_magnetic, ahead))
+    for k, j in enumerate(rim_rows(r)):
+        rim_out[k * n : (k + 1) * n, :] = g_out[pl.ds(j, n, stride=r), :]
     first = jnp.where(odd_x(), 0, n - WIDTH)
     edge_out[...] = g_out[pl.ds(pl.multiple_of(first * r, r), WIDTH * r), :]
 
 
+def rim_rows(r):
+    return [j for j in range(r) if not REACH <= j < r - REACH]
+
+
 def update(n, r, generic, *refs):
     if generic:
-        g, other, edge, edge_m, far, far_m, d, m, even, odd, order, u_out, even_y, odd_y_out, u_pad = refs
+        g, mid, rim, edge, edge_m, far, far_m, d, m, even, odd, order, u_out, even_y, odd_y_out, u_pad, other = refs
     else:
-        g, other, edge, edge_m, d, m, even, odd, order, u_out, even_y, odd_y_out, u_pad = refs
+        g, mid, rim, edge, edge_m, d, m, even, odd, order, u_out, even_y, odd_y_out, u_pad, other = refs
+    for k, j in enumerate(range(REACH, r - REACH)):
+        other[pl.ds(j, n, stride=r), :] = mid[k * n : (k + 1) * n, :]
+    for k, j in enumerate(rim_rows(r)):
+        other[pl.ds(j, n, stride=r), :] = rim[k * n : (k + 1) * n, :]
     flip = odd_x()
     below, above, _, _ = edges()
     perm = order[...]
@@ -526,32 +590,36 @@
     return jnp.maximum(radius - math.sqrt(square), 0.0)
 
 
-def cover(n, r, radius, out):
+def cover(n, r, block, radius, out):
     x0, y0 = lax.axis_index("gx") * n, lax.axis_index("gy") * r
     total_x, total_y = n * lax.axis_size("gx"), r * lax.axis_size("gy")
     shape = (r, out.shape[-1])
     y = y0 + rows_of(shape)
-    one = jnp.ones(shape, jnp.float32)
+    ones = jnp.ones(shape, jnp.float32)
 
     def there(where, total):
         return ((where >= 0) & (where < total)).astype(jnp.float32)
 
-    across = [one] + [there(y - b, total_y) + there(y + b, total_y) for b in range(1, RMAX)]
-
-    def body(x, carry):
+    across = [ones] + [there(y - b, total_y) + there(y + b, total_y) for b in range(1, RMAX)]
+
+    def one(x):
         at = pl.ds(pl.multiple_of(x * r, r), r)
         rad = radius[at, :]
         where = jnp.full(shape, x0 + x, jnp.int32)
-        along = [one] + [there(where - a, total_x) + there(where + a, total_x) for a in range(1, RMAX)]
+        along = [ones] + [there(where - a, total_x) + there(where + a, total_x) for a in range(1, RMAX)]
         total = None
         for square, members in CLASSES:
             part = sum(across[b] * along[a] for b, a in members)
             part = weight(rad, square) * part
             total = part if total is None else total + part
         out[at, :] = 1.0 / total
+
+    def body(i, carry):
+        for k in range(block):
+            one(i * block + k)
         return carry
 
-    lax.fori_loop(0, n, body, 0)
+    lax.fori_loop(0, n // block, body, 0)
 
 
 def smooth(n, r, block, u, even, odd, radius, inverse, out, halo, sums):
@@ -635,7 +703,7 @@
     f = forward_rate.reshape(3 * STEPS, size, depth)
     more = size + 2 * r
     face_x = (SLOTS * r, depth)
-    face_y = (5 * n + EXTRA, depth)
+    face_y = (5 * n, depth)
     lines = n + 2 * BASE
 
     f32 = jnp.float32
@@ -658,27 +726,46 @@
     odd = send(odd, x_odd)
 
     inner = functools.partial(step_inner, n, r, 16)
-    h1, e1, c1, t1 = call(inner, [(3, more, depth)] * 2 + [(more, depth), (3, size, depth)], [e, h, p, q, d], flops=100 * size * depth)
+    h1, e1, c1, t1, even_y, odd_y_ = call(
+        inner,
+        [(3, more, depth)] * 2 + [(more, depth), (3, size, depth)] + [face_y] * 2,
+        [e, h, p, q, d],
+        flops=100 * size * depth,
+    )
+    odd_y_ = send(odd_y_, y_odd)
+    even_y = send(even_y, y_even)
     ends = functools.partial(step_edges, n, r)
-    h1, e1, c1, rows, even_y, odd_y_ = call(
+    h1, e1, c1, rows, even_late, odd_late = call(
         ends,
-        [(3, more, depth)] * 2 + [(more, depth), (2, lines, depth)] + [face_y] * 2,
+        [(3, more, depth)] * 2 + [(more, depth), (2, lines, depth)] + [(LATE, depth)] * 2,
         [e, h, p, q, d, even, odd, h1, e1, c1],
         aliases={7: 0, 8: 1, 9: 2},
     )
-    odd_y_ = send(odd_y_, y_odd)
-    even_y = send(even_y, y_even)
+    odd_late = send(odd_late, y_odd)
+    even_late = send(even_late, y_even)
+    (mid,) = call(
+        functools.partial(step_mid, n, r, 16),
+        [((r - 2 * REACH) * n, depth)],
+        [h1, e1, c1, t1, d, f],
+        flops=100 * size * depth,
+        scratch=[VMEM((size, depth), jnp.float32)],
+    )
+    mid = send(mid, mirror)
 
     radius = jnp.broadcast_to(filter_radius.astype(jnp.float32)[:, :, None], (n, r, depth)).reshape(size, depth)
     order = jnp.broadcast_to(partner_rows[:, None], (r, depth))
-    (inverse,) = call(functools.partial(cover, n, r), [(size, depth)], [radius], flops=100 * size * depth)
-
-    final = functools.partial(step_last, n, r, 16)
-    args = [h1, e1, c1, t1, d, rows, even_y, odd_y_, f]
-    e2, h2, g, edge = step_call(final, n, r, depth, args)
+    (inverse,) = call(functools.partial(cover, n, r, 16), [(size, depth)], [radius], flops=100 * size * depth)
+
+    e2, h2, g, rim, edge = call(
+        functools.partial(step_last, n, r, 16),
+        [(3, size, depth)] * 2 + [(size, depth), (2 * REACH * n, depth), (WIDTH * r, depth)],
+        [h1, e1, c1, t1, d, rows, even_y, odd_y_, even_late, odd_late, f],
+        flops=150 * size * depth,
+        scratch=[VMEM((2, 5, lines, depth), jnp.float32), VMEM((10, lines, depth), jnp.float32)],
+    )
+    rim = send(rim, mirror)
+    edge_m = send(edge, mirror_even)
     edge_e = send(edge, x_even)
-    edge_m = send(edge, mirror_even)
-    other = send(g, mirror)
     generic = lax.axis_size("gx") != 4
     extra = []
     if generic:
@@ -687,45 +774,25 @@
         extra = [send(far, x_odd), send(far, mirror_odd)]
     full = n + 2 * WIDTH
     wide = -(-full // 8) * 8
-    u, even_u, odd_u = scratch_call(
+    u, even_u, odd_u = call(
         functools.partial(update, n, r, generic),
         [(full * r, depth), (WIDTH * wide, depth), (WIDTH * wide, depth)],
-        [g, other, edge_e, edge_m] + extra + [d, m, even, odd, order],
-        [VMEM((wide * r, depth), jnp.float32)],
+        [g, mid, rim, edge_e, edge_m] + extra + [d, m, even, odd, order],
+        scratch=[VMEM((wide * r, depth), jnp.float32), VMEM((size, depth), jnp.float32)],
     )
     odd_u = send(odd_u, y_odd)
     even_u = send(even_u, y_even)
-    (out,) = scratch_call(
+    (out,) = call(
         functools.partial(smooth, n, r, 16),
         [(size, depth)],
         [u, even_u, odd_u, radius, inverse],
-        [VMEM((wide * r, depth), jnp.float32), VMEM((WIDTH, full * r, depth), jnp.float32)],
+        scratch=[VMEM((wide * r, depth), jnp.float32), VMEM((WIDTH, full * r, depth), jnp.float32)],
     )
     return (
         e2.reshape(3, n, r, depth),
         h2.reshape(3, n, r, depth),
         out.reshape(n, r, depth),
     )
-
-
-def scratch_call(kernel, outs, args, scratch):
-    args = [pltpu.with_memory_space_constraint(a, VMEM) for a in args]
-    spec = pl.BlockSpec(memory_space=VMEM)
-    return pl.pallas_call(
-        kernel,
-        out_shape=tuple(VMEM(s, jnp.float32) for s in outs),
-        in_specs=[spec] * len(args),
-        out_specs=tuple([spec] * len(outs)),
-        scratch_shapes=scratch,
-        compiler_params=pltpu.CompilerParams(vmem_limit_bytes=16 * 2**20),
-    )(*args)
-
-
-def step_call(kernel, n, r, depth, args):
-    more = (3, (n + 2) * r, depth)
-    scratch = [VMEM(more, jnp.float32)] * 2 + [VMEM((10, n + 2 * BASE, depth), jnp.float32), VMEM((2, r, depth), jnp.float32)]
-    size = (3, n * r, depth)
-    return scratch_call(kernel, [size, size, (n * r, depth), (WIDTH * r, depth)], args, scratch)
 
 
 def solution(mesh):

time: 27.5 us -> 25.7 us (0.935)
  the two profiles are of different devices: /device:TPU:8 before, /device:TPU:12 now
where the time goes in v3:
time: 25.7 us; the launch traced here: 25.4 us
  starting transfers between devices  12.3 us (48%)
  waiting for transfers between devices  5.99 us (23%)
  Pallas kernels  3.87 us (15%)
  local copies, waits for them, and re-layouts  2.52 us (10%)
  between operations  0.77 us (3%)
    ppermute x12, starting transfers between devices, send(): return lax.ppermute(block, AXES, route)  12.3 us
    ppermute x12, waiting for transfers between devices, send(): return lax.ppermute(block, AXES, route)  5.99 us
    pallas_call x7, Pallas kernels, call(): pl.pallas_call(kernel, out_shape=tuple((VMEM(s, jnp.float32) for s in out...  2.81 us
    unnamed x21, local copies, waits for them, and re-layouts  2.19 us
    pallas_call x1, Pallas kernels, local(): pl.pallas_call(functools.partial(pack_x, n, r), out_shape=(VMEM(face_x, f...  1.06 us
  transfers between devices with their start and end apart: 12, of which 4 were waited for; matrix products, arithmetic and copies ran while one was open for 7% of the time, Pallas kernels for 9%

profile of v3, /device:TPU:12, one launch (start us, length us, event | category | flops | bytes accessed | tf_op | source)
XLA Modules:
  0.0 25.4 jit_solution(16016814276734512551)
XLA Ops:
  0.7 1.1 %shard_map.112 = (f32[160,128]{1,0:T(8,128)S(1)}, f32[160,128]{1,0:T(8,128)S(1)}) custom-call(f32[3,256,128]{2,1,0:T(8,128)} %bitcast.19, f32[3,256,128]{2,1,0:T(8,128)} %bitcast.22, f32[3,256,128]{2,1,0:T(8,128)} %bitcast.25, f32[3,256,128]{2,1,0:T(8,128)} %bitcast.28, f32[256,128]{1,0:T(8,128)} %bitcast.13, s32[256,128]{1,0:T(8,128)} %bitcast.33), custom_call_target="tpu_custom_call" | custom-call | tf_op jit(solution)/shard_map/pallas_call | solution.py:710
  1.8 0.6 %collective-permute-start.1 = (f32[160,128]{1,0:T(8,128)S(1)}, f32[160,128]{1,0:T(8,128)S(1)}, u32[]{:S(2)}, u32[]{:S(2)}) collective-permute-start(f32[160,128]{1,0:T(8,128)S(1)} %get-tuple-element.26), channel_id=1, source_target_pairs={{0,1},{1,0},{2,3},{3,2},{4,5},{5,4},{6,7},{7,6},{8,16},{9,17},{10,... | collective-permute-start | bytes 245768 | tf_op jit(solution)/shard_map/ppermute | solution.py:78
  2.4 0.5 %shard_map.113 = (f32[3,272,128]{2,1,0:T(8,128)S(1)}, f32[3,272,128]{2,1,0:T(8,128)S(1)}, f32[272,128]{1,0:T(8,128)S(1)}, f32[3,256,128]{2,1,0:T(8,128)S(1)}, f3...) custom-call(f32[3,256,128]{2,1,0:T(8,128)S(1)} %bitcast.20, f32[3,256,128]{2,1,0:T(8,128)S(1)} %bitcast.23, ...), custom_call_target="tpu_custom_call" | custom-call | flops 3276800 | bytes 3235840 | tf_op jit(solution)/shard_map/pallas_call | solution.py:127
  2.9 1.6 %collective-permute-start.2 = (f32[160,128]{1,0:T(8,128)S(1)}, f32[160,128]{1,0:T(8,128)S(1)}, u32[]{:S(2)}, u32[]{:S(2)}) collective-permute-start(f32[160,128]{1,0:T(8,128)S(1)} %get-tuple-element.35), channel_id=1, source_target_pairs={{0,1},{1,0},{2,3},{3,2},{4,5},{5,4},{6,7},{7,6},{8,9},{9,8},{10,11... | collective-permute-start | bytes 245768 | tf_op jit(solution)/shard_map/ppermute | solution.py:78
  4.5 1.5 %collective-permute-start.3 = (f32[160,128]{1,0:T(8,128)S(1)}, f32[160,128]{1,0:T(8,128)S(1)}, u32[]{:S(2)}, u32[]{:S(2)}) collective-permute-start(f32[160,128]{1,0:T(8,128)S(1)} %get-tuple-element.36), channel_id=1, source_target_pairs={{0,8},{1,2},{2,1},{3,4},{4,3},{5,6},{6,5},{7,15},{8,0},{9,10},{10,... | collective-permute-start | bytes 245768 | tf_op jit(solution)/shard_map/ppermute | solution.py:78
  6.1 0.3 %collective-permute-done.1.odd.refs_8_ = f32[160,128]{1,0:T(8,128)S(1)} collective-permute-done((f32[160,128]{1,0:T(8,128)S(1)}, f32[160,128]{1,0:T(8,128)S(1)}, u32[]{:S(2)}, u32[]{:S(2)}) %collective-permute-start.1) | collective-permute-done | bytes 81952 | tf_op jit(solution)/shard_map/ppermute | solution.py:78
  6.3 0.2 shard_map.114
  6.6 0.5 %collective-permute-start.4 = (f32[16,128]{1,0:T(8,128)S(1)}, f32[16,128]{1,0:T(8,128)S(1)}, u32[]{:S(2)}, u32[]{:S(2)}) collective-permute-start(f32[16,128]{1,0:T(8,128)S(1)} %get-tuple-element.37), channel_id=1, source_target_pairs={{0,1},{1,0},{2,3},{3,2},{4,5},{5,4},{6,7},{7,6},{8,9},{9,8},{10,11... | collective-permute-start | bytes 24584 | tf_op jit(solution)/shard_map/ppermute | solution.py:78
  7.1 2.5 %collective-permute-start.5 = (f32[16,128]{1,0:T(8,128)S(1)}, f32[16,128]{1,0:T(8,128)S(1)}, u32[]{:S(2)}, u32[]{:S(2)}) collective-permute-start(f32[16,128]{1,0:T(8,128)S(1)} %get-tuple-element.38), channel_id=1, source_target_pairs={{0,8},{1,2},{2,1},{3,4},{4,3},{5,6},{6,5},{7,15},{8,0},{9,10},{10,... | collective-permute-start | bytes 24584 | tf_op jit(solution)/shard_map/ppermute | solution.py:78
  9.6 0.5 %shard_map.116 = f32[128,128]{1,0:T(8,128)S(1)} custom-call(f32[3,272,128]{2,1,0:T(8,128)S(1)} %get-tuple-element.30.h, f32[3,272,128]{2,1,0:T(8,128)S(1)} %get-tuple-element.31.e, f32[272,128]{1,0:T(8,128)S(1)} %get-tuple-element.32.c_ref, f32[3,256,128]{2,1,0:T(8,128)S(1)} %get-tuple-element.33.t, f32[256,128]{1,0:T(8,128)S(1)} %bitcast.16, ...), custom_call_target="tpu_custom_call" | custom-call | flops 3276800 | bytes 2351104 | tf_op jit(solution)/shard_map/pallas_call | solution.py:127
  10.3 1.3 %collective-permute-done.5.odd_late = f32[16,128]{1,0:T(8,128)S(1)} collective-permute-done((f32[16,128]{1,0:T(8,128)S(1)}, f32[16,128]{1,0:T(8,128)S(1)}, u32[]{:S(2)}, u32[]{:S(2)}) %collective-permute-start.5) | collective-permute-done | bytes 8224 | tf_op jit(solution)/shard_map/ppermute | solution.py:78
  11.7 0.6 %shard_map.115 = (f32[3,256,128]{2,1,0:T(8,128)S(1)}, f32[3,256,128]{2,1,0:T(8,128)S(1)}, f32[256,128]{1,0:T(8,128)S(1)}, f32[128,128]{1,0:T(8,128)S(1)}, f32[24,128]{1,0:T(8,128)S(1)}) custom-call(f32[3,272,128]{2,1,0:T(8,128)S(1)} %get-tuple-element.30.h, f32[3,272,128]{2,1,0:T(8,128)S(1)} %get-tuple-element.31.e, f32[272,128]{1,0:T(8,128)S(1)} %get-tuple-element.32.c_ref, ...), custom_call_target="tpu_custom_call" | custom-call | flops 4915200 | bytes 3510272 | tf_op jit(solution)/shard_map/pallas_call | solution.py:127
  12.3 0.4 %collective-permute-start.7 = (f32[128,128]{1,0:T(8,128)S(1)}, f32[128,128]{1,0:T(8,128)S(1)}, u32[]{:S(2)}, u32[]{:S(2)}) collective-permute-start(f32[128,128]{1,0:T(8,128)S(1)} %get-tuple-element.42), channel_id=1, source_target_pairs={{0,24},{1,25},{2,26},{3,27},{4,28},{5,29},{6,30},{7,31},{8,16},{9,... | collective-permute-start | bytes 196616 | tf_op jit(solution)/shard_map/ppermute | solution.py:78
  12.7 0.7 %collective-permute-start.8 = (f32[24,128]{1,0:T(8,128)S(1)}, f32[24,128]{1,0:T(8,128)S(1)}, u32[]{:S(2)}, u32[]{:S(2)}) collective-permute-start(f32[24,128]{1,0:T(8,128)S(1)} %get-tuple-element.43), channel_id=1, source_target_pairs={{0,8},{1,9},{2,10},{3,11},{4,12},{5,13},{6,14},{7,15},{8,0},{9,1},... | collective-permute-start | bytes 36872 | tf_op jit(solution)/shard_map/ppermute | solution.py:78
  13.4 1.1 %collective-permute-start.9 = (f32[24,128]{1,0:T(8,128)S(1)}, f32[24,128]{1,0:T(8,128)S(1)}, u32[]{:S(2)}, u32[]{:S(2)}) collective-permute-start(f32[24,128]{1,0:T(8,128)S(1)} %get-tuple-element.43), channel_id=1, source_target_pairs={{0,16},{1,17},{2,18},{3,19},{4,20},{5,21},{6,22},{7,23},{8,24},{9,... | collective-permute-start | bytes 36872 | tf_op jit(solution)/shard_map/ppermute | solution.py:78
  14.5 2.6 %collective-permute-done.9.refs_4_ = f32[24,128]{1,0:T(8,128)S(1)} collective-permute-done((f32[24,128]{1,0:T(8,128)S(1)}, f32[24,128]{1,0:T(8,128)S(1)}, u32[]{:S(2)}, u32[]{:S(2)}) %collective-permute-start.9) | collective-permute-done | bytes 12320 | tf_op jit(solution)/shard_map/ppermute | solution.py:78
  17.3 2.0 %collective-permute-start.10 = (f32[120,128]{1,0:T(8,128)S(1)}, f32[120,128]{1,0:T(8,128)S(1)}, u32[]{:S(2)}, u32[]{:S(2)}) collective-permute-start(f32[120,128]{1,0:T(8,128)S(1)} %get-tuple-element.45), channel_id=1, source_target_pairs={{0,1},{1,0},{2,3},{3,2},{4,5},{5,4},{6,7},{7,6},{8,9},{9,8},{10,11... | collective-permute-start | bytes 184328 | tf_op jit(solution)/shard_map/ppermute | solution.py:78
  19.2 1.1 %collective-permute-start.11 = (f32[120,128]{1,0:T(8,128)S(1)}, f32[120,128]{1,0:T(8,128)S(1)}, u32[]{:S(2)}, u32[]{:S(2)}) collective-permute-start(f32[120,128]{1,0:T(8,128)S(1)} %get-tuple-element.46), channel_id=1, source_target_pairs={{0,8},{1,2},{2,1},{3,4},{4,3},{5,6},{6,5},{7,15},{8,0},{9,10},{10,... | collective-permute-start | bytes 184328 | tf_op jit(solution)/shard_map/ppermute | solution.py:78
  20.7 0.4 %shard_map.118.inverse = f32[256,128]{1,0:T(8,128)S(1)} custom-call(f32[256,128]{1,0:T(8,128)S(1)} %broadcast_in_dim.16.radius), custom_call_target="tpu_custom_call" | custom-call | flops 3276800 | bytes 262144 | tf_op jit(solution)/shard_map/pallas_call | solution.py:127
  21.1 0.7 %copy.19 = f32[3,32,8,128]{3,2,1,0:T(8,128)} copy(f32[3,32,8,128]{3,2,1,0:T(8,128)S(1)} %bitcast.12) | data formatting | bytes 786432
  21.8 0.7 %copy.20 = f32[3,32,8,128]{3,2,1,0:T(8,128)} copy(f32[3,32,8,128]{3,2,1,0:T(8,128)S(1)} %bitcast.11) | data formatting | bytes 786432
  22.6 1.8 %collective-permute-done.11.odd = f32[120,128]{1,0:T(8,128)S(1)} collective-permute-done((f32[120,128]{1,0:T(8,128)S(1)}, f32[120,128]{1,0:T(8,128)S(1)}, u32[]{:S(2)}, u32[]{:S(2)}) %collective-permute-start.11) | collective-permute-done | bytes 61472 | tf_op jit(solution)/shard_map/ppermute | solution.py:78
  24.4 0.4 %shard_map.119 = f32[256,128]{1,0:T(8,128)S(1)} custom-call(f32[304,128]{1,0:T(8,128)S(1)} %get-tuple-element.44.u, f32[120,128]{1,0:T(8,128)S(1)} %collective-permute-done.10.even, f32[120,128]{1,0:T(8,128)S(1)} %collective-permute-done.11.odd, f32[256,128]{1,0:T(8,128)S(1)} %broadcast_in_dim.16.radius, f32[256,128]{1,0:T(8,128)S(1)} %shard_map.118.inverse), custom_call_target="tpu_custom_call" | custom-call | bytes 671744 | tf_op jit(solution)/shard_map/pallas_call | solution.py:127
  24.8 0.7 %copy.21 = f32[32,8,128]{2,1,0:T(8,128)} copy(f32[32,8,128]{2,1,0:T(8,128)S(1)} %bitcast.10) | data formatting | bytes 262144
  (34 shorter events, 0.7 us)
Async XLA Ops:
  0.6 1.8 %copy-start = (f32[32,8,128]{2,1,0:T(8,128)S(1)}, f32[32,8,128]{2,1,0:T(8,128)}, u32[]{:S(2)}) copy-start(f32[32,8,128]{2,1,0:T(8,128)} %param.13) | copy-start | bytes 393220
  0.6 1.8 %copy-start.1 = (f32[3,32,8,128]{3,2,1,0:T(8,128)S(1)}, f32[3,32,8,128]{3,2,1,0:T(8,128)}, u32[]{:S(2)}) copy-start(f32[3,32,8,128]{3,2,1,0:T(8,128)} %param.9) | copy-start | bytes 1179652
  0.7 1.8 %copy-start.2 = (f32[3,32,8,128]{3,2,1,0:T(8,128)S(1)}, f32[3,32,8,128]{3,2,1,0:T(8,128)}, u32[]{:S(2)}) copy-start(f32[3,32,8,128]{3,2,1,0:T(8,128)} %param.10) | copy-start | bytes 1179652
  0.7 1.8 %copy-start.3 = (f32[3,32,8,128]{3,2,1,0:T(8,128)S(1)}, f32[3,32,8,128]{3,2,1,0:T(8,128)}, u32[]{:S(2)}) copy-start(f32[3,32,8,128]{3,2,1,0:T(8,128)} %param.11) | copy-start | bytes 1179652
  0.7 1.7 %copy-start.4 = (f32[3,32,8,128]{3,2,1,0:T(8,128)S(1)}, f32[3,32,8,128]{3,2,1,0:T(8,128)}, u32[]{:S(2)}) copy-start(f32[3,32,8,128]{3,2,1,0:T(8,128)} %param.12) | copy-start | bytes 1179652
  1.8 4.3 %collective-permute-start = (f32[160,128]{1,0:T(8,128)S(1)}, f32[160,128]{1,0:T(8,128)S(1)}, u32[]{:S(2)}, u32[]{:S(2)}) collective-permute-start(f32[160,128]{1,0:T(8,128)S(1)} %get-tuple-element.25), channel_id=1, source_target_pairs={{0,8},{1,9},{2,10},{3,11},{4,12},{5,13},{6,14},{7,15},{8,0},{9,1},... | collective-permute-start | bytes 245768 | tf_op jit(solution)/shard_map/ppermute | solution.py:78
  1.8 4.5 %collective-permute-start.1 = (f32[160,128]{1,0:T(8,128)S(1)}, f32[160,128]{1,0:T(8,128)S(1)}, u32[]{:S(2)}, u32[]{:S(2)}) collective-permute-start(f32[160,128]{1,0:T(8,128)S(1)} %get-tuple-element.26), channel_id=1, source_target_pairs={{0,1},{1,0},{2,3},{3,2},{4,5},{5,4},{6,7},{7,6},{8,16},{9,17},{10,... | collective-permute-start | bytes 245768 | tf_op jit(solution)/shard_map/ppermute | solution.py:78
  2.9 7.4 %collective-permute-start.2 = (f32[160,128]{1,0:T(8,128)S(1)}, f32[160,128]{1,0:T(8,128)S(1)}, u32[]{:S(2)}, u32[]{:S(2)}) collective-permute-start(f32[160,128]{1,0:T(8,128)S(1)} %get-tuple-element.35), channel_id=1, source_target_pairs={{0,1},{1,0},{2,3},{3,2},{4,5},{5,4},{6,7},{7,6},{8,9},{9,8},{10,11... | collective-permute-start | bytes 245768 | tf_op jit(solution)/shard_map/ppermute | solution.py:78
  4.5 5.8 %collective-permute-start.3 = (f32[160,128]{1,0:T(8,128)S(1)}, f32[160,128]{1,0:T(8,128)S(1)}, u32[]{:S(2)}, u32[]{:S(2)}) collective-permute-start(f32[160,128]{1,0:T(8,128)S(1)} %get-tuple-element.36), channel_id=1, source_target_pairs={{0,8},{1,2},{2,1},{3,4},{4,3},{5,6},{6,5},{7,15},{8,0},{9,10},{10,... | collective-permute-start | bytes 245768 | tf_op jit(solution)/shard_map/ppermute | solution.py:78
  6.3 3.3 %copy-start.5 = (f32[2,3,32,8,128]{4,3,2,1,0:T(8,128)S(1)}, f32[2,3,32,8,128]{4,3,2,1,0:T(8,128)}, u32[]{:S(2)}) copy-start(f32[2,3,32,8,128]{4,3,2,1,0:T(8,128)} %param.14) | copy-start | bytes 2359300
  6.6 3.8 %collective-permute-start.4 = (f32[16,128]{1,0:T(8,128)S(1)}, f32[16,128]{1,0:T(8,128)S(1)}, u32[]{:S(2)}, u32[]{:S(2)}) collective-permute-start(f32[16,128]{1,0:T(8,128)S(1)} %get-tuple-element.37), channel_id=1, source_target_pairs={{0,1},{1,0},{2,3},{3,2},{4,5},{5,4},{6,7},{7,6},{8,9},{9,8},{10,11... | collective-permute-start | bytes 24584 | tf_op jit(solution)/shard_map/ppermute | solution.py:78
  7.1 4.5 %collective-permute-start.5 = (f32[16,128]{1,0:T(8,128)S(1)}, f32[16,128]{1,0:T(8,128)S(1)}, u32[]{:S(2)}, u32[]{:S(2)}) collective-permute-start(f32[16,128]{1,0:T(8,128)S(1)} %get-tuple-element.38), channel_id=1, source_target_pairs={{0,8},{1,2},{2,1},{3,4},{4,3},{5,6},{6,5},{7,15},{8,0},{9,10},{10,... | collective-permute-start | bytes 24584 | tf_op jit(solution)/shard_map/ppermute | solution.py:78
  10.2 6.9 %collective-permute-start.6 = (f32[128,128]{1,0:T(8,128)S(1)}, f32[128,128]{1,0:T(8,128)S(1)}, u32[]{:S(2)}, u32[]{:S(2)}) collective-permute-start(f32[128,128]{1,0:T(8,128)S(1)} %shard_map.116), channel_id=1, source_target_pairs={{0,24},{1,25},{2,26},{3,27},{4,28},{5,29},{6,30},{7,31},{8,16},{9,... | collective-permute-start | bytes 196616 | tf_op jit(solution)/shard_map/ppermute | solution.py:78
  11.6 5.5 %copy-start.6 = (s32[32,8,128]{2,1,0:T(8,128)S(1)}, s32[32,8,128]{2,1,0:T(8,128)}, u32[]{:S(2)}) copy-start(s32[32,8,128]{2,1,0:T(8,128)} %param.15) | copy-start | bytes 393220
  12.3 4.8 %collective-permute-start.7 = (f32[128,128]{1,0:T(8,128)S(1)}, f32[128,128]{1,0:T(8,128)S(1)}, u32[]{:S(2)}, u32[]{:S(2)}) collective-permute-start(f32[128,128]{1,0:T(8,128)S(1)} %get-tuple-element.42), channel_id=1, source_target_pairs={{0,24},{1,25},{2,26},{3,27},{4,28},{5,29},{6,30},{7,31},{8,16},{9,... | collective-permute-start | bytes 196616 | tf_op jit(solution)/shard_map/ppermute | solution.py:78
  12.7 4.4 %copy-start.8 = (s32[8]{0:T(128)S(1)}, s32[8]{0:T(128)}, u32[]{:S(2)}) copy-start(s32[8]{0:T(128)} %param.16) | copy-start | bytes 100
  12.7 1.8 %collective-permute-start.8 = (f32[24,128]{1,0:T(8,128)S(1)}, f32[24,128]{1,0:T(8,128)S(1)}, u32[]{:S(2)}, u32[]{:S(2)}) collective-permute-start(f32[24,128]{1,0:T(8,128)S(1)} %get-tuple-element.43), channel_id=1, source_target_pairs={{0,8},{1,9},{2,10},{3,11},{4,12},{5,13},{6,14},{7,15},{8,0},{9,1},... | collective-permute-start | bytes 36872 | tf_op jit(solution)/shard_map/ppermute | solution.py:78
  13.4 3.7 %collective-permute-start.9 = (f32[24,128]{1,0:T(8,128)S(1)}, f32[24,128]{1,0:T(8,128)S(1)}, u32[]{:S(2)}, u32[]{:S(2)}) collective-permute-start(f32[24,128]{1,0:T(8,128)S(1)} %get-tuple-element.43), channel_id=1, source_target_pairs={{0,16},{1,17},{2,18},{3,19},{4,20},{5,21},{6,22},{7,23},{8,24},{9,... | collective-permute-start | bytes 36872 | tf_op jit(solution)/shard_map/ppermute | solution.py:78
  17.2 3.2 %copy-start.7 = (s32[32,8]{0,1:T(8,128)S(1)}, s32[32,8]{0,1:T(8,128)}, u32[]{:S(2)}) copy-start(s32[32,8]{0,1:T(8,128)} %param.17) | copy-start | bytes 3076
  17.3 5.3 %collective-permute-start.10 = (f32[120,128]{1,0:T(8,128)S(1)}, f32[120,128]{1,0:T(8,128)S(1)}, u32[]{:S(2)}, u32[]{:S(2)}) collective-permute-start(f32[120,128]{1,0:T(8,128)S(1)} %get-tuple-element.45), channel_id=1, source_target_pairs={{0,1},{1,0},{2,3},{3,2},{4,5},{5,4},{6,7},{7,6},{8,9},{9,8},{10,11... | collective-permute-start | bytes 184328 | tf_op jit(solution)/shard_map/ppermute | solution.py:78
  19.2 5.1 %collective-permute-start.11 = (f32[120,128]{1,0:T(8,128)S(1)}, f32[120,128]{1,0:T(8,128)S(1)}, u32[]{:S(2)}, u32[]{:S(2)}) collective-permute-start(f32[120,128]{1,0:T(8,128)S(1)} %get-tuple-element.46), channel_id=1, source_target_pairs={{0,8},{1,2},{2,1},{3,4},{4,3},{5,6},{6,5},{7,15},{8,0},{9,10},{10,... | collective-permute-start | bytes 184328 | tf_op jit(solution)/shard_map/ppermute | solution.py:78

commit v4 on v3

--- a/solution.py
+++ b/solution.py
@@ -394,7 +394,7 @@
 
 
 def step_last(
-    n, r, block, h, e, c_ref, t, d, rows, even, odd, even_late, odd_late, f, e_out, h_out, g_out, rim_out, edge_out, face, fix
+    n, r, block, h, e, c_ref, t, d, rows, even, odd, odd_late, even_late, f, e_out, h_out, g_out, rim_out, edge_out, face, fix
 ):
     flip = odd_y()
     below, above, low, high = edges()
@@ -524,9 +524,9 @@
 
 def update(n, r, generic, *refs):
     if generic:
-        g, mid, rim, edge, edge_m, far, far_m, d, m, even, odd, order, u_out, even_y, odd_y_out, u_pad, other = refs
+        g, mid, rim, edge_m, edge, far, far_m, d, m, even, odd, order, u_out, even_y, odd_y_out, u_pad, other = refs
     else:
-        g, mid, rim, edge, edge_m, d, m, even, odd, order, u_out, even_y, odd_y_out, u_pad, other = refs
+        g, mid, rim, edge_m, edge, d, m, even, odd, order, u_out, even_y, odd_y_out, u_pad, other = refs
     for k, j in enumerate(range(REACH, r - REACH)):
         other[pl.ds(j, n, stride=r), :] = mid[k * n : (k + 1) * n, :]
     for k, j in enumerate(rim_rows(r)):
@@ -759,7 +759,7 @@
     e2, h2, g, rim, edge = call(
         functools.partial(step_last, n, r, 16),
         [(3, size, depth)] * 2 + [(size, depth), (2 * REACH * n, depth), (WIDTH * r, depth)],
-        [h1, e1, c1, t1, d, rows, even_y, odd_y_, even_late, odd_late, f],
+        [h1, e1, c1, t1, d, rows, even_y, odd_y_, odd_late, even_late, f],
         flops=150 * size * depth,
         scratch=[VMEM((2, 5, lines, depth), jnp.float32), VMEM((10, lines, depth), jnp.float32)],
     )
@@ -777,7 +777,7 @@
     u, even_u, odd_u = call(
         functools.partial(update, n, r, generic),
         [(full * r, depth), (WIDTH * wide, depth), (WIDTH * wide, depth)],
-        [g, mid, rim, edge_e, edge_m] + extra + [d, m, even, odd, order],
+        [g, mid, rim, edge_m, edge_e] + extra + [d, m, even, odd, order],
         scratch=[VMEM((wide * r, depth), jnp.float32), VMEM((size, depth), jnp.float32)],
     )
     odd_u = send(odd_u, y_odd)

time: 25.7 us -> 24.7 us (0.961)
  the two profiles are of different devices: /device:TPU:12 before, /device:TPU:8 now
where the time goes in v4:
time: 24.7 us; the launch traced here: 24.4 us
  starting transfers between devices  10.7 us (43%)
  waiting for transfers between devices  6.6 us (27%)
  Pallas kernels  3.87 us (16%)
  local copies, waits for them, and re-layouts  2.52 us (10%)
  between operations  0.77 us (3%)
    ppermute x12, starting transfers between devices, send(): return lax.ppermute(block, AXES, route)  10.7 us
    ppermute x12, waiting for transfers between devices, send(): return lax.ppermute(block, AXES, route)  6.6 us
    pallas_call x7, Pallas kernels, call(): pl.pallas_call(kernel, out_shape=tuple((VMEM(s, jnp.float32) for s in out...  2.81 us
    unnamed x21, local copies, waits for them, and re-layouts  2.19 us
    pallas_call x1, Pallas kernels, local(): pl.pallas_call(functools.partial(pack_x, n, r), out_shape=(VMEM(face_x, f...  1.06 us
  transfers between devices with their start and end apart: 12, of which 7 were waited for; matrix products, arithmetic and copies ran while one was open for 7% of the time, Pallas kernels for 10%

profile of v4, /device:TPU:8, one launch (start us, length us, event | category | flops | bytes accessed | tf_op | source)
XLA Modules:
  0.0 24.4 jit_solution(11253458752357090859)
XLA Ops:
  0.7 1.1 %shard_map.112 = (f32[160,128]{1,0:T(8,128)S(1)}, f32[160,128]{1,0:T(8,128)S(1)}) custom-call(f32[3,256,128]{2,1,0:T(8,128)} %bitcast.19, f32[3,256,128]{2,1,0:T(8,128)} %bitcast.22, f32[3,256,128]{2,1,0:T(8,128)} %bitcast.25, f32[3,256,128]{2,1,0:T(8,128)} %bitcast.28, f32[256,128]{1,0:T(8,128)} %bitcast.13, s32[256,128]{1,0:T(8,128)} %bitcast.33), custom_call_target="tpu_custom_call" | custom-call | tf_op jit(solution)/shard_map/pallas_call | solution.py:710
  1.8 1.6 %collective-permute-start.1 = (f32[160,128]{1,0:T(8,128)S(1)}, f32[160,128]{1,0:T(8,128)S(1)}, u32[]{:S(2)}, u32[]{:S(2)}) collective-permute-start(f32[160,128]{1,0:T(8,128)S(1)} %get-tuple-element.26), channel_id=1, source_target_pairs={{0,1},{1,0},{2,3},{3,2},{4,5},{5,4},{6,7},{7,6},{8,16},{9,17},{10,... | collective-permute-start | bytes 245768 | tf_op jit(solution)/shard_map/ppermute | solution.py:78
  3.4 0.5 %shard_map.113 = (f32[3,272,128]{2,1,0:T(8,128)S(1)}, f32[3,272,128]{2,1,0:T(8,128)S(1)}, f32[272,128]{1,0:T(8,128)S(1)}, f32[3,256,128]{2,1,0:T(8,128)S(1)}, f3...) custom-call(f32[3,256,128]{2,1,0:T(8,128)S(1)} %bitcast.20, f32[3,256,128]{2,1,0:T(8,128)S(1)} %bitcast.23, ...), custom_call_target="tpu_custom_call" | custom-call | flops 3276800 | bytes 3235840 | tf_op jit(solution)/shard_map/pallas_call | solution.py:127
  4.0 0.6 %collective-permute-start.2 = (f32[160,128]{1,0:T(8,128)S(1)}, f32[160,128]{1,0:T(8,128)S(1)}, u32[]{:S(2)}, u32[]{:S(2)}) collective-permute-start(f32[160,128]{1,0:T(8,128)S(1)} %get-tuple-element.35), channel_id=1, source_target_pairs={{0,1},{1,0},{2,3},{3,2},{4,5},{5,4},{6,7},{7,6},{8,9},{9,8},{10,11... | collective-permute-start | bytes 245768 | tf_op jit(solution)/shard_map/ppermute | solution.py:78
  4.5 1.4 %collective-permute-start.3 = (f32[160,128]{1,0:T(8,128)S(1)}, f32[160,128]{1,0:T(8,128)S(1)}, u32[]{:S(2)}, u32[]{:S(2)}) collective-permute-start(f32[160,128]{1,0:T(8,128)S(1)} %get-tuple-element.36), channel_id=1, source_target_pairs={{0,8},{1,2},{2,1},{3,4},{4,3},{5,6},{6,5},{7,15},{8,0},{9,10},{10,... | collective-permute-start | bytes 245768 | tf_op jit(solution)/shard_map/ppermute | solution.py:78
  5.9 0.4 %collective-permute-done.1.odd.refs_8_ = f32[160,128]{1,0:T(8,128)S(1)} collective-permute-done((f32[160,128]{1,0:T(8,128)S(1)}, f32[160,128]{1,0:T(8,128)S(1)}, u32[]{:S(2)}, u32[]{:S(2)}) %collective-permute-start.1) | collective-permute-done | bytes 81952 | tf_op jit(solution)/shard_map/ppermute | solution.py:78
  6.6 1.4 %collective-permute-start.4 = (f32[16,128]{1,0:T(8,128)S(1)}, f32[16,128]{1,0:T(8,128)S(1)}, u32[]{:S(2)}, u32[]{:S(2)}) collective-permute-start(f32[16,128]{1,0:T(8,128)S(1)} %get-tuple-element.37), channel_id=1, source_target_pairs={{0,8},{1,2},{2,1},{3,4},{4,3},{5,6},{6,5},{7,15},{8,0},{9,10},{10,... | collective-permute-start | bytes 24584 | tf_op jit(solution)/shard_map/ppermute | solution.py:78
  8.0 1.6 %collective-permute-start.5 = (f32[16,128]{1,0:T(8,128)S(1)}, f32[16,128]{1,0:T(8,128)S(1)}, u32[]{:S(2)}, u32[]{:S(2)}) collective-permute-start(f32[16,128]{1,0:T(8,128)S(1)} %get-tuple-element.38), channel_id=1, source_target_pairs={{0,1},{1,0},{2,3},{3,2},{4,5},{5,4},{6,7},{7,6},{8,9},{9,8},{10,11... | collective-permute-start | bytes 24584 | tf_op jit(solution)/shard_map/ppermute | solution.py:78
  9.6 0.5 %shard_map.116 = f32[128,128]{1,0:T(8,128)S(1)} custom-call(f32[3,272,128]{2,1,0:T(8,128)S(1)} %get-tuple-element.30.h, f32[3,272,128]{2,1,0:T(8,128)S(1)} %get-tuple-element.31.e, f32[272,128]{1,0:T(8,128)S(1)} %get-tuple-element.32.c_ref, f32[3,256,128]{2,1,0:T(8,128)S(1)} %get-tuple-element.33.t, f32[256,128]{1,0:T(8,128)S(1)} %bitcast.16, ...), custom_call_target="tpu_custom_call" | custom-call | flops 3276800 | bytes 2351104 | tf_op jit(solution)/shard_map/pallas_call | solution.py:127
  10.7 0.4 %collective-permute-done.4.odd_late = f32[16,128]{1,0:T(8,128)S(1)} collective-permute-done((f32[16,128]{1,0:T(8,128)S(1)}, f32[16,128]{1,0:T(8,128)S(1)}, u32[]{:S(2)}, u32[]{:S(2)}) %collective-permute-start.4) | collective-permute-done | bytes 8224 | tf_op jit(solution)/shard_map/ppermute | solution.py:78
  11.1 0.5 %collective-permute-done.5.even_late = f32[16,128]{1,0:T(8,128)S(1)} collective-permute-done((f32[16,128]{1,0:T(8,128)S(1)}, f32[16,128]{1,0:T(8,128)S(1)}, u32[]{:S(2)}, u32[]{:S(2)}) %collective-permute-start.5) | collective-permute-done | bytes 8224 | tf_op jit(solution)/shard_map/ppermute | solution.py:78
  11.7 0.6 %shard_map.115 = (f32[3,256,128]{2,1,0:T(8,128)S(1)}, f32[3,256,128]{2,1,0:T(8,128)S(1)}, f32[256,128]{1,0:T(8,128)S(1)}, f32[128,128]{1,0:T(8,128)S(1)}, f32[24,128]{1,0:T(8,128)S(1)}) custom-call(f32[3,272,128]{2,1,0:T(8,128)S(1)} %get-tuple-element.30.h, f32[3,272,128]{2,1,0:T(8,128)S(1)} %get-tuple-element.31.e, f32[272,128]{1,0:T(8,128)S(1)} %get-tuple-element.32.c_ref, ...), custom_call_target="tpu_custom_call" | custom-call | flops 4915200 | bytes 3510272 | tf_op jit(solution)/shard_map/pallas_call | solution.py:127
  12.3 0.4 %collective-permute-start.7 = (f32[128,128]{1,0:T(8,128)S(1)}, f32[128,128]{1,0:T(8,128)S(1)}, u32[]{:S(2)}, u32[]{:S(2)}) collective-permute-start(f32[128,128]{1,0:T(8,128)S(1)} %get-tuple-element.42), channel_id=1, source_target_pairs={{0,24},{1,25},{2,26},{3,27},{4,28},{5,29},{6,30},{7,31},{8,16},{9,... | collective-permute-start | bytes 196616 | tf_op jit(solution)/shard_map/ppermute | solution.py:78
  12.7 1.0 %collective-permute-start.8 = (f32[24,128]{1,0:T(8,128)S(1)}, f32[24,128]{1,0:T(8,128)S(1)}, u32[]{:S(2)}, u32[]{:S(2)}) collective-permute-start(f32[24,128]{1,0:T(8,128)S(1)} %get-tuple-element.43), channel_id=1, source_target_pairs={{0,16},{1,17},{2,18},{3,19},{4,20},{5,21},{6,22},{7,23},{8,24},{9,... | collective-permute-start | bytes 36872 | tf_op jit(solution)/shard_map/ppermute | solution.py:78
  13.8 0.5 %collective-permute-start.9 = (f32[24,128]{1,0:T(8,128)S(1)}, f32[24,128]{1,0:T(8,128)S(1)}, u32[]{:S(2)}, u32[]{:S(2)}) collective-permute-start(f32[24,128]{1,0:T(8,128)S(1)} %get-tuple-element.43), channel_id=1, source_target_pairs={{0,8},{1,9},{2,10},{3,11},{4,12},{5,13},{6,14},{7,15},{8,0},{9,1},... | collective-permute-start | bytes 36872 | tf_op jit(solution)/shard_map/ppermute | solution.py:78
  14.2 2.5 %collective-permute-done.8.refs_3_ = f32[24,128]{1,0:T(8,128)S(1)} collective-permute-done((f32[24,128]{1,0:T(8,128)S(1)}, f32[24,128]{1,0:T(8,128)S(1)}, u32[]{:S(2)}, u32[]{:S(2)}) %collective-permute-start.8) | collective-permute-done | bytes 12320 | tf_op jit(solution)/shard_map/ppermute | solution.py:78
  16.9 1.3 %collective-permute-start.10 = (f32[120,128]{1,0:T(8,128)S(1)}, f32[120,128]{1,0:T(8,128)S(1)}, u32[]{:S(2)}, u32[]{:S(2)}) collective-permute-start(f32[120,128]{1,0:T(8,128)S(1)} %get-tuple-element.45), channel_id=1, source_target_pairs={{0,1},{1,0},{2,3},{3,2},{4,5},{5,4},{6,7},{7,6},{8,9},{9,8},{10,11... | collective-permute-start | bytes 184328 | tf_op jit(solution)/shard_map/ppermute | solution.py:78
  18.2 0.6 %collective-permute-start.11 = (f32[120,128]{1,0:T(8,128)S(1)}, f32[120,128]{1,0:T(8,128)S(1)}, u32[]{:S(2)}, u32[]{:S(2)}) collective-permute-start(f32[120,128]{1,0:T(8,128)S(1)} %get-tuple-element.46), channel_id=1, source_target_pairs={{0,8},{1,2},{2,1},{3,4},{4,3},{5,6},{6,5},{7,15},{8,0},{9,10},{10,... | collective-permute-start | bytes 184328 | tf_op jit(solution)/shard_map/ppermute | solution.py:78
  19.1 0.4 %shard_map.118.inverse = f32[256,128]{1,0:T(8,128)S(1)} custom-call(f32[256,128]{1,0:T(8,128)S(1)} %broadcast_in_dim.16.radius), custom_call_target="tpu_custom_call" | custom-call | flops 3276800 | bytes 262144 | tf_op jit(solution)/shard_map/pallas_call | solution.py:127
  19.5 0.7 %copy.19 = f32[3,32,8,128]{3,2,1,0:T(8,128)} copy(f32[3,32,8,128]{3,2,1,0:T(8,128)S(1)} %bitcast.12) | data formatting | bytes 786432
  20.2 0.7 %copy.20 = f32[3,32,8,128]{3,2,1,0:T(8,128)} copy(f32[3,32,8,128]{3,2,1,0:T(8,128)S(1)} %bitcast.11) | data formatting | bytes 786432
  21.2 2.2 %collective-permute-done.11.odd = f32[120,128]{1,0:T(8,128)S(1)} collective-permute-done((f32[120,128]{1,0:T(8,128)S(1)}, f32[120,128]{1,0:T(8,128)S(1)}, u32[]{:S(2)}, u32[]{:S(2)}) %collective-permute-start.11) | collective-permute-done | bytes 61472 | tf_op jit(solution)/shard_map/ppermute | solution.py:78
  23.4 0.4 %shard_map.119 = f32[256,128]{1,0:T(8,128)S(1)} custom-call(f32[304,128]{1,0:T(8,128)S(1)} %get-tuple-element.44.u, f32[120,128]{1,0:T(8,128)S(1)} %collective-permute-done.10.even, f32[120,128]{1,0:T(8,128)S(1)} %collective-permute-done.11.odd, f32[256,128]{1,0:T(8,128)S(1)} %broadcast_in_dim.16.radius, f32[256,128]{1,0:T(8,128)S(1)} %shard_map.118.inverse), custom_call_target="tpu_custom_call" | custom-call | bytes 671744 | tf_op jit(solution)/shard_map/pallas_call | solution.py:127
  23.8 0.7 %copy.21 = f32[32,8,128]{2,1,0:T(8,128)} copy(f32[32,8,128]{2,1,0:T(8,128)S(1)} %bitcast.10) | data formatting | bytes 262144
  (34 shorter events, 1.5 us)
Async XLA Ops:
  0.6 2.8 %copy-start = (f32[32,8,128]{2,1,0:T(8,128)S(1)}, f32[32,8,128]{2,1,0:T(8,128)}, u32[]{:S(2)}) copy-start(f32[32,8,128]{2,1,0:T(8,128)} %param.13) | copy-start | bytes 393220
  0.6 2.8 %copy-start.1 = (f32[3,32,8,128]{3,2,1,0:T(8,128)S(1)}, f32[3,32,8,128]{3,2,1,0:T(8,128)}, u32[]{:S(2)}) copy-start(f32[3,32,8,128]{3,2,1,0:T(8,128)} %param.9) | copy-start | bytes 1179652
  0.7 2.8 %copy-start.2 = (f32[3,32,8,128]{3,2,1,0:T(8,128)S(1)}, f32[3,32,8,128]{3,2,1,0:T(8,128)}, u32[]{:S(2)}) copy-start(f32[3,32,8,128]{3,2,1,0:T(8,128)} %param.10) | copy-start | bytes 1179652
  0.7 2.8 %copy-start.3 = (f32[3,32,8,128]{3,2,1,0:T(8,128)S(1)}, f32[3,32,8,128]{3,2,1,0:T(8,128)}, u32[]{:S(2)}) copy-start(f32[3,32,8,128]{3,2,1,0:T(8,128)} %param.11) | copy-start | bytes 1179652
  0.7 2.8 %copy-start.4 = (f32[3,32,8,128]{3,2,1,0:T(8,128)S(1)}, f32[3,32,8,128]{3,2,1,0:T(8,128)}, u32[]{:S(2)}) copy-start(f32[3,32,8,128]{3,2,1,0:T(8,128)} %param.12) | copy-start | bytes 1179652
  1.8 4.2 %collective-permute-start = (f32[160,128]{1,0:T(8,128)S(1)}, f32[160,128]{1,0:T(8,128)S(1)}, u32[]{:S(2)}, u32[]{:S(2)}) collective-permute-start(f32[160,128]{1,0:T(8,128)S(1)} %get-tuple-element.25), channel_id=1, source_target_pairs={{0,8},{1,9},{2,10},{3,11},{4,12},{5,13},{6,14},{7,15},{8,0},{9,1},... | collective-permute-start | bytes 245768 | tf_op jit(solution)/shard_map/ppermute | solution.py:78
  1.8 4.5 %collective-permute-start.1 = (f32[160,128]{1,0:T(8,128)S(1)}, f32[160,128]{1,0:T(8,128)S(1)}, u32[]{:S(2)}, u32[]{:S(2)}) collective-permute-start(f32[160,128]{1,0:T(8,128)S(1)} %get-tuple-element.26), channel_id=1, source_target_pairs={{0,1},{1,0},{2,3},{3,2},{4,5},{5,4},{6,7},{7,6},{8,16},{9,17},{10,... | collective-permute-start | bytes 245768 | tf_op jit(solution)/shard_map/ppermute | solution.py:78
  4.0 6.4 %collective-permute-start.2 = (f32[160,128]{1,0:T(8,128)S(1)}, f32[160,128]{1,0:T(8,128)S(1)}, u32[]{:S(2)}, u32[]{:S(2)}) collective-permute-start(f32[160,128]{1,0:T(8,128)S(1)} %get-tuple-element.35), channel_id=1, source_target_pairs={{0,1},{1,0},{2,3},{3,2},{4,5},{5,4},{6,7},{7,6},{8,9},{9,8},{10,11... | collective-permute-start | bytes 245768 | tf_op jit(solution)/shard_map/ppermute | solution.py:78
  4.5 6.2 %collective-permute-start.3 = (f32[160,128]{1,0:T(8,128)S(1)}, f32[160,128]{1,0:T(8,128)S(1)}, u32[]{:S(2)}, u32[]{:S(2)}) collective-permute-start(f32[160,128]{1,0:T(8,128)S(1)} %get-tuple-element.36), channel_id=1, source_target_pairs={{0,8},{1,2},{2,1},{3,4},{4,3},{5,6},{6,5},{7,15},{8,0},{9,10},{10,... | collective-permute-start | bytes 245768 | tf_op jit(solution)/shard_map/ppermute | solution.py:78
  6.3 3.3 %copy-start.5 = (f32[2,3,32,8,128]{4,3,2,1,0:T(8,128)S(1)}, f32[2,3,32,8,128]{4,3,2,1,0:T(8,128)}, u32[]{:S(2)}) copy-start(f32[2,3,32,8,128]{4,3,2,1,0:T(8,128)} %param.14) | copy-start | bytes 2359300
  6.6 4.6 %collective-permute-start.4 = (f32[16,128]{1,0:T(8,128)S(1)}, f32[16,128]{1,0:T(8,128)S(1)}, u32[]{:S(2)}, u32[]{:S(2)}) collective-permute-start(f32[16,128]{1,0:T(8,128)S(1)} %get-tuple-element.37), channel_id=1, source_target_pairs={{0,8},{1,2},{2,1},{3,4},{4,3},{5,6},{6,5},{7,15},{8,0},{9,10},{10,... | collective-permute-start | bytes 24584 | tf_op jit(solution)/shard_map/ppermute | solution.py:78
  8.0 3.7 %collective-permute-start.5 = (f32[16,128]{1,0:T(8,128)S(1)}, f32[16,128]{1,0:T(8,128)S(1)}, u32[]{:S(2)}, u32[]{:S(2)}) collective-permute-start(f32[16,128]{1,0:T(8,128)S(1)} %get-tuple-element.38), channel_id=1, source_target_pairs={{0,1},{1,0},{2,3},{3,2},{4,5},{5,4},{6,7},{7,6},{8,9},{9,8},{10,11... | collective-permute-start | bytes 24584 | tf_op jit(solution)/shard_map/ppermute | solution.py:78
  10.2 6.5 %collective-permute-start.6 = (f32[128,128]{1,0:T(8,128)S(1)}, f32[128,128]{1,0:T(8,128)S(1)}, u32[]{:S(2)}, u32[]{:S(2)}) collective-permute-start(f32[128,128]{1,0:T(8,128)S(1)} %shard_map.116), channel_id=1, source_target_pairs={{0,24},{1,25},{2,26},{3,27},{4,28},{5,29},{6,30},{7,31},{8,16},{9,... | collective-permute-start | bytes 196616 | tf_op jit(solution)/shard_map/ppermute | solution.py:78
  11.6 5.2 %copy-start.6 = (s32[32,8,128]{2,1,0:T(8,128)S(1)}, s32[32,8,128]{2,1,0:T(8,128)}, u32[]{:S(2)}) copy-start(s32[32,8,128]{2,1,0:T(8,128)} %param.15) | copy-start | bytes 393220
  12.3 4.4 %collective-permute-start.7 = (f32[128,128]{1,0:T(8,128)S(1)}, f32[128,128]{1,0:T(8,128)S(1)}, u32[]{:S(2)}, u32[]{:S(2)}) collective-permute-start(f32[128,128]{1,0:T(8,128)S(1)} %get-tuple-element.42), channel_id=1, source_target_pairs={{0,24},{1,25},{2,26},{3,27},{4,28},{5,29},{6,30},{7,31},{8,16},{9,... | collective-permute-start | bytes 196616 | tf_op jit(solution)/shard_map/ppermute | solution.py:78
  12.7 4.0 %copy-start.8 = (s32[8]{0:T(128)S(1)}, s32[8]{0:T(128)}, u32[]{:S(2)}) copy-start(s32[8]{0:T(128)} %param.16) | copy-start | bytes 100
  12.7 4.0 %collective-permute-start.8 = (f32[24,128]{1,0:T(8,128)S(1)}, f32[24,128]{1,0:T(8,128)S(1)}, u32[]{:S(2)}, u32[]{:S(2)}) collective-permute-start(f32[24,128]{1,0:T(8,128)S(1)} %get-tuple-element.43), channel_id=1, source_target_pairs={{0,16},{1,17},{2,18},{3,19},{4,20},{5,21},{6,22},{7,23},{8,24},{9,... | collective-permute-start | bytes 36872 | tf_op jit(solution)/shard_map/ppermute | solution.py:78
  13.8 3.0 %collective-permute-start.9 = (f32[24,128]{1,0:T(8,128)S(1)}, f32[24,128]{1,0:T(8,128)S(1)}, u32[]{:S(2)}, u32[]{:S(2)}) collective-permute-start(f32[24,128]{1,0:T(8,128)S(1)} %get-tuple-element.43), channel_id=1, source_target_pairs={{0,8},{1,9},{2,10},{3,11},{4,12},{5,13},{6,14},{7,15},{8,0},{9,1},... | collective-permute-start | bytes 36872 | tf_op jit(solution)/shard_map/ppermute | solution.py:78
  16.8 2.0 %copy-start.7 = (s32[32,8]{0,1:T(8,128)S(1)}, s32[32,8]{0,1:T(8,128)}, u32[]{:S(2)}) copy-start(s32[32,8]{0,1:T(8,128)} %param.17) | copy-start | bytes 3076
  16.9 4.3 %collective-permute-start.10 = (f32[120,128]{1,0:T(8,128)S(1)}, f32[120,128]{1,0:T(8,128)S(1)}, u32[]{:S(2)}, u32[]{:S(2)}) collective-permute-start(f32[120,128]{1,0:T(8,128)S(1)} %get-tuple-element.45), channel_id=1, source_target_pairs={{0,1},{1,0},{2,3},{3,2},{4,5},{5,4},{6,7},{7,6},{8,9},{9,8},{10,11... | collective-permute-start | bytes 184328 | tf_op jit(solution)/shard_map/ppermute | solution.py:78
  18.2 5.1 %collective-permute-start.11 = (f32[120,128]{1,0:T(8,128)S(1)}, f32[120,128]{1,0:T(8,128)S(1)}, u32[]{:S(2)}, u32[]{:S(2)}) collective-permute-start(f32[120,128]{1,0:T(8,128)S(1)} %get-tuple-element.46), channel_id=1, source_target_pairs={{0,8},{1,2},{2,1},{3,4},{4,3},{5,6},{6,5},{7,15},{8,0},{9,10},{10,... | collective-permute-start | bytes 184328 | tf_op jit(solution)/shard_map/ppermute | solution.py:78

commit v5 on v4

--- a/solution.py
+++ b/solution.py
@@ -393,22 +393,28 @@
         out[(j - REACH) * n : (j - REACH + 1) * n, :] = g[pl.ds(j, n, stride=r), :]
 
 
-def step_last(
-    n, r, block, h, e, c_ref, t, d, rows, even, odd, odd_late, even_late, f, e_out, h_out, g_out, rim_out, edge_out, face, fix
-):
+def step_last(n, r, late, h, e, c_ref, t, d, rows, even, odd, *refs):
+    if late:
+        odd_late, even_late, f, _, _, _, e_out, h_out, g_out, rim_out, edge_out, face, fix = refs
+    else:
+        f, e_out, h_out, g_out, face, fix = refs
     flip = odd_y()
     below, above, low, high = edges()
     hxm, hzm, dx, dz, ry, exp_, ezp, hxm2, hzm2, wm = range(10)
     last = r - 1
-    upward, downward = late_rows(n)
+    apart = jnp.zeros((BASE, h.shape[-1]), jnp.float32)
     for k in range(5):
         at = slice(k * n, (k + 1) * n)
+        for side in range(2):
+            face[side, k, :BASE, :] = apart
+            face[side, k, BASE + n :, :] = apart
         face[0, k, BASE : BASE + n, :] = jnp.where(flip, even[at, :], odd[at, :])
         face[1, k, BASE : BASE + n, :] = jnp.where(flip, odd[at, :], even[at, :])
-    for k, ((field_u, x_u), (field_v, x_v)) in enumerate(zip(upward, downward)):
-        at = slice(k, k + 1)
-        face[0, field_u, BASE + x_u : BASE + x_u + 1, :] = jnp.where(flip, even_late[at, :], odd_late[at, :])
-        face[1, field_v, BASE + x_v : BASE + x_v + 1, :] = jnp.where(flip, odd_late[at, :], even_late[at, :])
+    if late:
+        for k, ((field_u, x_u), (field_v, x_v)) in enumerate(zip(*late_rows(n))):
+            at = slice(k, k + 1)
+            face[0, field_u, BASE + x_u : BASE + x_u + 1, :] = jnp.where(flip, even_late[at, :], odd_late[at, :])
+            face[1, field_v, BASE + x_v : BASE + x_v + 1, :] = jnp.where(flip, odd_late[at, :], even_late[at, :])
 
     def up(k, x=0, size=n):
         return keep(low, face[0, k, BASE + x : BASE + x + size, :])
@@ -503,15 +509,21 @@
         g_out[at, :] = total
         return mine, next_magnetic, ahead
 
-    def body(i, carry):
-        for k in range(block):
-            carry = one(i * block + k, carry)
-        return carry
-
-    magnetic, now = after_one(-1)
-    next_magnetic, ahead = after_one(0)
-    start = tuple(keep(below, v) for v in second_h(-1, magnetic, now, ahead))
-    lax.fori_loop(0, n // block, body, (start, next_magnetic, ahead))
+    def run(first, end):
+        magnetic, now = after_one(first - 1)
+        next_magnetic, ahead = after_one(first)
+        last_h = second_h(first - 1, magnetic, now, ahead)
+        if first == 0:
+            last_h = tuple(keep(below, v) for v in last_h)
+        carry = (last_h, next_magnetic, ahead)
+        for x in range(first, end):
+            carry = one(x, carry)
+
+    if not late:
+        run(REACH, n - REACH)
+        return
+    run(0, REACH)
+    run(n - REACH, n)
     for k, j in enumerate(rim_rows(r)):
         rim_out[k * n : (k + 1) * n, :] = g_out[pl.ds(j, n, stride=r), :]
     first = jnp.where(odd_x(), 0, n - WIDTH)
@@ -725,7 +737,7 @@
     even = send(even, x_even)
     odd = send(odd, x_odd)
 
-    inner = functools.partial(step_inner, n, r, 16)
+    inner = functools.partial(step_inner, n, r, 32)
     h1, e1, c1, t1, even_y, odd_y_ = call(
         inner,
         [(3, more, depth)] * 2 + [(more, depth), (3, size, depth)] + [face_y] * 2,
@@ -744,7 +756,7 @@
     odd_late = send(odd_late, y_odd)
     even_late = send(even_late, y_even)
     (mid,) = call(
-        functools.partial(step_mid, n, r, 16),
+        functools.partial(step_mid, n, r, 32),
         [((r - 2 * REACH) * n, depth)],
         [h1, e1, c1, t1, d, f],
         flops=100 * size * depth,
@@ -756,12 +768,16 @@
     order = jnp.broadcast_to(partner_rows[:, None], (r, depth))
     (inverse,) = call(functools.partial(cover, n, r, 16), [(size, depth)], [radius], flops=100 * size * depth)
 
+    known = [h1, e1, c1, t1, d, rows, even_y, odd_y_]
+    fields = [(3, size, depth)] * 2 + [(size, depth)]
+    lists = [VMEM((2, 5, lines, depth), f32), VMEM((10, lines, depth), f32)]
+    e2, h2, g = call(functools.partial(step_last, n, r, False), fields, known + [f], flops=150 * size * depth, scratch=lists)
     e2, h2, g, rim, edge = call(
-        functools.partial(step_last, n, r, 16),
-        [(3, size, depth)] * 2 + [(size, depth), (2 * REACH * n, depth), (WIDTH * r, depth)],
-        [h1, e1, c1, t1, d, rows, even_y, odd_y_, odd_late, even_late, f],
-        flops=150 * size * depth,
-        scratch=[VMEM((2, 5, lines, depth), jnp.float32), VMEM((10, lines, depth), jnp.float32)],
+        functools.partial(step_last, n, r, True),
+        fields + [(2 * REACH * n, depth), (WIDTH * r, depth)],
+        known + [odd_late, even_late, f, e2, h2, g],
+        aliases={11: 0, 12: 1, 13: 2},
+        scratch=lists,
     )
     rim = send(rim, mirror)
     edge_m = send(edge, mirror_even)
@@ -783,7 +799,7 @@
     odd_u = send(odd_u, y_odd)
     even_u = send(even_u, y_even)
     (out,) = call(
-        functools.partial(smooth, n, r, 16),
+        functools.partial(smooth, n, r, 32),
         [(size, depth)],
         [u, even_u, odd_u, radius, inverse],
         scratch=[VMEM((wide * r, depth), jnp.float32), VMEM((WIDTH, full * r, depth), jnp.float32)],

time: 24.7 us -> 24.2 us (0.980)
    pallas_call x7 -> x8, Pallas kernels: 2.81 us -> 2.71 us  [call(): pl.pallas_call(kernel, out_shape=tuple((VMEM(s, jnp.float32) for s in out...]
  transfers between devices with their start and end apart: 12 -> 12, of which waited for: 7 -> 6; matrix products, arithmetic and copies ran while one was open for 7% -> 7% of each run, Pallas kernels for 10% -> 9%
where the time goes in v5:
time: 24.2 us; the launch traced here: 24 us
  starting transfers between devices  10.5 us (43%)
  waiting for transfers between devices  6.41 us (26%)
  Pallas kernels  3.77 us (16%)
  local copies, waits for them, and re-layouts  2.52 us (10%)
  between operations  0.77 us (3%)
    ppermute x12, starting transfers between devices, send(): return lax.ppermute(block, AXES, route)  10.5 us
    ppermute x12, waiting for transfers between devices, send(): return lax.ppermute(block, AXES, route)  6.41 us
    pallas_call x8, Pallas kernels, call(): pl.pallas_call(kernel, out_shape=tuple((VMEM(s, jnp.float32) for s in out...  2.71 us
    unnamed x21, local copies, waits for them, and re-layouts  2.19 us
    pallas_call x1, Pallas kernels, local(): pl.pallas_call(functools.partial(pack_x, n, r), out_shape=(VMEM(face_x, f...  1.06 us
  transfers between devices with their start and end apart: 12, of which 6 were waited for; matrix products, arithmetic and copies ran while one was open for 7% of the time, Pallas kernels for 9%

profile of v5, /device:TPU:8, one launch (start us, length us, event | category | flops | bytes accessed | tf_op | source)
XLA Modules:
  0.0 24.0 jit_solution(10993642444337884881)
XLA Ops:
  0.7 1.1 %shard_map.112 = (f32[160,128]{1,0:T(8,128)S(1)}, f32[160,128]{1,0:T(8,128)S(1)}) custom-call(f32[3,256,128]{2,1,0:T(8,128)} %bitcast.23, f32[3,256,128]{2,1,0:T(8,128)} %bitcast.26, f32[3,256,128]{2,1,0:T(8,128)} %bitcast.29, f32[3,256,128]{2,1,0:T(8,128)} %bitcast.32, f32[256,128]{1,0:T(8,128)} %bitcast.16, s32[256,128]{1,0:T(8,128)} %bitcast.35), custom_call_target="tpu_custom_call" | custom-call | tf_op jit(solution)/shard_map/pallas_call | solution.py:722
  1.8 1.6 %collective-permute-start.1 = (f32[160,128]{1,0:T(8,128)S(1)}, f32[160,128]{1,0:T(8,128)S(1)}, u32[]{:S(2)}, u32[]{:S(2)}) collective-permute-start(f32[160,128]{1,0:T(8,128)S(1)} %get-tuple-element.29), channel_id=1, source_target_pairs={{0,1},{1,0},{2,3},{3,2},{4,5},{5,4},{6,7},{7,6},{8,16},{9,17},{10,... | collective-permute-start | bytes 245768 | tf_op jit(solution)/shard_map/ppermute | solution.py:78
  3.4 0.4 %shard_map.113 = (f32[3,272,128]{2,1,0:T(8,128)S(1)}, f32[3,272,128]{2,1,0:T(8,128)S(1)}, f32[272,128]{1,0:T(8,128)S(1)}, f32[3,256,128]{2,1,0:T(8,128)S(1)}, f3...) custom-call(f32[3,256,128]{2,1,0:T(8,128)S(1)} %bitcast.24, f32[3,256,128]{2,1,0:T(8,128)S(1)} %bitcast.27, ...), custom_call_target="tpu_custom_call" | custom-call | flops 3276800 | bytes 3235840 | tf_op jit(solution)/shard_map/pallas_call | solution.py:127
  3.9 0.6 %collective-permute-start.2 = (f32[160,128]{1,0:T(8,128)S(1)}, f32[160,128]{1,0:T(8,128)S(1)}, u32[]{:S(2)}, u32[]{:S(2)}) collective-permute-start(f32[160,128]{1,0:T(8,128)S(1)} %get-tuple-element.38), channel_id=1, source_target_pairs={{0,1},{1,0},{2,3},{3,2},{4,5},{5,4},{6,7},{7,6},{8,9},{9,8},{10,11... | collective-permute-start | bytes 245768 | tf_op jit(solution)/shard_map/ppermute | solution.py:78
  4.4 1.4 %collective-permute-start.3 = (f32[160,128]{1,0:T(8,128)S(1)}, f32[160,128]{1,0:T(8,128)S(1)}, u32[]{:S(2)}, u32[]{:S(2)}) collective-permute-start(f32[160,128]{1,0:T(8,128)S(1)} %get-tuple-element.39), channel_id=1, source_target_pairs={{0,8},{1,2},{2,1},{3,4},{4,3},{5,6},{6,5},{7,15},{8,0},{9,10},{10,... | collective-permute-start | bytes 245768 | tf_op jit(solution)/shard_map/ppermute | solution.py:78
  5.9 0.5 %collective-permute-done.1.odd.refs_8_ = f32[160,128]{1,0:T(8,128)S(1)} collective-permute-done((f32[160,128]{1,0:T(8,128)S(1)}, f32[160,128]{1,0:T(8,128)S(1)}, u32[]{:S(2)}, u32[]{:S(2)}) %collective-permute-start.1) | collective-permute-done | bytes 81952 | tf_op jit(solution)/shard_map/ppermute | solution.py:78
  6.6 1.4 %collective-permute-start.4 = (f32[16,128]{1,0:T(8,128)S(1)}, f32[16,128]{1,0:T(8,128)S(1)}, u32[]{:S(2)}, u32[]{:S(2)}) collective-permute-start(f32[16,128]{1,0:T(8,128)S(1)} %get-tuple-element.40), channel_id=1, source_target_pairs={{0,8},{1,2},{2,1},{3,4},{4,3},{5,6},{6,5},{7,15},{8,0},{9,10},{10,... | collective-permute-start | bytes 24584 | tf_op jit(solution)/shard_map/ppermute | solution.py:78
  8.0 1.6 %collective-permute-start.5 = (f32[16,128]{1,0:T(8,128)S(1)}, f32[16,128]{1,0:T(8,128)S(1)}, u32[]{:S(2)}, u32[]{:S(2)}) collective-permute-start(f32[16,128]{1,0:T(8,128)S(1)} %get-tuple-element.41), channel_id=1, source_target_pairs={{0,1},{1,0},{2,3},{3,2},{4,5},{5,4},{6,7},{7,6},{8,9},{9,8},{10,11... | collective-permute-start | bytes 24584 | tf_op jit(solution)/shard_map/ppermute | solution.py:78
  9.6 0.4 %shard_map.117 = f32[128,128]{1,0:T(8,128)S(1)} custom-call(f32[3,272,128]{2,1,0:T(8,128)S(1)} %get-tuple-element.33.h, f32[3,272,128]{2,1,0:T(8,128)S(1)} %get-tuple-element.34.e, f32[272,128]{1,0:T(8,128)S(1)} %get-tuple-element.35.c_ref, f32[3,256,128]{2,1,0:T(8,128)S(1)} %get-tuple-element.36.t, f32[256,128]{1,0:T(8,128)S(1)} %bitcast.19, ...), custom_call_target="tpu_custom_call" | custom-call | flops 3276800 | bytes 2351104 | tf_op jit(solution)/shard_map/pallas_call | solution.py:127
  10.2 0.4 %collective-permute-done.3.odd = f32[160,128]{1,0:T(8,128)S(1)} collective-permute-done((f32[160,128]{1,0:T(8,128)S(1)}, f32[160,128]{1,0:T(8,128)S(1)}, u32[]{:S(2)}, u32[]{:S(2)}) %collective-permute-start.3) | collective-permute-done | bytes 81952 | tf_op jit(solution)/shard_map/ppermute | solution.py:78
  10.6 0.5 %shard_map.115 = (f32[3,256,128]{2,1,0:T(8,128)S(1)}, f32[3,256,128]{2,1,0:T(8,128)S(1)}, f32[256,128]{1,0:T(8,128)S(1)}) custom-call(f32[3,272,128]{2,1,0:T(8,128)S(1)} %get-tuple-element.33.h, f32[3,272,128]{2,1,0:T(8,128)S(1)} %get-tuple-element.34.e, f32[272,128]{1,0:T(8,128)S(1)} %get-tuple-element.35.c_ref, f32[3,256,128]{2,1,0:T(8,128)S(1)} %get-tuple-element.36.t, ...), custom_call_target="tpu_custom_call" | custom-call | flops 4915200 | bytes 3416064 | tf_op jit(solution)/shard_map/pallas_call | solution.py:127
  11.1 0.5 %collective-permute-done.5.refs_1_ = f32[16,128]{1,0:T(8,128)S(1)} collective-permute-done((f32[16,128]{1,0:T(8,128)S(1)}, f32[16,128]{1,0:T(8,128)S(1)}, u32[]{:S(2)}, u32[]{:S(2)}) %collective-permute-start.5) | collective-permute-done | bytes 8224 | tf_op jit(solution)/shard_map/ppermute | solution.py:78
  11.9 0.8 %collective-permute-start.7 = (f32[128,128]{1,0:T(8,128)S(1)}, f32[128,128]{1,0:T(8,128)S(1)}, u32[]{:S(2)}, u32[]{:S(2)}) collective-permute-start(f32[128,128]{1,0:T(8,128)S(1)} %get-tuple-element.48), channel_id=1, source_target_pairs={{0,24},{1,25},{2,26},{3,27},{4,28},{5,29},{6,30},{7,31},{8,16},{9,... | collective-permute-start | bytes 196616 | tf_op jit(solution)/shard_map/ppermute | solution.py:78
  12.8 0.9 %collective-permute-start.8 = (f32[24,128]{1,0:T(8,128)S(1)}, f32[24,128]{1,0:T(8,128)S(1)}, u32[]{:S(2)}, u32[]{:S(2)}) collective-permute-start(f32[24,128]{1,0:T(8,128)S(1)} %get-tuple-element.49), channel_id=1, source_target_pairs={{0,16},{1,17},{2,18},{3,19},{4,20},{5,21},{6,22},{7,23},{8,24},{9,... | collective-permute-start | bytes 36872 | tf_op jit(solution)/shard_map/ppermute | solution.py:78
  13.8 2.8 %collective-permute-done.8.refs_3_ = f32[24,128]{1,0:T(8,128)S(1)} collective-permute-done((f32[24,128]{1,0:T(8,128)S(1)}, f32[24,128]{1,0:T(8,128)S(1)}, u32[]{:S(2)}, u32[]{:S(2)}) %collective-permute-start.8) | collective-permute-done | bytes 12320 | tf_op jit(solution)/shard_map/ppermute | solution.py:78
  16.8 1.0 %collective-permute-start.10 = (f32[120,128]{1,0:T(8,128)S(1)}, f32[120,128]{1,0:T(8,128)S(1)}, u32[]{:S(2)}, u32[]{:S(2)}) collective-permute-start(f32[120,128]{1,0:T(8,128)S(1)} %get-tuple-element.51), channel_id=1, source_target_pairs={{0,1},{1,0},{2,3},{3,2},{4,5},{5,4},{6,7},{7,6},{8,9},{9,8},{10,11... | collective-permute-start | bytes 184328 | tf_op jit(solution)/shard_map/ppermute | solution.py:78
  17.9 0.8 %collective-permute-start.11 = (f32[120,128]{1,0:T(8,128)S(1)}, f32[120,128]{1,0:T(8,128)S(1)}, u32[]{:S(2)}, u32[]{:S(2)}) collective-permute-start(f32[120,128]{1,0:T(8,128)S(1)} %get-tuple-element.52), channel_id=1, source_target_pairs={{0,8},{1,2},{2,1},{3,4},{4,3},{5,6},{6,5},{7,15},{8,0},{9,10},{10,... | collective-permute-start | bytes 184328 | tf_op jit(solution)/shard_map/ppermute | solution.py:78
  18.9 0.4 %shard_map.119.inverse = f32[256,128]{1,0:T(8,128)S(1)} custom-call(f32[256,128]{1,0:T(8,128)S(1)} %broadcast_in_dim.16.radius), custom_call_target="tpu_custom_call" | custom-call | flops 3276800 | bytes 262144 | tf_op jit(solution)/shard_map/pallas_call | solution.py:127
  19.3 0.7 %copy.25 = f32[3,32,8,128]{3,2,1,0:T(8,128)} copy(f32[3,32,8,128]{3,2,1,0:T(8,128)S(1)} %bitcast.10) | data formatting | bytes 786432
  20.1 0.7 %copy.26 = f32[3,32,8,128]{3,2,1,0:T(8,128)} copy(f32[3,32,8,128]{3,2,1,0:T(8,128)S(1)} %bitcast.11) | data formatting | bytes 786432
  20.8 0.3 %collective-permute-done.10.even = f32[120,128]{1,0:T(8,128)S(1)} collective-permute-done((f32[120,128]{1,0:T(8,128)S(1)}, f32[120,128]{1,0:T(8,128)S(1)}, u32[]{:S(2)}, u32[]{:S(2)}) %collective-permute-start.10) | collective-permute-done | bytes 61472 | tf_op jit(solution)/shard_map/ppermute | solution.py:78
  21.1 1.9 %collective-permute-done.11.odd = f32[120,128]{1,0:T(8,128)S(1)} collective-permute-done((f32[120,128]{1,0:T(8,128)S(1)}, f32[120,128]{1,0:T(8,128)S(1)}, u32[]{:S(2)}, u32[]{:S(2)}) %collective-permute-start.11) | collective-permute-done | bytes 61472 | tf_op jit(solution)/shard_map/ppermute | solution.py:78
  23.0 0.4 %shard_map.120 = f32[256,128]{1,0:T(8,128)S(1)} custom-call(f32[304,128]{1,0:T(8,128)S(1)} %get-tuple-element.50.u, f32[120,128]{1,0:T(8,128)S(1)} %collective-permute-done.10.even, f32[120,128]{1,0:T(8,128)S(1)} %collective-permute-done.11.odd, f32[256,128]{1,0:T(8,128)S(1)} %broadcast_in_dim.16.radius, f32[256,128]{1,0:T(8,128)S(1)} %shard_map.119.inverse), custom_call_target="tpu_custom_call" | custom-call | bytes 671744 | tf_op jit(solution)/shard_map/pallas_call | solution.py:127
  23.4 0.7 %copy.27 = f32[32,8,128]{2,1,0:T(8,128)} copy(f32[32,8,128]{2,1,0:T(8,128)S(1)} %bitcast.12) | data formatting | bytes 262144
  (35 shorter events, 1.4 us)
Async XLA Ops:
  0.6 2.8 %copy-start.1 = (f32[32,8,128]{2,1,0:T(8,128)S(1)}, f32[32,8,128]{2,1,0:T(8,128)}, u32[]{:S(2)}) copy-start(f32[32,8,128]{2,1,0:T(8,128)} %param.13) | copy-start | bytes 393220
  0.6 2.8 %copy-start.2 = (f32[3,32,8,128]{3,2,1,0:T(8,128)S(1)}, f32[3,32,8,128]{3,2,1,0:T(8,128)}, u32[]{:S(2)}) copy-start(f32[3,32,8,128]{3,2,1,0:T(8,128)} %param.9) | copy-start | bytes 1179652
  0.7 2.8 %copy-start.3 = (f32[3,32,8,128]{3,2,1,0:T(8,128)S(1)}, f32[3,32,8,128]{3,2,1,0:T(8,128)}, u32[]{:S(2)}) copy-start(f32[3,32,8,128]{3,2,1,0:T(8,128)} %param.10) | copy-start | bytes 1179652
  0.7 2.8 %copy-start.4 = (f32[3,32,8,128]{3,2,1,0:T(8,128)S(1)}, f32[3,32,8,128]{3,2,1,0:T(8,128)}, u32[]{:S(2)}) copy-start(f32[3,32,8,128]{3,2,1,0:T(8,128)} %param.11) | copy-start | bytes 1179652
  0.7 2.8 %copy-start.5 = (f32[3,32,8,128]{3,2,1,0:T(8,128)S(1)}, f32[3,32,8,128]{3,2,1,0:T(8,128)}, u32[]{:S(2)}) copy-start(f32[3,32,8,128]{3,2,1,0:T(8,128)} %param.12) | copy-start | bytes 1179652
  1.8 4.1 %collective-permute-start = (f32[160,128]{1,0:T(8,128)S(1)}, f32[160,128]{1,0:T(8,128)S(1)}, u32[]{:S(2)}, u32[]{:S(2)}) collective-permute-start(f32[160,128]{1,0:T(8,128)S(1)} %get-tuple-element.28), channel_id=1, source_target_pairs={{0,8},{1,9},{2,10},{3,11},{4,12},{5,13},{6,14},{7,15},{8,0},{9,1},... | collective-permute-start | bytes 245768 | tf_op jit(solution)/shard_map/ppermute | solution.py:78
  1.8 4.5 %collective-permute-start.1 = (f32[160,128]{1,0:T(8,128)S(1)}, f32[160,128]{1,0:T(8,128)S(1)}, u32[]{:S(2)}, u32[]{:S(2)}) collective-permute-start(f32[160,128]{1,0:T(8,128)S(1)} %get-tuple-element.29), channel_id=1, source_target_pairs={{0,1},{1,0},{2,3},{3,2},{4,5},{5,4},{6,7},{7,6},{8,16},{9,17},{10,... | collective-permute-start | bytes 245768 | tf_op jit(solution)/shard_map/ppermute | solution.py:78
  3.9 6.3 %collective-permute-start.2 = (f32[160,128]{1,0:T(8,128)S(1)}, f32[160,128]{1,0:T(8,128)S(1)}, u32[]{:S(2)}, u32[]{:S(2)}) collective-permute-start(f32[160,128]{1,0:T(8,128)S(1)} %get-tuple-element.38), channel_id=1, source_target_pairs={{0,1},{1,0},{2,3},{3,2},{4,5},{5,4},{6,7},{7,6},{8,9},{9,8},{10,11... | collective-permute-start | bytes 245768 | tf_op jit(solution)/shard_map/ppermute | solution.py:78
  4.4 6.2 %collective-permute-start.3 = (f32[160,128]{1,0:T(8,128)S(1)}, f32[160,128]{1,0:T(8,128)S(1)}, u32[]{:S(2)}, u32[]{:S(2)}) collective-permute-start(f32[160,128]{1,0:T(8,128)S(1)} %get-tuple-element.39), channel_id=1, source_target_pairs={{0,8},{1,2},{2,1},{3,4},{4,3},{5,6},{6,5},{7,15},{8,0},{9,10},{10,... | collective-permute-start | bytes 245768 | tf_op jit(solution)/shard_map/ppermute | solution.py:78
  6.3 3.3 %copy-start = (f32[2,3,32,8,128]{4,3,2,1,0:T(8,128)S(1)}, f32[2,3,32,8,128]{4,3,2,1,0:T(8,128)}, u32[]{:S(2)}) copy-start(f32[2,3,32,8,128]{4,3,2,1,0:T(8,128)} %param.14) | copy-start | bytes 2359300
  6.6 4.6 %collective-permute-start.4 = (f32[16,128]{1,0:T(8,128)S(1)}, f32[16,128]{1,0:T(8,128)S(1)}, u32[]{:S(2)}, u32[]{:S(2)}) collective-permute-start(f32[16,128]{1,0:T(8,128)S(1)} %get-tuple-element.40), channel_id=1, source_target_pairs={{0,8},{1,2},{2,1},{3,4},{4,3},{5,6},{6,5},{7,15},{8,0},{9,10},{10,... | collective-permute-start | bytes 24584 | tf_op jit(solution)/shard_map/ppermute | solution.py:78
  8.0 3.7 %collective-permute-start.5 = (f32[16,128]{1,0:T(8,128)S(1)}, f32[16,128]{1,0:T(8,128)S(1)}, u32[]{:S(2)}, u32[]{:S(2)}) collective-permute-start(f32[16,128]{1,0:T(8,128)S(1)} %get-tuple-element.41), channel_id=1, source_target_pairs={{0,1},{1,0},{2,3},{3,2},{4,5},{5,4},{6,7},{7,6},{8,9},{9,8},{10,11... | collective-permute-start | bytes 24584 | tf_op jit(solution)/shard_map/ppermute | solution.py:78
  10.0 6.6 %collective-permute-start.6 = (f32[128,128]{1,0:T(8,128)S(1)}, f32[128,128]{1,0:T(8,128)S(1)}, u32[]{:S(2)}, u32[]{:S(2)}) collective-permute-start(f32[128,128]{1,0:T(8,128)S(1)} %shard_map.117), channel_id=1, source_target_pairs={{0,24},{1,25},{2,26},{3,27},{4,28},{5,29},{6,30},{7,31},{8,16},{9,... | collective-permute-start | bytes 196616 | tf_op jit(solution)/shard_map/ppermute | solution.py:78
  11.6 5.1 %copy-start.6 = (s32[32,8,128]{2,1,0:T(8,128)S(1)}, s32[32,8,128]{2,1,0:T(8,128)}, u32[]{:S(2)}) copy-start(s32[32,8,128]{2,1,0:T(8,128)} %param.15) | copy-start | bytes 393220
  11.9 4.7 %collective-permute-start.7 = (f32[128,128]{1,0:T(8,128)S(1)}, f32[128,128]{1,0:T(8,128)S(1)}, u32[]{:S(2)}, u32[]{:S(2)}) collective-permute-start(f32[128,128]{1,0:T(8,128)S(1)} %get-tuple-element.48), channel_id=1, source_target_pairs={{0,24},{1,25},{2,26},{3,27},{4,28},{5,29},{6,30},{7,31},{8,16},{9,... | collective-permute-start | bytes 196616 | tf_op jit(solution)/shard_map/ppermute | solution.py:78
  12.7 3.9 %copy-start.8 = (s32[8]{0:T(128)S(1)}, s32[8]{0:T(128)}, u32[]{:S(2)}) copy-start(s32[8]{0:T(128)} %param.16) | copy-start | bytes 100
  12.8 3.9 %collective-permute-start.8 = (f32[24,128]{1,0:T(8,128)S(1)}, f32[24,128]{1,0:T(8,128)S(1)}, u32[]{:S(2)}, u32[]{:S(2)}) collective-permute-start(f32[24,128]{1,0:T(8,128)S(1)} %get-tuple-element.49), channel_id=1, source_target_pairs={{0,16},{1,17},{2,18},{3,19},{4,20},{5,21},{6,22},{7,23},{8,24},{9,... | collective-permute-start | bytes 36872 | tf_op jit(solution)/shard_map/ppermute | solution.py:78
  13.7 3.0 %collective-permute-start.9 = (f32[24,128]{1,0:T(8,128)S(1)}, f32[24,128]{1,0:T(8,128)S(1)}, u32[]{:S(2)}, u32[]{:S(2)}) collective-permute-start(f32[24,128]{1,0:T(8,128)S(1)} %get-tuple-element.49), channel_id=1, source_target_pairs={{0,8},{1,9},{2,10},{3,11},{4,12},{5,13},{6,14},{7,15},{8,0},{9,1},... | collective-permute-start | bytes 36872 | tf_op jit(solution)/shard_map/ppermute | solution.py:78
  16.7 1.9 %copy-start.7 = (s32[32,8]{0,1:T(8,128)S(1)}, s32[32,8]{0,1:T(8,128)}, u32[]{:S(2)}) copy-start(s32[32,8]{0,1:T(8,128)} %param.17) | copy-start | bytes 3076
  16.8 4.3 %collective-permute-start.10 = (f32[120,128]{1,0:T(8,128)S(1)}, f32[120,128]{1,0:T(8,128)S(1)}, u32[]{:S(2)}, u32[]{:S(2)}) collective-permute-start(f32[120,128]{1,0:T(8,128)S(1)} %get-tuple-element.51), channel_id=1, source_target_pairs={{0,1},{1,0},{2,3},{3,2},{4,5},{5,4},{6,7},{7,6},{8,9},{9,8},{10,11... | collective-permute-start | bytes 184328 | tf_op jit(solution)/shard_map/ppermute | solution.py:78
  17.9 5.1 %collective-permute-start.11 = (f32[120,128]{1,0:T(8,128)S(1)}, f32[120,128]{1,0:T(8,128)S(1)}, u32[]{:S(2)}, u32[]{:S(2)}) collective-permute-start(f32[120,128]{1,0:T(8,128)S(1)} %get-tuple-element.52), channel_id=1, source_target_pairs={{0,8},{1,2},{2,1},{3,4},{4,3},{5,6},{6,5},{7,15},{8,0},{9,10},{10,... | collective-permute-start | bytes 184328 | tf_op jit(solution)/shard_map/ppermute | solution.py:78

commit v6 on v5

--- a/solution.py
+++ b/solution.py
@@ -536,9 +536,9 @@
 
 def update(n, r, generic, *refs):
     if generic:
-        g, mid, rim, edge_m, edge, far, far_m, d, m, even, odd, order, u_out, even_y, odd_y_out, u_pad, other = refs
+        g, mid, edge_m, rim, edge, far, far_m, d, m, even, odd, order, u_out, even_y, odd_y_out, u_pad, other = refs
     else:
-        g, mid, rim, edge_m, edge, d, m, even, odd, order, u_out, even_y, odd_y_out, u_pad, other = refs
+        g, mid, edge_m, rim, edge, d, m, even, odd, order, u_out, even_y, odd_y_out, u_pad, other = refs
     for k, j in enumerate(range(REACH, r - REACH)):
         other[pl.ds(j, n, stride=r), :] = mid[k * n : (k + 1) * n, :]
     for k, j in enumerate(rim_rows(r)):
@@ -793,7 +793,7 @@
     u, even_u, odd_u = call(
         functools.partial(update, n, r, generic),
         [(full * r, depth), (WIDTH * wide, depth), (WIDTH * wide, depth)],
-        [g, mid, rim, edge_m, edge_e] + extra + [d, m, even, odd, order],
+        [g, mid, edge_m, rim, edge_e] + extra + [d, m, even, odd, order],
         scratch=[VMEM((wide * r, depth), jnp.float32), VMEM((size, depth), jnp.float32)],
     )
     odd_u = send(odd_u, y_odd)

time: 24.2 us -> 24.2 us (level)
  no operation moved by 1% of the time
where the time goes in v6:
time: 24.2 us; the launch traced here: 24 us
  starting transfers between devices  10.5 us (43%)
  waiting for transfers between devices  6.41 us (26%)
  Pallas kernels  3.77 us (16%)
  local copies, waits for them, and re-layouts  2.52 us (10%)
  between operations  0.77 us (3%)
    ppermute x12, starting transfers between devices, send(): return lax.ppermute(block, AXES, route)  10.5 us
    ppermute x12, waiting for transfers between devices, send(): return lax.ppermute(block, AXES, route)  6.41 us
    pallas_call x8, Pallas kernels, call(): pl.pallas_call(kernel, out_shape=tuple((VMEM(s, jnp.float32) for s in out...  2.71 us
    unnamed x21, local copies, waits for them, and re-layouts  2.19 us
    pallas_call x1, Pallas kernels, local(): pl.pallas_call(functools.partial(pack_x, n, r), out_shape=(VMEM(face_x, f...  1.06 us
  transfers between devices with their start and end apart: 12, of which 6 were waited for; matrix products, arithmetic and copies ran while one was open for 7% of the time, Pallas kernels for 9%

profile of v6, /device:TPU:8, one launch (start us, length us, event | category | flops | bytes accessed | tf_op | source)
XLA Modules:
  0.0 24.0 jit_solution(16479194768845822548)
XLA Ops:
  0.7 1.1 %shard_map.112 = (f32[160,128]{1,0:T(8,128)S(1)}, f32[160,128]{1,0:T(8,128)S(1)}) custom-call(f32[3,256,128]{2,1,0:T(8,128)} %bitcast.23, f32[3,256,128]{2,1,0:T(8,128)} %bitcast.26, f32[3,256,128]{2,1,0:T(8,128)} %bitcast.29, f32[3,256,128]{2,1,0:T(8,128)} %bitcast.32, f32[256,128]{1,0:T(8,128)} %bitcast.16, s32[256,128]{1,0:T(8,128)} %bitcast.35), custom_call_target="tpu_custom_call" | custom-call | tf_op jit(solution)/shard_map/pallas_call | solution.py:722
  1.8 1.6 %collective-permute-start.1 = (f32[160,128]{1,0:T(8,128)S(1)}, f32[160,128]{1,0:T(8,128)S(1)}, u32[]{:S(2)}, u32[]{:S(2)}) collective-permute-start(f32[160,128]{1,0:T(8,128)S(1)} %get-tuple-element.29), channel_id=1, source_target_pairs={{0,1},{1,0},{2,3},{3,2},{4,5},{5,4},{6,7},{7,6},{8,16},{9,17},{10,... | collective-permute-start | bytes 245768 | tf_op jit(solution)/shard_map/ppermute | solution.py:78
  3.4 0.4 %shard_map.113 = (f32[3,272,128]{2,1,0:T(8,128)S(1)}, f32[3,272,128]{2,1,0:T(8,128)S(1)}, f32[272,128]{1,0:T(8,128)S(1)}, f32[3,256,128]{2,1,0:T(8,128)S(1)}, f3...) custom-call(f32[3,256,128]{2,1,0:T(8,128)S(1)} %bitcast.24, f32[3,256,128]{2,1,0:T(8,128)S(1)} %bitcast.27, ...), custom_call_target="tpu_custom_call" | custom-call | flops 3276800 | bytes 3235840 | tf_op jit(solution)/shard_map/pallas_call | solution.py:127
  3.9 0.6 %collective-permute-start.2 = (f32[160,128]{1,0:T(8,128)S(1)}, f32[160,128]{1,0:T(8,128)S(1)}, u32[]{:S(2)}, u32[]{:S(2)}) collective-permute-start(f32[160,128]{1,0:T(8,128)S(1)} %get-tuple-element.38), channel_id=1, source_target_pairs={{0,1},{1,0},{2,3},{3,2},{4,5},{5,4},{6,7},{7,6},{8,9},{9,8},{10,11... | collective-permute-start | bytes 245768 | tf_op jit(solution)/shard_map/ppermute | solution.py:78
  4.4 1.4 %collective-permute-start.3 = (f32[160,128]{1,0:T(8,128)S(1)}, f32[160,128]{1,0:T(8,128)S(1)}, u32[]{:S(2)}, u32[]{:S(2)}) collective-permute-start(f32[160,128]{1,0:T(8,128)S(1)} %get-tuple-element.39), channel_id=1, source_target_pairs={{0,8},{1,2},{2,1},{3,4},{4,3},{5,6},{6,5},{7,15},{8,0},{9,10},{10,... | collective-permute-start | bytes 245768 | tf_op jit(solution)/shard_map/ppermute | solution.py:78
  5.9 0.5 %collective-permute-done.1.odd.refs_8_ = f32[160,128]{1,0:T(8,128)S(1)} collective-permute-done((f32[160,128]{1,0:T(8,128)S(1)}, f32[160,128]{1,0:T(8,128)S(1)}, u32[]{:S(2)}, u32[]{:S(2)}) %collective-permute-start.1) | collective-permute-done | bytes 81952 | tf_op jit(solution)/shard_map/ppermute | solution.py:78
  6.6 1.4 %collective-permute-start.4 = (f32[16,128]{1,0:T(8,128)S(1)}, f32[16,128]{1,0:T(8,128)S(1)}, u32[]{:S(2)}, u32[]{:S(2)}) collective-permute-start(f32[16,128]{1,0:T(8,128)S(1)} %get-tuple-element.40), channel_id=1, source_target_pairs={{0,8},{1,2},{2,1},{3,4},{4,3},{5,6},{6,5},{7,15},{8,0},{9,10},{10,... | collective-permute-start | bytes 24584 | tf_op jit(solution)/shard_map/ppermute | solution.py:78
  8.0 1.6 %collective-permute-start.5 = (f32[16,128]{1,0:T(8,128)S(1)}, f32[16,128]{1,0:T(8,128)S(1)}, u32[]{:S(2)}, u32[]{:S(2)}) collective-permute-start(f32[16,128]{1,0:T(8,128)S(1)} %get-tuple-element.41), channel_id=1, source_target_pairs={{0,1},{1,0},{2,3},{3,2},{4,5},{5,4},{6,7},{7,6},{8,9},{9,8},{10,11... | collective-permute-start | bytes 24584 | tf_op jit(solution)/shard_map/ppermute | solution.py:78
  9.6 0.4 %shard_map.117 = f32[128,128]{1,0:T(8,128)S(1)} custom-call(f32[3,272,128]{2,1,0:T(8,128)S(1)} %get-tuple-element.33.h, f32[3,272,128]{2,1,0:T(8,128)S(1)} %get-tuple-element.34.e, f32[272,128]{1,0:T(8,128)S(1)} %get-tuple-element.35.c_ref, f32[3,256,128]{2,1,0:T(8,128)S(1)} %get-tuple-element.36.t, f32[256,128]{1,0:T(8,128)S(1)} %bitcast.19, ...), custom_call_target="tpu_custom_call" | custom-call | flops 3276800 | bytes 2351104 | tf_op jit(solution)/shard_map/pallas_call | solution.py:127
  10.2 0.4 %collective-permute-done.3.odd = f32[160,128]{1,0:T(8,128)S(1)} collective-permute-done((f32[160,128]{1,0:T(8,128)S(1)}, f32[160,128]{1,0:T(8,128)S(1)}, u32[]{:S(2)}, u32[]{:S(2)}) %collective-permute-start.3) | collective-permute-done | bytes 81952 | tf_op jit(solution)/shard_map/ppermute | solution.py:78
  10.6 0.5 %shard_map.115 = (f32[3,256,128]{2,1,0:T(8,128)S(1)}, f32[3,256,128]{2,1,0:T(8,128)S(1)}, f32[256,128]{1,0:T(8,128)S(1)}) custom-call(f32[3,272,128]{2,1,0:T(8,128)S(1)} %get-tuple-element.33.h, f32[3,272,128]{2,1,0:T(8,128)S(1)} %get-tuple-element.34.e, f32[272,128]{1,0:T(8,128)S(1)} %get-tuple-element.35.c_ref, f32[3,256,128]{2,1,0:T(8,128)S(1)} %get-tuple-element.36.t, ...), custom_call_target="tpu_custom_call" | custom-call | flops 4915200 | bytes 3416064 | tf_op jit(solution)/shard_map/pallas_call | solution.py:127
  11.1 0.5 %collective-permute-done.5.refs_1_ = f32[16,128]{1,0:T(8,128)S(1)} collective-permute-done((f32[16,128]{1,0:T(8,128)S(1)}, f32[16,128]{1,0:T(8,128)S(1)}, u32[]{:S(2)}, u32[]{:S(2)}) %collective-permute-start.5) | collective-permute-done | bytes 8224 | tf_op jit(solution)/shard_map/ppermute | solution.py:78
  11.9 0.8 %collective-permute-start.8 = (f32[128,128]{1,0:T(8,128)S(1)}, f32[128,128]{1,0:T(8,128)S(1)}, u32[]{:S(2)}, u32[]{:S(2)}) collective-permute-start(f32[128,128]{1,0:T(8,128)S(1)} %get-tuple-element.49), channel_id=1, source_target_pairs={{0,24},{1,25},{2,26},{3,27},{4,28},{5,29},{6,30},{7,31},{8,16},{9,... | collective-permute-start | bytes 196616 | tf_op jit(solution)/shard_map/ppermute | solution.py:78
  12.8 0.9 %collective-permute-start.7 = (f32[24,128]{1,0:T(8,128)S(1)}, f32[24,128]{1,0:T(8,128)S(1)}, u32[]{:S(2)}, u32[]{:S(2)}) collective-permute-start(f32[24,128]{1,0:T(8,128)S(1)} %get-tuple-element.48), channel_id=1, source_target_pairs={{0,16},{1,17},{2,18},{3,19},{4,20},{5,21},{6,22},{7,23},{8,24},{9,... | collective-permute-start | bytes 36872 | tf_op jit(solution)/shard_map/ppermute | solution.py:78
  13.8 2.8 %collective-permute-done.7.refs_2_ = f32[24,128]{1,0:T(8,128)S(1)} collective-permute-done((f32[24,128]{1,0:T(8,128)S(1)}, f32[24,128]{1,0:T(8,128)S(1)}, u32[]{:S(2)}, u32[]{:S(2)}) %collective-permute-start.7) | collective-permute-done | bytes 12320 | tf_op jit(solution)/shard_map/ppermute | solution.py:78
  16.8 1.0 %collective-permute-start.10 = (f32[120,128]{1,0:T(8,128)S(1)}, f32[120,128]{1,0:T(8,128)S(1)}, u32[]{:S(2)}, u32[]{:S(2)}) collective-permute-start(f32[120,128]{1,0:T(8,128)S(1)} %get-tuple-element.51), channel_id=1, source_target_pairs={{0,1},{1,0},{2,3},{3,2},{4,5},{5,4},{6,7},{7,6},{8,9},{9,8},{10,11... | collective-permute-start | bytes 184328 | tf_op jit(solution)/shard_map/ppermute | solution.py:78
  17.9 0.8 %collective-permute-start.11 = (f32[120,128]{1,0:T(8,128)S(1)}, f32[120,128]{1,0:T(8,128)S(1)}, u32[]{:S(2)}, u32[]{:S(2)}) collective-permute-start(f32[120,128]{1,0:T(8,128)S(1)} %get-tuple-element.52), channel_id=1, source_target_pairs={{0,8},{1,2},{2,1},{3,4},{4,3},{5,6},{6,5},{7,15},{8,0},{9,10},{10,... | collective-permute-start | bytes 184328 | tf_op jit(solution)/shard_map/ppermute | solution.py:78
  18.9 0.4 %shard_map.119.inverse = f32[256,128]{1,0:T(8,128)S(1)} custom-call(f32[256,128]{1,0:T(8,128)S(1)} %broadcast_in_dim.16.radius), custom_call_target="tpu_custom_call" | custom-call | flops 3276800 | bytes 262144 | tf_op jit(solution)/shard_map/pallas_call | solution.py:127
  19.3 0.7 %copy.25 = f32[3,32,8,128]{3,2,1,0:T(8,128)} copy(f32[3,32,8,128]{3,2,1,0:T(8,128)S(1)} %bitcast.10) | data formatting | bytes 786432
  20.1 0.7 %copy.26 = f32[3,32,8,128]{3,2,1,0:T(8,128)} copy(f32[3,32,8,128]{3,2,1,0:T(8,128)S(1)} %bitcast.11) | data formatting | bytes 786432
  20.8 0.3 %collective-permute-done.10.even = f32[120,128]{1,0:T(8,128)S(1)} collective-permute-done((f32[120,128]{1,0:T(8,128)S(1)}, f32[120,128]{1,0:T(8,128)S(1)}, u32[]{:S(2)}, u32[]{:S(2)}) %collective-permute-start.10) | collective-permute-done | bytes 61472 | tf_op jit(solution)/shard_map/ppermute | solution.py:78
  21.1 1.9 %collective-permute-done.11.odd = f32[120,128]{1,0:T(8,128)S(1)} collective-permute-done((f32[120,128]{1,0:T(8,128)S(1)}, f32[120,128]{1,0:T(8,128)S(1)}, u32[]{:S(2)}, u32[]{:S(2)}) %collective-permute-start.11) | collective-permute-done | bytes 61472 | tf_op jit(solution)/shard_map/ppermute | solution.py:78
  23.0 0.4 %shard_map.120 = f32[256,128]{1,0:T(8,128)S(1)} custom-call(f32[304,128]{1,0:T(8,128)S(1)} %get-tuple-element.50.u, f32[120,128]{1,0:T(8,128)S(1)} %collective-permute-done.10.even, f32[120,128]{1,0:T(8,128)S(1)} %collective-permute-done.11.odd, f32[256,128]{1,0:T(8,128)S(1)} %broadcast_in_dim.16.radius, f32[256,128]{1,0:T(8,128)S(1)} %shard_map.119.inverse), custom_call_target="tpu_custom_call" | custom-call | bytes 671744 | tf_op jit(solution)/shard_map/pallas_call | solution.py:127
  23.4 0.7 %copy.27 = f32[32,8,128]{2,1,0:T(8,128)} copy(f32[32,8,128]{2,1,0:T(8,128)S(1)} %bitcast.12) | data formatting | bytes 262144
  (35 shorter events, 1.4 us)
Async XLA Ops:
  0.6 2.8 %copy-start.1 = (f32[32,8,128]{2,1,0:T(8,128)S(1)}, f32[32,8,128]{2,1,0:T(8,128)}, u32[]{:S(2)}) copy-start(f32[32,8,128]{2,1,0:T(8,128)} %param.13) | copy-start | bytes 393220
  0.6 2.8 %copy-start.2 = (f32[3,32,8,128]{3,2,1,0:T(8,128)S(1)}, f32[3,32,8,128]{3,2,1,0:T(8,128)}, u32[]{:S(2)}) copy-start(f32[3,32,8,128]{3,2,1,0:T(8,128)} %param.9) | copy-start | bytes 1179652
  0.7 2.8 %copy-start.3 = (f32[3,32,8,128]{3,2,1,0:T(8,128)S(1)}, f32[3,32,8,128]{3,2,1,0:T(8,128)}, u32[]{:S(2)}) copy-start(f32[3,32,8,128]{3,2,1,0:T(8,128)} %param.10) | copy-start | bytes 1179652
  0.7 2.8 %copy-start.4 = (f32[3,32,8,128]{3,2,1,0:T(8,128)S(1)}, f32[3,32,8,128]{3,2,1,0:T(8,128)}, u32[]{:S(2)}) copy-start(f32[3,32,8,128]{3,2,1,0:T(8,128)} %param.11) | copy-start | bytes 1179652
  0.7 2.8 %copy-start.5 = (f32[3,32,8,128]{3,2,1,0:T(8,128)S(1)}, f32[3,32,8,128]{3,2,1,0:T(8,128)}, u32[]{:S(2)}) copy-start(f32[3,32,8,128]{3,2,1,0:T(8,128)} %param.12) | copy-start | bytes 1179652
  1.8 4.1 %collective-permute-start = (f32[160,128]{1,0:T(8,128)S(1)}, f32[160,128]{1,0:T(8,128)S(1)}, u32[]{:S(2)}, u32[]{:S(2)}) collective-permute-start(f32[160,128]{1,0:T(8,128)S(1)} %get-tuple-element.28), channel_id=1, source_target_pairs={{0,8},{1,9},{2,10},{3,11},{4,12},{5,13},{6,14},{7,15},{8,0},{9,1},... | collective-permute-start | bytes 245768 | tf_op jit(solution)/shard_map/ppermute | solution.py:78
  1.8 4.5 %collective-permute-start.1 = (f32[160,128]{1,0:T(8,128)S(1)}, f32[160,128]{1,0:T(8,128)S(1)}, u32[]{:S(2)}, u32[]{:S(2)}) collective-permute-start(f32[160,128]{1,0:T(8,128)S(1)} %get-tuple-element.29), channel_id=1, source_target_pairs={{0,1},{1,0},{2,3},{3,2},{4,5},{5,4},{6,7},{7,6},{8,16},{9,17},{10,... | collective-permute-start | bytes 245768 | tf_op jit(solution)/shard_map/ppermute | solution.py:78
  3.9 6.3 %collective-permute-start.2 = (f32[160,128]{1,0:T(8,128)S(1)}, f32[160,128]{1,0:T(8,128)S(1)}, u32[]{:S(2)}, u32[]{:S(2)}) collective-permute-start(f32[160,128]{1,0:T(8,128)S(1)} %get-tuple-element.38), channel_id=1, source_target_pairs={{0,1},{1,0},{2,3},{3,2},{4,5},{5,4},{6,7},{7,6},{8,9},{9,8},{10,11... | collective-permute-start | bytes 245768 | tf_op jit(solution)/shard_map/ppermute | solution.py:78
  4.4 6.2 %collective-permute-start.3 = (f32[160,128]{1,0:T(8,128)S(1)}, f32[160,128]{1,0:T(8,128)S(1)}, u32[]{:S(2)}, u32[]{:S(2)}) collective-permute-start(f32[160,128]{1,0:T(8,128)S(1)} %get-tuple-element.39), channel_id=1, source_target_pairs={{0,8},{1,2},{2,1},{3,4},{4,3},{5,6},{6,5},{7,15},{8,0},{9,10},{10,... | collective-permute-start | bytes 245768 | tf_op jit(solution)/shard_map/ppermute | solution.py:78
  6.3 3.3 %copy-start = (f32[2,3,32,8,128]{4,3,2,1,0:T(8,128)S(1)}, f32[2,3,32,8,128]{4,3,2,1,0:T(8,128)}, u32[]{:S(2)}) copy-start(f32[2,3,32,8,128]{4,3,2,1,0:T(8,128)} %param.14) | copy-start | bytes 2359300
  6.6 4.6 %collective-permute-start.4 = (f32[16,128]{1,0:T(8,128)S(1)}, f32[16,128]{1,0:T(8,128)S(1)}, u32[]{:S(2)}, u32[]{:S(2)}) collective-permute-start(f32[16,128]{1,0:T(8,128)S(1)} %get-tuple-element.40), channel_id=1, source_target_pairs={{0,8},{1,2},{2,1},{3,4},{4,3},{5,6},{6,5},{7,15},{8,0},{9,10},{10,... | collective-permute-start | bytes 24584 | tf_op jit(solution)/shard_map/ppermute | solution.py:78
  8.0 3.7 %collective-permute-start.5 = (f32[16,128]{1,0:T(8,128)S(1)}, f32[16,128]{1,0:T(8,128)S(1)}, u32[]{:S(2)}, u32[]{:S(2)}) collective-permute-start(f32[16,128]{1,0:T(8,128)S(1)} %get-tuple-element.41), channel_id=1, source_target_pairs={{0,1},{1,0},{2,3},{3,2},{4,5},{5,4},{6,7},{7,6},{8,9},{9,8},{10,11... | collective-permute-start | bytes 24584 | tf_op jit(solution)/shard_map/ppermute | solution.py:78
  10.0 6.6 %collective-permute-start.6 = (f32[128,128]{1,0:T(8,128)S(1)}, f32[128,128]{1,0:T(8,128)S(1)}, u32[]{:S(2)}, u32[]{:S(2)}) collective-permute-start(f32[128,128]{1,0:T(8,128)S(1)} %shard_map.117), channel_id=1, source_target_pairs={{0,24},{1,25},{2,26},{3,27},{4,28},{5,29},{6,30},{7,31},{8,16},{9,... | collective-permute-start | bytes 196616 | tf_op jit(solution)/shard_map/ppermute | solution.py:78
  11.6 5.1 %copy-start.6 = (s32[32,8,128]{2,1,0:T(8,128)S(1)}, s32[32,8,128]{2,1,0:T(8,128)}, u32[]{:S(2)}) copy-start(s32[32,8,128]{2,1,0:T(8,128)} %param.15) | copy-start | bytes 393220
  11.9 4.7 %collective-permute-start.8 = (f32[128,128]{1,0:T(8,128)S(1)}, f32[128,128]{1,0:T(8,128)S(1)}, u32[]{:S(2)}, u32[]{:S(2)}) collective-permute-start(f32[128,128]{1,0:T(8,128)S(1)} %get-tuple-element.49), channel_id=1, source_target_pairs={{0,24},{1,25},{2,26},{3,27},{4,28},{5,29},{6,30},{7,31},{8,16},{9,... | collective-permute-start | bytes 196616 | tf_op jit(solution)/shard_map/ppermute | solution.py:78
  12.7 3.9 %copy-start.8 = (s32[8]{0:T(128)S(1)}, s32[8]{0:T(128)}, u32[]{:S(2)}) copy-start(s32[8]{0:T(128)} %param.16) | copy-start | bytes 100
  12.8 3.9 %collective-permute-start.7 = (f32[24,128]{1,0:T(8,128)S(1)}, f32[24,128]{1,0:T(8,128)S(1)}, u32[]{:S(2)}, u32[]{:S(2)}) collective-permute-start(f32[24,128]{1,0:T(8,128)S(1)} %get-tuple-element.48), channel_id=1, source_target_pairs={{0,16},{1,17},{2,18},{3,19},{4,20},{5,21},{6,22},{7,23},{8,24},{9,... | collective-permute-start | bytes 36872 | tf_op jit(solution)/shard_map/ppermute | solution.py:78
  13.7 3.0 %collective-permute-start.9 = (f32[24,128]{1,0:T(8,128)S(1)}, f32[24,128]{1,0:T(8,128)S(1)}, u32[]{:S(2)}, u32[]{:S(2)}) collective-permute-start(f32[24,128]{1,0:T(8,128)S(1)} %get-tuple-element.48), channel_id=1, source_target_pairs={{0,8},{1,9},{2,10},{3,11},{4,12},{5,13},{6,14},{7,15},{8,0},{9,1},... | collective-permute-start | bytes 36872 | tf_op jit(solution)/shard_map/ppermute | solution.py:78
  16.7 1.9 %copy-start.7 = (s32[32,8]{0,1:T(8,128)S(1)}, s32[32,8]{0,1:T(8,128)}, u32[]{:S(2)}) copy-start(s32[32,8]{0,1:T(8,128)} %param.17) | copy-start | bytes 3076
  16.8 4.3 %collective-permute-start.10 = (f32[120,128]{1,0:T(8,128)S(1)}, f32[120,128]{1,0:T(8,128)S(1)}, u32[]{:S(2)}, u32[]{:S(2)}) collective-permute-start(f32[120,128]{1,0:T(8,128)S(1)} %get-tuple-element.51), channel_id=1, source_target_pairs={{0,1},{1,0},{2,3},{3,2},{4,5},{5,4},{6,7},{7,6},{8,9},{9,8},{10,11... | collective-permute-start | bytes 184328 | tf_op jit(solution)/shard_map/ppermute | solution.py:78
  17.9 5.1 %collective-permute-start.11 = (f32[120,128]{1,0:T(8,128)S(1)}, f32[120,128]{1,0:T(8,128)S(1)}, u32[]{:S(2)}, u32[]{:S(2)}) collective-permute-start(f32[120,128]{1,0:T(8,128)S(1)} %get-tuple-element.52), channel_id=1, source_target_pairs={{0,8},{1,2},{2,1},{3,4},{4,3},{5,6},{6,5},{7,15},{8,0},{9,10},{10,... | collective-permute-start | bytes 184328 | tf_op jit(solution)/shard_map/ppermute | solution.py:78
